TPU v7x, 128 devices: a whole 4x4x4 slice. The times are simulated.
128 devices in a mesh: seq: 16 (over y, z), head: 8 (over x, core).
Axes of the slice: x: 4, y: 4, z: 4, core: 2. Of those that a mesh axis runs over, the one named last changes fastest.
Arguments:
- tokens: bfloat16 [4, 16384, 8192], P(None, 'seq', 'head'), may hold values from -60 to 60
- state_inputs: bfloat16 [4, 16384, 1024], P(None, 'seq', 'head'), may hold values from -4 to 4
- state_reads: bfloat16 [4, 16384, 1024], P(None, 'seq', 'head'), may hold values from -2.1213203 to 2.1213203
- log_decay: float32 [4, 128, 16384], P(None, 'head', 'seq'), may hold values from -1 to 0
- norm_gain: float32 [8192], P('head'), may hold values from 0.5 to 1.5
- probe_tokens: bfloat16 [96, 64, 8192], P('seq', None, 'head'), may hold values from -60 to 60
- probe_inputs: bfloat16 [96, 64, 1024], P('seq', None, 'head'), may hold values from -4 to 4
- probe_reads: bfloat16 [96, 64, 1024], P('seq', None, 'head'), may hold values from -2.1213203 to 2.1213203
- probe_decay: float32 [96, 128, 64], P('seq', 'head'), may hold values from -1 to 0
- branch_premise: int32 [96], replicated, may hold values from 0 to 3
- branch_position: int32 [96], replicated, may hold values from 0 to 16383, as said below
Outputs:
- premise_out: bfloat16 [4, 16384, 8192], P(None, 'seq', 'head')
- probe_out: bfloat16 [96, 64, 8192], P('seq', None, 'head')
Inputs may be any that keep to these rules, and one draw needn't show every extreme that they name: `branch_position`: probes g * 6 to g * 6 + 5 branch at positions whose values of position // 1024 are all different.
All inputs are finite; a program needn't handle non-finite values.
Results may differ from a plain program's by a relative error of at most 0.0046.
Values may be sent and summed in bfloat16 or wider, within the bound.
No kernel may reach another device: no remote copies, remote signals or barrier semaphores. Data moves between devices by JAX's collectives and lax.ppermute only.
A program may use at most 256 MiB of HBM per device.

v0:
```python
import jax
import jax.numpy as jnp
from jax import lax
from jax.sharding import PartitionSpec as P

DSTATE = 128
DIN = 8192
SPAN = 256


PRECISE = lax.Precision.HIGHEST
EPSILON = 1e-05


def entering(value, axis, join, neutral):
    count, mine = (lax.axis_size(axis), lax.axis_index(axis))
    pieces = jax.tree.map(lambda part: lax.all_gather(part, axis), value)
    total = jax.tree.map(
        lambda part, zero: jnp.full_like(part, 0) + jnp.asarray(zero, part.dtype), value, neutral
    )

    def turn(position, total):
        longer = join(total, jax.tree.map(lambda part: part[position], pieces))
        return jax.tree.map(lambda new, old: jnp.where(position < mine, new, old), longer, total)

    return lax.fori_loop(0, count - 1, turn, total)


def split_heads(seq_x, seq_in, seq_read, seq_decay, block_len):
    row_count, seq_length, full_width = seq_x.shape
    heads_dev = seq_decay.shape[1]
    groups_dev = seq_in.shape[2] // DSTATE
    per_group = heads_dev // groups_dev
    headdim = full_width // heads_dev
    block_count = seq_length // block_len
    block_x = seq_x.reshape(row_count, block_count, block_len, groups_dev, per_group, headdim)
    block_in = seq_in.reshape(row_count, block_count, block_len, groups_dev, DSTATE)
    block_read = seq_read.reshape(row_count, block_count, block_len, groups_dev, DSTATE)
    block_decay = seq_decay.reshape(row_count, groups_dev, per_group, block_count, block_len)
    return (block_x, block_in, block_read, jnp.cumsum(block_decay, axis=-1))


def local_blocks(block_x, block_in, block_read, cumulative):

    def one_row(pieces):
        row_x, row_in, row_read, row_cum = pieces
        block_len = row_x.shape[1]
        gram_block = jnp.einsum(
            "kqgn,kugn->gkqu", row_read, row_in, preferred_element_type=jnp.float32
        )
        spread = row_cum[..., :, None] - row_cum[..., None, :]
        causal = jnp.arange(block_len)[:, None] >= jnp.arange(block_len)[None, :]
        weights = (
            jnp.where(causal, jnp.exp(jnp.where(causal, spread, 0.0)), 0.0) * gram_block[:, None]
        )
        inner_part = jnp.einsum(
            "ghkqu,kughp->kqghp",
            weights.astype(jnp.bfloat16),
            row_x,
            preferred_element_type=jnp.float32,
        )
        tail_decay = jnp.exp(row_cum[..., -1:] - row_cum)
        scaled = (row_x * jnp.transpose(tail_decay, (2, 3, 0, 1))[..., None]).astype(jnp.bfloat16)
        written = jnp.einsum(
            "kqghp,kqgn->kghpn", scaled, row_in, preferred_element_type=jnp.float32
        )
        return (inner_part, written)

    return lax.map(one_row, (block_x, block_in, block_read, cumulative))


def block_starts(written, cumulative):
    totals = cumulative[..., -1]

    def advance(carried, step_in):
        step_total, step_written = step_in
        return (jnp.exp(step_total)[..., None, None] * carried + step_written, carried)

    zero_state = jnp.zeros(written.shape[:1] + written.shape[2:], jnp.float32)
    final_state, starts = lax.scan(
        advance, zero_state, (jnp.moveaxis(totals, -1, 0), jnp.moveaxis(written, 1, 0))
    )
    return (final_state, starts, totals)


def state_output(block_read, starts, cumulative):
    product = jnp.einsum(
        "rkqgn,krghpn->rkqghp", block_read.astype(jnp.float32), starts, precision=PRECISE
    )
    return jnp.exp(jnp.transpose(cumulative, (0, 3, 4, 1, 2)))[..., None] * product


def branch_states(block_x, block_in, cumulative, true_starts, premise_ids, offsets, present):
    block_len = block_x.shape[2]

    def one_branch(premise, offset):
        block_idx = offset // block_len
        within = offset % block_len
        start_state = true_starts[block_idx, premise]
        row_x = block_x[premise, block_idx]
        row_in = block_in[premise, block_idx]
        row_cum = cumulative[premise, :, :, block_idx]
        here_cum = lax.dynamic_index_in_dim(row_cum, within, axis=2, keepdims=False)
        keep_mask = jnp.arange(block_len) <= within
        weights = jnp.where(
            keep_mask, jnp.exp(jnp.where(keep_mask, here_cum[..., None] - row_cum, 0.0)), 0.0
        )
        scaled = (row_x * jnp.transpose(weights, (2, 0, 1))[..., None]).astype(jnp.bfloat16)
        fresh_part = jnp.einsum(
            "qghp,qgn->ghpn", scaled, row_in, preferred_element_type=jnp.float32
        )
        return jnp.exp(here_cum)[..., None, None] * start_state + fresh_part

    states = jax.vmap(one_branch)(premise_ids, offsets)
    return jnp.where(present[:, None, None, None, None], states, 0.0)


def chain_step(earlier, later_part):
    return (
        earlier[0] + later_part[0],
        jnp.exp(later_part[0])[..., None, None] * earlier[1] + later_part[1],
    )


def local(
    tokens,
    state_inputs,
    state_reads,
    log_decay,
    norm_gain,
    probe_tokens,
    probe_inputs,
    probe_reads,
    probe_decay,
    branch_premise,
    branch_position,
):
    seq_count = lax.axis_size("seq")
    myself = lax.axis_index("seq")
    row_count = tokens.shape[0]
    seq_dev = tokens.shape[1]
    probe_dev = probe_tokens.shape[0]
    probe_len = probe_tokens.shape[1]
    probe_block = min(probe_len, SPAN)
    main_x, main_in, main_read, main_cum = split_heads(
        tokens, state_inputs, state_reads, log_decay, SPAN
    )
    main_inner, main_written = local_blocks(main_x, main_in, main_read, main_cum)
    main_final, main_starts, main_totals = block_starts(main_written, main_cum)
    device_total = jnp.sum(main_totals, axis=-1)
    identity = (jnp.zeros_like(device_total), jnp.zeros_like(main_final))
    _, incoming = entering((device_total, main_final), "seq", chain_step, identity)
    before = jnp.cumsum(main_totals, axis=-1) - main_totals
    lift_factor = jnp.exp(jnp.transpose(before, (3, 0, 1, 2)))[..., None, None]
    true_starts = main_starts + lift_factor * incoming[None]
    main_y = main_inner + state_output(main_read, true_starts, main_cum)
    probe_x, probe_in, probe_read, probe_cum = split_heads(
        probe_tokens, probe_inputs, probe_reads, probe_decay, probe_block
    )
    probe_inner, probe_written = local_blocks(probe_x, probe_in, probe_read, probe_cum)
    _, probe_starts, probe_totals = block_starts(probe_written, probe_cum)
    probe_before = jnp.cumsum(probe_totals, axis=-1) - probe_totals
    keeper_count = branch_position.shape[0] // probe_dev
    positions = branch_position.reshape(keeper_count, probe_dev)
    premises = branch_premise.reshape(keeper_count, probe_dev)
    owned_here = positions // seq_dev == myself
    present = jnp.any(owned_here, axis=1)
    offsets = jnp.sum(jnp.where(owned_here, positions - myself * seq_dev, 0), axis=1)
    chosen = jnp.sum(jnp.where(owned_here, premises, 0), axis=1)
    outgoing = branch_states(main_x, main_in, main_cum, true_starts, chosen, offsets, present)
    mine_pos = lax.dynamic_slice_in_dim(branch_position, myself * probe_dev, probe_dev)
    owner_of = mine_pos // seq_dev
    selector = owner_of[:, None] == jnp.arange(seq_count, dtype=jnp.int32)[None, :]
    arrived = lax.all_to_all(outgoing[:, None], "seq", split_axis=0, concat_axis=0, tiled=True)
    anchor = jnp.dot(
        selector.astype(jnp.float32), arrived.reshape(seq_count, -1), precision=PRECISE
    )
    anchor = anchor.reshape((probe_dev,) + outgoing.shape[1:])
    probe_lift = jnp.exp(jnp.transpose(probe_before, (3, 0, 1, 2)))[..., None, None]
    probe_y = probe_inner + state_output(
        probe_read, probe_starts + probe_lift * anchor[None], probe_cum
    )
    main_flat = main_y.reshape(row_count, seq_dev, -1)
    probe_flat = probe_y.reshape(probe_dev, probe_len, -1)
    main_square, probe_square = lax.psum(
        (jnp.sum(main_flat * main_flat, axis=-1), jnp.sum(probe_flat * probe_flat, axis=-1)), "head"
    )
    premise_out = (
        main_flat * lax.rsqrt(main_square / DIN + EPSILON)[..., None] * norm_gain
    ).astype(jnp.bfloat16)
    probe_out = (
        probe_flat * lax.rsqrt(probe_square / DIN + EPSILON)[..., None] * norm_gain
    ).astype(jnp.bfloat16)
    return (premise_out, probe_out)


def solution(mesh):
    return jax.shard_map(
        local,
        mesh=mesh,
        in_specs=(
            P(None, "seq", "head"),
            P(None, "seq", "head"),
            P(None, "seq", "head"),
            P(None, "head", "seq"),
            P("head"),
            P("seq", None, "head"),
            P("seq", None, "head"),
            P("seq", None, "head"),
            P("seq", "head", None),
            P(),
            P(),
        ),
        out_specs=(P(None, "seq", "head"), P("seq", None, "head")),
        check_vma=False,
    )
```

profile of v0, /device:TPU:112, one launch (start us, length us, event | category | flops | bytes accessed | tf_op | source)
XLA Modules:
  0.0 604.2 jit_solution(14526944571075451542)
XLA Ops:
  8.4 9.1 %reduce-window.6 = f32[4,1,16,4,2,128]{5,2,3,4,1,0:T(8,128)S(1)} reduce-window(f32[4,1,16,4,2,128]{5,2,3,4,1,0:T(8,128)S(1)} %copy.130, f32[]{:T(128)} %constant.170.clone.1), window={size=1x1x1x1x1x128 pad=0_0x0_0x0_0x0_0x0_0x127_0}, to_apply=%region_0.0 | reduce-window | flops 8323072 | bytes 524292 | tf_op jit(solution)/shard_map/reduce-window
  20.2 11.4 %copy.129 = bf16[4,1024,1024]{1,2,0:T(8,128)(2,1)} copy(bf16[4,1024,1024]{2,1,0:T(8,128)(2,1)} %param.19) | data formatting | bytes 16777216 | tf_op args[0]
  31.5 14.6 %reshape.484 = bf16[4,4,256,1,16,64]{2,1,5,4,0,3:T(4,128)(2,1)} reshape(bf16[4,1024,1024]{1,2,0:T(8,128)(2,1)} %copy.129) | data formatting | bytes 16777216 | tf_op jit(solution)/shard_map/reshape | solution.py:36
  48.2 52.1 %while.56 = (s32[]{:T(128)}, f32[4,4,256,1,16,64]{2,5,4,1,3,0:T(8,128)}, f32[4,4,1,16,64,128]{5,4,3,0,2,1:T(8,128)}, bf16[4,4,256,1,16,64]{2,1,5,4,0,3:T(4,128)(...) while((s32[]{:T(128)}, ...), condition=%wide.region_3.4_spmd, body=%wide.region_2.3_spmd.sunk | while | flops 896614400 | bytes 18221928 | solution.py:69
  51.9 6.1 %bitcast_dynamic-update-slice_fusion.6 = f32[4,4,256,1,16,64]{2,5,4,1,3,0:T(8,128)} fusion(f32[4,4,256,1,16,64]{2,5,4,1,3,0:T(8,128)} %get-tuple-element.630, s32[]{:T(128)S(6)} %copy.219, f32[4,256,256]{2,1,0:T(8,128)S(1)} %fusion.92, f32[16,4,256]{2,0,1:T(8,128)S(1)} %get-tuple-element.603, pred[256,256]{1,0:T(8,128)(4,1)S(1)} %iota_compare_fusion.6, ...), kind=kOutput, calls=%fused_computation.41.clone.1 | convolution fusion | flops 557842432 | bytes 7536644 | tf_op jit(solution)/shard_map/while/body/eval_jaxpr/ghkqu,kughp->kqghp/dot_general | solution.py:56
  58.3 3.0 bitcast_dynamic-update-slice_fusion.7
  64.9 6.1 %bitcast_dynamic-update-slice_fusion.6 = f32[4,4,256,1,16,64]{2,5,4,1,3,0:T(8,128)} fusion(f32[4,4,256,1,16,64]{2,5,4,1,3,0:T(8,128)} %get-tuple-element.630, s32[]{:T(128)S(6)} %copy.219, f32[4,256,256]{2,1,0:T(8,128)S(1)} %fusion.92, f32[16,4,256]{2,0,1:T(8,128)S(1)} %get-tuple-element.603, pred[256,256]{1,0:T(8,128)(4,1)S(1)} %iota_compare_fusion.6, ...), kind=kOutput, calls=%fused_computation.41.clone.1 | convolution fusion | flops 557842432 | bytes 7536644 | tf_op jit(solution)/shard_map/while/body/eval_jaxpr/ghkqu,kughp->kqghp/dot_general | solution.py:56
  71.3 3.0 bitcast_dynamic-update-slice_fusion.7
  77.9 6.1 %bitcast_dynamic-update-slice_fusion.6 = f32[4,4,256,1,16,64]{2,5,4,1,3,0:T(8,128)} fusion(f32[4,4,256,1,16,64]{2,5,4,1,3,0:T(8,128)} %get-tuple-element.630, s32[]{:T(128)S(6)} %copy.219, f32[4,256,256]{2,1,0:T(8,128)S(1)} %fusion.92, f32[16,4,256]{2,0,1:T(8,128)S(1)} %get-tuple-element.603, pred[256,256]{1,0:T(8,128)(4,1)S(1)} %iota_compare_fusion.6, ...), kind=kOutput, calls=%fused_computation.41.clone.1 | convolution fusion | flops 557842432 | bytes 7536644 | tf_op jit(solution)/shard_map/while/body/eval_jaxpr/ghkqu,kughp->kqghp/dot_general | solution.py:56
  90.9 6.1 %bitcast_dynamic-update-slice_fusion.6 = f32[4,4,256,1,16,64]{2,5,4,1,3,0:T(8,128)} fusion(f32[4,4,256,1,16,64]{2,5,4,1,3,0:T(8,128)} %get-tuple-element.630, s32[]{:T(128)S(6)} %copy.219, f32[4,256,256]{2,1,0:T(8,128)S(1)} %fusion.92, f32[16,4,256]{2,0,1:T(8,128)S(1)} %get-tuple-element.603, pred[256,256]{1,0:T(8,128)(4,1)S(1)} %iota_compare_fusion.6, ...), kind=kOutput, calls=%fused_computation.41.clone.1 | convolution fusion | flops 557842432 | bytes 7536644 | tf_op jit(solution)/shard_map/while/body/eval_jaxpr/ghkqu,kughp->kqghp/dot_general | solution.py:56
  97.2 3.0 bitcast_dynamic-update-slice_fusion.7
  100.2 13.8 %while.58 = (s32[]{:T(128)}, f32[4,1,16,64,128]{4,3,2,1,0:T(8,128)S(1)}, f32[4,4,1,16,64,128]{5,4,3,1,2,0:T(8,128)}, f32[4,4,1,16]{3,0,2,1:T(4,128)S(1)}, f32[4,...) while((s32[]{:T(128)}, f32[4,1,16,64,128]{4,3,2,1,0:T(8,128)S(1)}, ...), condition=%wide.region_5.6_spmd.clone, body=%wide.region_4.5_spmd.clone.sunk | while | flops 2097155 | bytes 10487148 | solution.py:80
  115.5 8.4 %copy.152 = bf16[4,4,256,1,16,64]{2,5,4,3,1,0:T(8,128)(2,1)} copy(bf16[4,4,256,1,16,64]{2,1,5,4,0,3:T(4,128)(2,1)} %get-tuple-element.711) | data formatting | bytes 16777216 | tf_op jit(solution)/shard_map/reshape | solution.py:36
  132.4 8.3 %gather_fusion.2 = bf16[16,256,16,64]{1,3,2,0:T(8,128)(2,1)} fusion(bf16[4,4,256,1,16,64]{2,5,4,3,1,0:T(8,128)(2,1)} %copy.152, s32[16]{0:T(128)S(1)} %get-tuple-element.467), kind=kCustom, calls=%fused_computation.2 | custom fusion | bytes 16777600 | tf_op jit(solution)/shard_map/vmap()/gather | solution.py:100
  143.6 22.2 %all-gather.2 = f32[16,4,16]{2,1,0:T(4,128)S(1)} all-gather(f32[1,4,16]{2,1,0:T(4,128)S(1)} %bitcast.319), channel_id=2, replica_groups=mesh['seq'=16,'head'=8] {'seq'}, dimensions={0}, use_global_device_ids=true | all-gather | bytes 4352 | tf_op jit(solution)/shard_map/all_gather | solution.py:17
  166.7 145.6 %all-gather.5.cloned.1.call-done = f32[64,1,16,64,128]{4,3,2,1,0:T(8,128)} async-done(((f32[4,1,16,64,128]{4,3,2,1,0:T(8,128)}), f32[64,1,16,64,128]{4,3,2,1,0:T(8,128)}) %all-gather.5.cloned.1.call-update) | async-done | bytes 33554448 | tf_op jit(solution)/shard_map/all_gather | solution.py:17
  312.3 31.9 %while.59 = (s32[]{:T(128)}, f32[4,1,16,64,128]{4,3,2,1,0:T(8,128)S(1)}, s32[]{:T(128)}, f32[16,4,1,16]{3,1,2,0:T(4,128)S(1)}, f32[16,4,1,16,64,128]{5,4,3,1,2,0:T(8,128)}, /*index=5*/s32[]{:T(128)}, s32[]{:T(128)}) while((s32[]{:T(128)}, f32[4,1,16,64,128]{4,3,2,1,0:T(8,128)S(1)}, s32[]{:T(128)}, f32[16,4,1,16]{3,1,2,0:T(4,128)S(1)}, ...), condition=%wide.region_9.10_spmd.clone, body=%wide.region_8.9_spmd.clone.sunk | while | flops 2097156 | bytes 6292337 | solution.py:26
  344.2 6.0 bitcast_add_fusion.2
  350.2 7.7 %gather_fusion.1 = f32[16,16,64,128]{3,2,1,0:T(8,128)} fusion(f32[4,4,1,16,64,128]{5,4,3,2,1,0:T(8,128)} %bitcast_add_fusion.2, s32[16]{0:T(128)S(1)} %get-tuple-element.468), kind=kCustom, calls=%fused_computation.1 | custom fusion | bytes 16777600 | tf_op jit(solution)/shard_map/vmap()/gather | solution.py:99
  357.9 11.9 %select_bitcast_fusion = f32[16,1,1,16,64,128]{5,4,3,2,1,0:T(8,128)} fusion(f32[16,16,64,128]{3,2,1,0:T(8,128)} %gather_fusion.1, f32[16,16]{1,0:T(8,128)S(1)} %exp.116, pred[16]{0:T(512)(128)(4,1)S(1)} %get-tuple-element.461, bf16[16,256,16,64]{1,3,2,0:T(8,128)(2,1)} %gather_fusion.2, f32[16,256,16]{1,2,0:T(8,128)S(1)} %copy-done.5, ...), kind=kOutput, calls=%fused_computation.75 | convolution fusion | flops 1092616192 | bytes 26477584 | tf_op jit(solution)/shard_map/vmap(qghp,qgn->ghpn)/dot_general | solution.py:109
  369.8 7.3 %all-to-all-start = ((f32[16,1,1,16,64,128]{5,4,3,2,1,0:T(8,128)}), f32[16,1,1,16,64,128]{5,4,3,2,1,0:T(8,128)}, u32[]{:S(2)}, u32[]{:S(2)}) async-start(f32[16,1,1,16,64,128]{5,4,3,2,1,0:T(8,128)} %select_bitcast_fusion), calls=%async_computation | async-start | bytes 16777216 | tf_op jit(solution)/shard_map/all_to_all | solution.py:174
  377.2 3.0 reduce_window_sum.50
  386.9 17.9 %while.57 = (s32[]{:T(128)}, f32[6,1,64,1,16,64]{2,5,4,3,1,0:T(8,128)}, bf16[6,1,64,1,16,64]{2,5,4,3,1,0:T(8,128)(2,1)}, f32[6,1,16,1,64]{4,2,3,1,0:T(8,128)S(1)...) while((s32[]{:T(128)}, ...), condition=%wide.region_14.15_spmd, body=%wide.region_13.14_spmd.sunk | while | flops 9768962 | bytes 907353 | solution.py:69
  404.8 16.5 %multiply_reduce_fusion = (f32[4,4,256]{2,1,0:T(4,128)S(1)}, f32[4,4,256,1,16,64]{2,5,4,1,0,3:T(8,128)}) fusion(bf16[4,4,256,128,1]{3,2,4,1,0:T(8,128)(2,1)S(1)} %bitcast.300, f32[4,4,256,16]{2,3,1,0:T(8,128)S(1)} %copy-done.4, f32[4,4,256,1,16,64]{2,5,4,1,3,0:T(8,128)} %get-tuple-element.225, f32[4,16,64,128]{3,2,1,0:T(8,128)S(1)} %bitcast.295, ...), kind=kOutput, calls=%fused_computation.68 | convolution fusion | flops 6463418368 | bytes 45368320 | tf_op jit(solution)/shard_map/rkqgn,krghpn->rkqghp/dot_general | solution.py:87
  421.2 20.9 %copy.145 = f32[4,4,256,1,16,64]{2,1,5,4,0,3:T(4,128)} copy(f32[4,4,256,1,16,64]{2,5,4,1,0,3:T(8,128)} %get-tuple-element.472) | data formatting | bytes 33554432 | tf_op jit(solution)/shard_map/add | solution.py:156
  442.2 20.8 %reshape.494 = f32[4,1024,1024]{1,2,0:T(8,128)} reshape(f32[4,4,256,1,16,64]{2,1,5,4,0,3:T(4,128)} %copy.145) | data formatting | bytes 33554432 | tf_op jit(solution)/shard_map/reshape | solution.py:183
  463.0 63.3 %all-to-all-done = f32[16,1,1,16,64,128]{5,4,3,2,1,0:T(8,128)} async-done(((f32[16,1,1,16,64,128]{5,4,3,2,1,0:T(8,128)}), f32[16,1,1,16,64,128]{5,4,3,2,1,0:T(8,128)}, u32[]{:S(2)}, u32[]{:S(2)}) %all-to-all-start) | async-done | bytes 8388640 | tf_op jit(solution)/shard_map/all_to_all | solution.py:174
  526.3 8.2 %copy.207 = f32[2,8,1024,128]{3,1,2,0:T(8,128)S(1)} copy(f32[2,8,1024,128]{3,2,1,0:T(8,128)} %bitcast.123) | data formatting | bytes 16777216
  536.2 8.5 %fusion.49 = f32[6,16,64,128]{3,0,2,1:T(8,128)S(1)} fusion(f32[16,64,128,16]{2,1,0,3:T(8,128)S(1)} %bitcast.296, f32[6,16]{0,1:T(8,128)S(1)} %bitcast.318, s32[6]{0:T(128)S(1)} %copy-done.11), kind=kOutput, calls=%fused_computation.82 | convolution fusion | flops 151781472 | bytes 11534744 | tf_op jit(solution)/shard_map/dot_general | solution.py:175
  547.1 24.3 %all-reduce.1 = (f32[4,1024]{1,0:T(4,128)S(1)}, f32[6,64]{1,0:T(8,128)S(1)}) all-reduce(f32[4,1024]{1,0:T(4,128)S(1)} %bitcast.315, f32[6,64]{1,0:T(8,128)S(1)} %get-tuple-element.473), channel_id=1, replica_groups=mesh['seq'=16,'head'=8] {'head'}, use_global_device_ids=true, to_apply=%region_11.12 | all-reduce | flops 4480 | bytes 35840 | tf_op jit(solution)/shard_map/psum | solution.py:185
  571.4 9.9 %multiply_convert_fusion.10 = bf16[4,1024,1024]{1,2,0:T(8,128)(2,1)} fusion(f32[4,1024,1024]{1,2,0:T(8,128)} %reshape.494, f32[1024]{0:T(1024)S(1)} %copy-done.10, f32[4,1024]{1,0:T(4,128)S(1)} %add_rsqrt_fusion), kind=kLoop, calls=%fused_computation.67 | loop fusion | flops 12582912 | bytes 25186304 | tf_op jit(solution)/shard_map/convert_element_type | solution.py:190
  581.3 11.3 %copy.160 = bf16[4,1024,1024]{2,1,0:T(8,128)(2,1)} copy(bf16[4,1024,1024]{1,2,0:T(8,128)(2,1)} %multiply_convert_fusion.10) | data formatting | bytes 16777216
  (171 shorter events, 116.3 us)
Async XLA Ops:
  7.2 305.2 %all-gather.5.cloned.1.call-start = ((), (), s32[]{:S(2)}) async-start(), calls=%async_computation.1 | async-start | bytes 35651584 | tf_op jit(solution)/shard_map/all_gather | solution.py:17
  31.5 16.6 %copy-start.1 = (bf16[4,1024,128]{2,1,0:T(8,128)(2,1)S(1)}, bf16[4,1024,128]{2,1,0:T(8,128)(2,1)}, u32[]{:S(2)}) copy-start(bf16[4,1024,128]{2,1,0:T(8,128)(2,1)} %param.21) | copy-start | bytes 3145732
  114.1 1.3 copy-start
  115.4 8.5 %copy-start.13 = (s32[96]{0:T(128)S(1)}, s32[96]{0:T(128)}, u32[]{:S(2)}) copy-start(s32[96]{0:T(128)} %param.29) | copy-start | bytes 1156
  115.4 8.6 %copy-start.12 = (s32[96]{0:T(128)S(1)}, s32[96]{0:T(128)}, u32[]{:S(2)}) copy-start(s32[96]{0:T(128)} %param.28) | copy-start | bytes 1156
  123.9 220.3 %copy-start.7 = (f32[4,4,16]{2,1,0:T(4,128)}, f32[4,4,16]{2,1,0:T(4,128)S(1)}, u32[]{:S(2)}) copy-start(f32[4,4,16]{2,1,0:T(4,128)S(1)} %copy.139) | copy-start | bytes 3076
  132.4 33.5 %copy-start.3 = (f32[16,16,256]{2,1,0:T(8,128)S(1)}, f32[16,16,256]{2,1,0:T(8,128)}, u32[]{:S(2)}) copy-start(f32[16,16,256]{2,1,0:T(8,128)} %gather_fusion) | copy-start | bytes 786436
  350.2 7.7 %copy-start.5 = (f32[16,256,16]{1,2,0:T(8,128)S(1)}, f32[16,256,16]{1,2,0:T(8,128)}, u32[]{:S(2)}) copy-start(f32[16,256,16]{1,2,0:T(8,128)} %select_bitcast_fusion.1) | copy-start | bytes 786436
  369.8 17.1 %copy-start.6 = (bf16[6,64,128]{2,1,0:T(8,128)(2,1)S(1)}, bf16[6,64,128]{2,1,0:T(8,128)(2,1)}, u32[]{:S(2)}) copy-start(bf16[6,64,128]{2,1,0:T(8,128)(2,1)} %param.26) | copy-start | bytes 294916
  369.8 156.5 %all-to-all-start = ((f32[16,1,1,16,64,128]{5,4,3,2,1,0:T(8,128)}), f32[16,1,1,16,64,128]{5,4,3,2,1,0:T(8,128)}, u32[]{:S(2)}, u32[]{:S(2)}) async-start(f32[16,1,1,16,64,128]{5,4,3,2,1,0:T(8,128)} %select_bitcast_fusion), calls=%async_computation | async-start | bytes 16777216 | tf_op jit(solution)/shard_map/all_to_all | solution.py:174
  377.2 27.6 %copy-start.4 = (f32[4,4,256,16]{2,3,1,0:T(8,128)S(1)}, f32[4,4,256,16]{2,3,1,0:T(8,128)}, u32[]{:S(2)}) copy-start(f32[4,4,256,16]{2,3,1,0:T(8,128)} %get-tuple-element.463) | copy-start | bytes 786436
  534.5 1.7 copy-start.9
  534.5 1.7 copy-start.11
  536.2 8.6 %copy-start.2 = (f32[6,1,64,1,16,64]{2,5,4,3,1,0:T(8,128)S(1)}, f32[6,1,64,1,16,64]{2,5,4,3,1,0:T(8,128)}, u32[]{:S(2)}) copy-start(f32[6,1,64,1,16,64]{2,5,4,3,1,0:T(8,128)} %get-tuple-element.230) | copy-start | bytes 4718596
  536.2 8.6 %copy-start.8 = (f32[6,64,16]{1,2,0:T(8,128)S(1)}, f32[6,64,16]{1,2,0:T(8,128)}, u32[]{:S(2)}) copy-start(f32[6,64,16]{1,2,0:T(8,128)} %exponential_bitcast_fusion.4) | copy-start | bytes 73732
  536.2 35.2 %copy-start.10 = (f32[1024]{0:T(1024)S(1)}, f32[1024]{0:T(1024)}, u32[]{:S(2)}) copy-start(f32[1024]{0:T(1024)} %param.23) | copy-start | bytes 12292
Sparse Core Ops, SparseCore 0:
  115.5 196.7 all-gather.4
where the time goes:
time: 614 us; the launch traced here: 604 us
  waiting for transfers between devices  209 us (34%)
  local copies, waits for them, and re-layouts  147 us (24%)
  matrix products  98.2 us (16%)
  other arithmetic  81.2 us (13%)
  blocking collectives  46.5 us (8%)
  between operations  14.6 us (2%)
  starting transfers between devices  7.38 us (1%)
    all_gather x1, waiting for transfers between devices, entering(): pieces = jax.tree.map(lambda part: lax.all_gather(part, axis), value)  146 us
    all_to_all x1, waiting for transfers between devices, local(): lax.all_to_all(outgoing[:, None], 'seq', split_axis=0, concat_axis=0, til...  63.3 us
    dot_general x10, matrix products, one_row(): jnp.einsum('ghkqu,kughp->kqghp', weights.astype(jnp.bfloat16), row_x, pre...  37 us
    unnamed x34, local copies, waits for them, and re-layouts  36.4 us
    select_n x15, other arithmetic, turn(): jnp.where(position < mine, new, old)  31.2 us
    psum x1, blocking collectives, local(): lax.psum((jnp.sum(main_flat * main_flat, axis=-1), jnp.sum(probe_flat * p...  24.3 us
    reshape x2, local copies, waits for them, and re-layouts, split_heads(): seq_x.reshape(row_count, block_count, block_len, groups_dev, per_group, h...  23 us
    all_gather x1, blocking collectives, entering(): pieces = jax.tree.map(lambda part: lax.all_gather(part, axis), value)  22.2 us
  transfers between devices with their start and end apart: 2, of which 2 were waited for; matrix products, arithmetic and copies ran while one was open for 19% of the time, Pallas kernels for 0%

commit v1 on v0

v1 whole, which is shorter than its diff:
```python
import functools

import jax
import jax.numpy as jnp
from jax import lax
from jax.experimental import pallas as pl
from jax.experimental.pallas import tpu as pltpu
from jax.sharding import PartitionSpec as P

F32 = jnp.float32
BF16 = jnp.bfloat16
DSTATE = 128
DIN = 8192
EPSILON = 1e-05
BLOCK = 128
EXTRA = 16


def dot(left, right, left_dim, right_dim, precision=None):
    return lax.dot_general(
        left,
        right,
        (((left_dim,), (right_dim,)), ((), ())),
        precision=precision,
        preferred_element_type=F32,
    )


def pieces(value, count):
    parts = []
    for _ in range(count):
        part = value.astype(BF16)
        parts.append(part)
        value = value - part.astype(F32)
    return parts


def spread(heads, width):
    shape = (heads, width)
    head = lax.broadcasted_iota(jnp.int32, shape, 0)
    channel = lax.broadcasted_iota(jnp.int32, shape, 1)
    per_head = width // heads
    return jnp.where(lax.div(channel, jnp.int32(per_head)) == head, 1.0, 0.0).astype(F32)


def spread_twice(one):
    half = one.astype(BF16)
    return jnp.concatenate([half, half], axis=0)


def widen(value, twice):
    return dot(jnp.concatenate(pieces(value, 2), axis=0), twice, 0, 0)


def widen_column(column, one):
    return jnp.sum(column * one, axis=0, keepdims=True)


def prefix(decay, length):
    heads = decay.shape[0]
    count = decay.shape[1] // length
    parts = pieces(decay, 3)
    rows = [part[:, k * length : (k + 1) * length] for k in range(count) for part in parts]
    shape = (length, length)
    upto = (
        lax.broadcasted_iota(jnp.int32, shape, 0) <= lax.broadcasted_iota(jnp.int32, shape, 1)
    )
    total = dot(jnp.concatenate(rows, axis=0), jnp.where(upto, 1.0, 0.0).astype(BF16), 1, 0)
    out = []
    for k in range(count):
        base = 3 * heads * k
        out.append(
            total[base : base + heads]
            + total[base + heads : base + 2 * heads]
            + total[base + 2 * heads : base + 3 * heads]
        )
    return out


def causal(queries, keys):
    shape = (queries, keys)
    return lax.broadcasted_iota(jnp.int32, shape, 0) >= lax.broadcasted_iota(jnp.int32, shape, 1)


def route_kernel(position_ref, me_ref, reads_ref, decay_ref, out_ref, *, seq_dev):
    slots = out_ref.shape[0]
    probe_dev, probe_len, _ = reads_ref.shape
    rows, heads, length = decay_ref.shape
    decay = decay_ref[...].reshape(rows * heads, length)
    ones = jnp.ones((EXTRA, length), BF16)
    fill = jnp.zeros((DSTATE - rows * heads, length), BF16)
    total = 0.0
    for part in pieces(decay, 3):
        total = total + dot(ones, jnp.concatenate([part, fill], axis=0), 1, 1)
    row = lax.broadcasted_iota(jnp.int32, (EXTRA, DSTATE), 0)
    block = jnp.zeros((EXTRA, DSTATE), F32)
    for index, part in enumerate(pieces(total, 3)):
        block = jnp.where(row == index, part.astype(F32), block)
    block = block.astype(BF16)
    nothing = jnp.zeros((probe_len, DSTATE), BF16)
    for slot in range(slots):
        out_ref[slot, 0:probe_len, :] = nothing
        out_ref[slot, probe_len : probe_len + EXTRA, :] = block
    for probe in range(probe_dev):
        owner = lax.div(position_ref[me_ref[0] * probe_dev + probe], jnp.int32(seq_dev))
        out_ref[owner, 0:probe_len, :] = reads_ref[probe]


def end_kernel(x_ref, in_ref, decay_ref, out_ref, scaled_ref):
    _, length, width = x_ref.shape
    heads = decay_ref.shape[1]
    twice = spread_twice(spread(heads, width))
    sums = prefix(decay_ref[0], BLOCK)
    after = jnp.zeros((heads, 1), F32)
    for k in reversed(range(length // BLOCK)):
        rows = slice(k * BLOCK, (k + 1) * BLOCK)
        last = sums[k][:, BLOCK - 1 : BLOCK]
        factor = widen(jnp.exp((last - sums[k]) + after), twice)
        scaled_ref[rows, :] = (x_ref[0, rows, :].astype(F32) * factor).astype(BF16)
        after = after + last
    out_ref[0] = dot(in_ref[0], scaled_ref[...], 0, 0).astype(BF16)


def find_slot(slot, position_ref, premise_ref, me, probe_dev, seq_dev):
    offset = jnp.int32(0)
    premise = jnp.int32(0)
    present = jnp.int32(0)
    for probe in range(probe_dev):
        position = position_ref[slot * probe_dev + probe]
        here = lax.div(position, jnp.int32(seq_dev)) == me
        offset = jnp.where(here, position - me * seq_dev, offset)
        premise = jnp.where(here, premise_ref[slot * probe_dev + probe], premise)
        present = jnp.where(here, jnp.int32(1), present)
    return offset, premise, present


def chain_factors(sums, one):
    middle = BLOCK // 2 - 1
    factors = []
    tail = None
    for k in range(len(sums)):
        mid = sums[k][:, middle : middle + 1]
        step = mid if tail is None else tail + mid
        factors.append(widen_column(jnp.exp(step), one))
        tail = sums[k][:, BLOCK - 1 : BLOCK] - mid
    return factors


def branch_kernel(
    position_ref,
    premise_ref,
    me_ref,
    x_ref,
    in_ref,
    decay_ref,
    routed_ref,
    out_ref,
    scale_ref,
    right_ref,
    state_ref,
    near_ref,
    far_ref,
    *,
    seq_dev,
    probe_dev,
):
    _, length, width = x_ref.shape
    heads = decay_ref.shape[1]
    slots, probe_len, _ = out_ref.shape
    row = pl.program_id(0)
    middle = BLOCK // 2 - 1

    @pl.when(row == 0)
    def _():
        out_ref[...] = jnp.zeros_like(out_ref)
        scale_ref[...] = jnp.zeros_like(scale_ref)

    one = spread(heads, width)
    twice = spread_twice(one)
    sums = prefix(decay_ref[0], BLOCK)
    factors = chain_factors(sums, one)
    before = jnp.zeros((heads, 1), F32)
    state_ref[...] = jnp.zeros_like(state_ref)
    for k in range(length // BLOCK):
        rows = slice(k * BLOCK, (k + 1) * BLOCK)
        near = sums[k] - sums[k][:, middle : middle + 1]
        near_ref[k] = near
        far_ref[k] = sums[k] + before
        before = before + sums[k][:, BLOCK - 1 : BLOCK]
        scaled = (x_ref[0, rows, :].astype(F32) * widen(jnp.exp(-near), twice)).astype(BF16)
        right_ref[k, 0:BLOCK, :] = scaled
        state = state_ref[...] * factors[k]
        right_ref[k, BLOCK : BLOCK + DSTATE, :] = state.astype(BF16)
        state_ref[...] = state + dot(in_ref[0, rows, :], scaled, 0, 0)

    def one_slot(slot, carry):
        offset, premise, present = find_slot(
            slot, position_ref, premise_ref, me_ref[0], probe_dev, seq_dev
        )

        @pl.when((present == 1) & (premise == row))
        def _():
            k = lax.div(offset, jnp.int32(BLOCK))
            within = offset - k * BLOCK
            reads = routed_ref[slot, 0:probe_len, :]
            inputs = in_ref[0, pl.ds(pl.multiple_of(k * BLOCK, BLOCK), BLOCK), :]
            keep = lax.broadcasted_iota(jnp.int32, (probe_len, BLOCK), 1) <= within
            gram = jnp.where(keep, dot(reads, inputs, 1, 1), 0.0).astype(BF16)
            product = dot(jnp.concatenate([gram, reads], axis=1), right_ref[k], 1, 0)
            here = lax.broadcasted_iota(jnp.int32, (heads, BLOCK), 1) == within

            def at(ref):
                value = jnp.sum(jnp.where(here, ref[k], 0.0), axis=1, keepdims=True)
                return widen_column(jnp.exp(value), one)

            out_ref[slot] = product * at(near_ref)
            scale_ref[slot] = jnp.broadcast_to(at(far_ref), (8, width))

        return carry

    lax.fori_loop(0, slots, one_slot, 0)


def scan_kernel(me_ref, part_ref, routed_ref, out_ref, *, probe_len, heads, rows):
    count, height, width = part_ref.shape
    premise = lax.div(me_ref[0] * height, jnp.int32(DSTATE))
    shape = (DSTATE, width)
    lane = lax.broadcasted_iota(jnp.int32, shape, 0) - premise * heads
    channel = lax.broadcasted_iota(jnp.int32, shape, 1)
    pick = jnp.where(lax.div(channel, jnp.int32(width // heads)) == lane, 1.0, 0.0).astype(BF16)
    state = jnp.zeros((height, width), F32)
    for k in range(count):
        out_ref[k] = state.astype(BF16)
        total = dot(routed_ref[k, probe_len : probe_len + EXTRA, :], pick, 1, 0)
        total = jnp.sum(total[0:8], axis=0, keepdims=True)
        state = state * jnp.exp(total) + part_ref[k].astype(F32)


def apply_kernel(
    position_ref,
    premise_ref,
    me_ref,
    incoming_ref,
    routed_ref,
    local_ref,
    scale_ref,
    out_ref,
    *,
    seq_dev,
    probe_dev,
):
    step, probe_len, _ = out_ref.shape
    for index in range(step):
        slot = pl.program_id(0) * step + index
        _, premise, _ = find_slot(slot, position_ref, premise_ref, me_ref[0], probe_dev, seq_dev)
        product = dot(routed_ref[index, 0:probe_len, :], incoming_ref[premise], 1, 0)
        out_ref[index] = (product * scale_ref[index, 0:1, :] + local_ref[index]).astype(BF16)


def squares(mixed):
    total = mixed[:, 0:128] * mixed[:, 0:128]
    for k in range(1, mixed.shape[1] // 128):
        part = mixed[:, 128 * k : 128 * (k + 1)]
        total = total + part * part
    return dot(jnp.ones((8, 128), F32), total, 1, 1, lax.Precision.HIGHEST)


def main_kernel(
    x_ref, in_ref, read_ref, decay_ref, incoming_ref, out_ref, square_ref, right_ref, state_ref
):
    _, length, width = x_ref.shape
    heads = decay_ref.shape[1]
    middle = BLOCK // 2 - 1
    one = spread(heads, width)
    twice = spread_twice(one)
    sums = prefix(decay_ref[0], BLOCK)
    factors = chain_factors(sums, one)
    mask = causal(BLOCK, BLOCK)
    line = lax.broadcasted_iota(jnp.int32, (8, BLOCK), 0)
    total = jnp.zeros((8, BLOCK), F32)
    state_ref[...] = incoming_ref[0].astype(F32)
    for k in range(length // BLOCK):
        rows = slice(k * BLOCK, (k + 1) * BLOCK)
        near = sums[k] - sums[k][:, middle : middle + 1]
        inputs = in_ref[0, rows, :]
        reads = read_ref[0, rows, :]
        scaled = (x_ref[0, rows, :].astype(F32) * widen(jnp.exp(-near), twice)).astype(BF16)
        right = right_ref.at[k % 2]
        right[0:BLOCK, :] = scaled
        state = state_ref[...] * factors[k]
        right[BLOCK : BLOCK + DSTATE, :] = state.astype(BF16)
        state_ref[...] = state + dot(inputs, scaled, 0, 0)
        gram = jnp.where(mask, dot(reads, inputs, 1, 1), 0.0).astype(BF16)
        product = dot(jnp.concatenate([gram, reads], axis=1), right[...], 1, 0)
        mixed = product * widen(jnp.exp(near), twice)
        out_ref[0, rows, :] = mixed
        total = jnp.where(line == k, squares(mixed), total)
    for copy in range(square_ref.shape[0]):
        square_ref[copy, 0] = total


def probe_kernel(
    position_ref,
    me_ref,
    x_ref,
    in_ref,
    read_ref,
    decay_ref,
    arrived_ref,
    out_ref,
    square_ref,
    *,
    seq_dev,
):
    probe_dev, length, width = x_ref.shape
    heads = decay_ref.shape[1]
    twice = spread_twice(spread(heads, width))
    mask = causal(length, length)
    line = lax.broadcasted_iota(jnp.int32, (8, 128), 0)
    total = jnp.zeros((8, 128), F32)
    pair = 128 // length
    for probe in range(probe_dev):
        owner = lax.div(position_ref[me_ref[0] * probe_dev + probe], jnp.int32(seq_dev))
        sums = prefix(decay_ref[probe], length)[0]
        inputs = in_ref[probe]
        scaled = (x_ref[probe].astype(F32) * widen(jnp.exp(-sums), twice)).astype(BF16)
        gram = jnp.where(mask, dot(read_ref[probe], inputs, 1, 1), 0.0).astype(BF16)
        product = dot(gram, scaled, 1, 0) + arrived_ref[owner].astype(F32)
        out_ref[0, probe * length : (probe + 1) * length, :] = product * widen(
            jnp.exp(sums), twice
        )
    for k in range(probe_dev // pair):
        total = jnp.where(line == k, squares(out_ref[0, 128 * k : 128 * (k + 1), :]), total)
    for copy in range(square_ref.shape[0]):
        square_ref[copy, 0] = total


def norm_kernel(mixed_ref, square_ref, gain_ref, out_ref):
    _, length, width = mixed_ref.shape
    total = jnp.sum(square_ref[:, 0], axis=0)
    rate = lax.rsqrt(total / DIN + EPSILON)
    high, low = (part.astype(F32) for part in pieces(rate, 2))
    left = jnp.concatenate([high, low, high, low], axis=0).astype(BF16)
    gain = gain_ref[...]
    gain_high, gain_low = (part.astype(F32) for part in pieces(gain, 2))
    shape = (32, width)
    line = lax.broadcasted_iota(jnp.int32, shape, 0)
    both = jnp.where(
        line < 16, jnp.broadcast_to(gain_high, shape), jnp.broadcast_to(gain_low, shape)
    )
    for k in range(length // 128):
        rows = slice(128 * k, 128 * (k + 1))
        right = jnp.where(lax.rem(line, 8) == k, both, 0.0).astype(BF16)
        out_ref[0, rows, :] = (mixed_ref[0, rows, :] * dot(left, right, 0, 0)).astype(BF16)


SMEM = pl.BlockSpec(memory_space=pltpu.SMEM)


def whole(shape):
    return pl.BlockSpec(shape, lambda *_: (0,) * len(shape))


def along(shape, dim=0):
    return pl.BlockSpec(shape, lambda i: tuple(i if d == dim else 0 for d in range(len(shape))))


def call(kernel, name, grid, in_specs, out_specs, out_shape, scratch=(), flops=0, moved=0):
    return pl.pallas_call(
        kernel,
        name=name,
        grid=grid,
        in_specs=in_specs,
        out_specs=out_specs,
        out_shape=out_shape,
        scratch_shapes=list(scratch),
        compiler_params=pltpu.CompilerParams(vmem_limit_bytes=58 * 1024 * 1024),
        cost_estimate=pl.CostEstimate(flops=flops, bytes_accessed=moved, transcendentals=0),
    )


def shaped(shape, dtype):
    return jax.ShapeDtypeStruct(shape, dtype)


def exchange(value, axis):
    return lax.all_to_all(value, axis, split_axis=0, concat_axis=0, tiled=True)


def local(
    tokens,
    state_inputs,
    state_reads,
    log_decay,
    norm_gain,
    probe_tokens,
    probe_inputs,
    probe_reads,
    probe_decay,
    branch_premise,
    branch_position,
):
    seq = lax.axis_size("seq")
    ring = lax.axis_size("head")
    me = lax.axis_index("seq").astype(jnp.int32).reshape(1)
    row_count, seq_dev, width = tokens.shape
    heads = log_decay.shape[1]
    probe_dev, probe_len, _ = probe_tokens.shape
    height = row_count * DSTATE // seq
    routed_shape = (seq, probe_len + EXTRA, DSTATE)

    routed = call(
        functools.partial(route_kernel, seq_dev=seq_dev),
        "route",
        (1,),
        [SMEM, SMEM, whole(probe_reads.shape), whole(log_decay.shape)],
        whole(routed_shape),
        shaped(routed_shape, BF16),
        moved=800_000,
    )(branch_position, me, probe_reads, log_decay)
    routed = exchange(routed, "seq")

    x_spec = along((1, seq_dev, width))
    in_spec = along((1, seq_dev, DSTATE))
    decay_spec = along((1, heads, seq_dev))
    state_spec = along((1, DSTATE, width))
    ends = call(
        end_kernel,
        "ends",
        (row_count,),
        [x_spec, in_spec, decay_spec],
        state_spec,
        shaped((row_count, DSTATE, width), BF16),
        [pltpu.VMEM((seq_dev, width), BF16)],
        flops=4_000_000_000,
        moved=11_000_000,
    )(tokens, state_inputs, log_decay)
    parts = exchange(ends.reshape(seq, height, width), "seq")

    count = seq_dev // BLOCK
    local_part, scale = call(
        functools.partial(branch_kernel, seq_dev=seq_dev, probe_dev=probe_dev),
        "branch",
        (row_count,),
        [SMEM, SMEM, SMEM, x_spec, in_spec, decay_spec, whole(routed_shape)],
        [whole((seq, probe_len, width)), whole((seq, 8, width))],
        [shaped((seq, probe_len, width), F32), shaped((seq, 8, width), F32)],
        [
            pltpu.VMEM((count, BLOCK + DSTATE, width), BF16),
            pltpu.VMEM((DSTATE, width), F32),
            pltpu.VMEM((count, heads, BLOCK), F32),
            pltpu.VMEM((count, heads, BLOCK), F32),
        ],
        flops=10_000_000_000,
        moved=14_000_000,
    )(branch_position, branch_premise, me, tokens, state_inputs, log_decay, routed)

    starts = call(
        functools.partial(scan_kernel, probe_len=probe_len, heads=heads, rows=row_count),
        "scan",
        (1,),
        [SMEM, whole((seq, height, width)), whole(routed_shape)],
        whole((seq, height, width)),
        shaped((seq, height, width), BF16),
        flops=1_000_000_000,
        moved=2_500_000,
    )(me, parts, routed)
    incoming = exchange(starts, "seq").reshape(row_count, DSTATE, width)

    step = 4
    answers = call(
        functools.partial(apply_kernel, seq_dev=seq_dev, probe_dev=probe_dev),
        "apply",
        (seq // step,),
        [
            SMEM,
            SMEM,
            SMEM,
            whole((row_count, DSTATE, width)),
            along((step,) + routed_shape[1:]),
            along((step, probe_len, width)),
            along((step, 8, width)),
        ],
        along((step, probe_len, width)),
        shaped((seq, probe_len, width), BF16),
        flops=1_000_000_000,
        moved=8_000_000,
    )(branch_position, branch_premise, me, incoming, routed, local_part, scale)
    arrived = exchange(answers, "seq")

    mixed, square = call(
        main_kernel,
        "main",
        (row_count,),
        [x_spec, in_spec, in_spec, decay_spec, state_spec],
        [x_spec, along((ring, 1, 8, 128), 1)],
        [shaped(tokens.shape, F32), shaped((ring, row_count, 8, 128), F32)],
        [pltpu.VMEM((2, BLOCK + DSTATE, width), BF16), pltpu.VMEM((DSTATE, width), F32)],
        flops=12_000_000_000,
        moved=28_000_000,
    )(tokens, state_inputs, state_reads, log_decay, incoming)
    square = exchange(square, "head")
    gain = norm_gain.reshape(1, width)
    premise_out = call(
        norm_kernel,
        "norm",
        (row_count,),
        [x_spec, along((ring, 1, 8, 128), 1), whole((1, width))],
        x_spec,
        shaped(tokens.shape, BF16),
        flops=2_000_000_000,
        moved=25_000_000,
    )(mixed, square, gain)

    probe_rows = (1, probe_dev * probe_len, width)
    probe_mixed, probe_square = call(
        functools.partial(probe_kernel, seq_dev=seq_dev),
        "probes",
        (1,),
        [SMEM, SMEM]
        + [
            whole(part.shape)
            for part in (probe_tokens, probe_inputs, probe_reads, probe_decay, arrived)
        ],
        [whole(probe_rows), whole((ring, 1, 8, 128))],
        [shaped(probe_rows, F32), shaped((ring, 1, 8, 128), F32)],
        flops=1_000_000_000,
        moved=5_000_000,
    )(
        branch_position,
        me,
        probe_tokens,
        probe_inputs,
        probe_reads,
        probe_decay,
        arrived,
    )
    probe_square = exchange(probe_square, "head")
    probe_out = call(
        norm_kernel,
        "probe_norm",
        (1,),
        [whole(probe_rows), whole((ring, 1, 8, 128)), whole((1, width))],
        whole(probe_rows),
        shaped(probe_rows, BF16),
        flops=100_000_000,
        moved=2_000_000,
    )(probe_mixed, probe_square, gain)
    return (premise_out, probe_out.reshape(probe_dev, probe_len, width))


def solution(mesh):
    return jax.shard_map(
        local,
        mesh=mesh,
        in_specs=(
            P(None, "seq", "head"),
            P(None, "seq", "head"),
            P(None, "seq", "head"),
            P(None, "head", "seq"),
            P("head"),
            P("seq", None, "head"),
            P("seq", None, "head"),
            P("seq", None, "head"),
            P("seq", "head", None),
            P(),
            P(),
        ),
        out_specs=(P(None, "seq", "head"), P("seq", None, "head")),
        check_vma=False,
    )
```

time: 614 us -> 143 us (0.23)
  the two profiles are of different devices: /device:TPU:112 before, /device:TPU:1 now
where the time goes in v1:
time: 143 us; the launch traced here: 141 us
  Pallas kernels  82 us (57%)
  starting transfers between devices  35.8 us (25%)
  blocking collectives  21.3 us (15%)
  local copies, waits for them, and re-layouts  1.57 us (1%)
    all_to_all x5, starting transfers between devices, exchange(): return lax.all_to_all(value, axis, split_axis=0, concat_axis=0, tiled=True)  35.8 us
    pallas_call x1, Pallas kernels, local(): call(main_kernel, 'main', (row_count,), [x_spec, in_spec, in_spec, decay_...  26.4 us
    all_to_all x1, blocking collectives, exchange(): return lax.all_to_all(value, axis, split_axis=0, concat_axis=0, tiled=True)  21.3 us
    pallas_call x1, Pallas kernels, local(): call(functools.partial(branch_kernel, seq_dev=seq_dev, probe_dev=probe_de...  17.6 us
    pallas_call x1, Pallas kernels, local(): call(norm_kernel, 'norm', (row_count,), [x_spec, along((ring, 1, 8, 128),...  9.94 us
    pallas_call x1, Pallas kernels, local(): call(end_kernel, 'ends', (row_count,), [x_spec, in_spec, decay_spec], sta...  8.98 us
    pallas_call x1, Pallas kernels, local(): call(functools.partial(probe_kernel, seq_dev=seq_dev), 'probes', (1,), [S...  5.94 us
    pallas_call x1, Pallas kernels, local(): call(functools.partial(apply_kernel, seq_dev=seq_dev, probe_dev=probe_dev...  5.53 us
  transfers between devices with their start and end apart: 5, of which 0 were waited for; matrix products, arithmetic and copies ran while one was open for 0% of the time, Pallas kernels for 49%

profile of v1, /device:TPU:1, one launch (start us, length us, event | category | flops | bytes accessed | tf_op | source)
XLA Modules:
  0.0 141.4 jit_solution(10583749490347306927)
XLA Ops:
  0.6 2.0 %route.1 = bf16[16,80,128]{2,1,0:T(8,128)(2,1)} custom-call(s32[96]{0:T(128)} %position_ref.7, s32[1]{0:T(128)} %bitcast.me_ref, bf16[6,64,128]{2,1,0:T(8,128)(2,1)} %read_ref.3, f32[4,16,1024]{2,1,0:T(8,128)} %decay_ref.8), custom_call_target="tpu_custom_call" | custom-call | bytes 800000 | tf_op jit(solution)/shard_map/route/pallas_call | solution.py:412
  2.6 8.6 %all-to-all-start.1 = ((bf16[16,80,128]{2,1,0:T(8,128)(2,1)}), bf16[16,80,128]{2,1,0:T(8,128)(2,1)S(1)}, u32[]{:S(2)}, u32[]{:S(2)}) async-start(bf16[16,80,128]{2,1,0:T(8,128)(2,1)} %route.1), calls=%async_computation.1 | async-start | bytes 655360 | tf_op jit(solution)/shard_map/all_to_all | solution.py:387
  11.2 9.0 %ends.1 = bf16[4,128,1024]{2,1,0:T(8,128)(2,1)} custom-call(bf16[4,1024,1024]{2,1,0:T(8,128)(2,1)} %x_ref.6, bf16[4,1024,128]{2,1,0:T(8,128)(2,1)} %in_ref.6, f32[4,16,1024]{2,1,0:T(8,128)} %decay_ref.8), custom_call_target="tpu_custom_call" | custom-call | flops 4000000000 | bytes 11000000 | tf_op jit(solution)/shard_map/ends/pallas_call | solution.py:427
  20.2 0.0 all-to-all-done.1.routed_ref
  20.2 0.0 copy-start.2
  20.2 21.3 %all_to_all.30.part_ref = bf16[16,32,1024]{2,1,0:T(8,128)(2,1)} all-to-all(bf16[16,32,1024]{2,1,0:T(8,128)(2,1)} %bitcast.7), channel_id=1, replica_groups=mesh['seq'=16,'head'=8] {'seq'}, dimensions={0} | all-to-all | bytes 2097152 | tf_op jit(solution)/shard_map/all_to_all | solution.py:387
  41.5 0.0 copy-done.2
  41.5 3.0 %scan.1 = bf16[16,32,1024]{2,1,0:T(8,128)(2,1)} custom-call(s32[1]{0:T(128)} %bitcast.me_ref, bf16[16,32,1024]{2,1,0:T(8,128)(2,1)} %all_to_all.30.part_ref, bf16[16,80,128]{2,1,0:T(8,128)(2,1)} %copy-done.2), custom_call_target="tpu_custom_call" | custom-call | flops 1000000000 | bytes 2500000 | tf_op jit(solution)/shard_map/scan/pallas_call | solution.py:458
  44.5 4.3 %all-to-all-start.2 = ((bf16[16,32,1024]{2,1,0:T(8,128)(2,1)}), bf16[16,32,1024]{2,1,0:T(8,128)(2,1)S(1)}, u32[]{:S(2)}, u32[]{:S(2)}) async-start(bf16[16,32,1024]{2,1,0:T(8,128)(2,1)} %scan.1), calls=%async_computation.2 | async-start | bytes 2097152 | tf_op jit(solution)/shard_map/all_to_all | solution.py:387
  48.7 17.6 %branch.1 = (f32[16,64,1024]{2,1,0:T(8,128)}, f32[16,8,1024]{2,1,0:T(8,128)}) custom-call(s32[96]{0:T(128)} %position_ref.7, s32[96]{0:T(128)} %premise_ref.3, s32[1]{0:T(128)} %bitcast.me_ref, bf16[4,1024,1024]{2,1,0:T(8,128)(2,1)} %x_ref.6, bf16[4,1024,128]{2,1,0:T(8,128)(2,1)} %in_ref.6, f32[4,16,1024]{2,1,0:T(8,128)} %decay_ref.8, ...), custom_call_target="tpu_custom_call" | custom-call | flops 10000000000 | bytes 14000000 | tf_op jit(solution)/shard_map/branch/pallas_call | solution.py:441
  66.3 0.0 all-to-all-done.2
  66.3 0.0 copy-start
  66.3 1.0 copy-done
  67.3 5.5 %apply.1 = bf16[16,64,1024]{2,1,0:T(8,128)(2,1)} custom-call(s32[96]{0:T(128)} %position_ref.7, s32[96]{0:T(128)} %premise_ref.3, s32[1]{0:T(128)} %bitcast.me_ref, bf16[4,128,1024]{2,1,0:T(8,128)(2,1)} %bitcast.5, bf16[16,80,128]{2,1,0:T(8,128)(2,1)} %copy-done.2, f32[16,64,1024]{2,1,0:T(8,128)} %get-tuple-element.10.local_ref, ...), custom_call_target="tpu_custom_call" | custom-call | flops 1000000000 | bytes 8000000 | tf_op jit(solution)/shard_map/apply/pallas_call | solution.py:471
  72.8 9.1 %all-to-all-start.4 = ((bf16[16,64,1024]{2,1,0:T(8,128)(2,1)}), bf16[16,64,1024]{2,1,0:T(8,128)(2,1)S(1)}, u32[]{:S(2)}, u32[]{:S(2)}) async-start(bf16[16,64,1024]{2,1,0:T(8,128)(2,1)} %apply.1), calls=%async_computation.4 | async-start | bytes 4194304 | tf_op jit(solution)/shard_map/all_to_all | solution.py:387
  81.9 26.4 %main.1 = (f32[4,1024,1024]{2,1,0:T(8,128)}, f32[8,4,8,128]{3,2,1,0:T(8,128)}) custom-call(bf16[4,1024,1024]{2,1,0:T(8,128)(2,1)} %x_ref.6, bf16[4,1024,128]{2,1,0:T(8,128)(2,1)} %in_ref.6, bf16[4,1024,128]{2,1,0:T(8,128)(2,1)} %read_ref.2, f32[4,16,1024]{2,1,0:T(8,128)} %decay_ref.8, bf16[4,128,1024]{2,1,0:T(8,128)(2,1)} %bitcast.6), custom_call_target="tpu_custom_call" | custom-call | flops 12000000000 | bytes 28000000 | tf_op jit(solution)/shard_map/main/pallas_call | solution.py:491
  108.3 0.0 all-to-all-done.4.arrived_ref
  108.3 0.0 copy-start.1
  108.3 9.0 %all-to-all-start.3 = ((f32[8,4,8,128]{3,2,1,0:T(8,128)}), f32[8,4,8,128]{3,2,1,0:T(8,128)S(1)}, u32[]{:S(2)}, u32[]{:S(2)}) async-start(f32[8,4,8,128]{3,2,1,0:T(8,128)} %get-tuple-element.9), calls=%async_computation.3 | async-start | bytes 262144 | tf_op jit(solution)/shard_map/all_to_all | solution.py:387
  117.3 0.0 copy-done.1
  117.3 5.9 %probes.1 = (f32[1,384,1024]{2,1,0:T(8,128)}, f32[8,1,8,128]{3,2,1,0:T(8,128)}) custom-call(s32[96]{0:T(128)} %position_ref.7, s32[1]{0:T(128)} %bitcast.me_ref, bf16[6,64,1024]{2,1,0:T(8,128)(2,1)} %x_ref.7, bf16[6,64,128]{2,1,0:T(8,128)(2,1)} %in_ref.7, bf16[6,64,128]{2,1,0:T(8,128)(2,1)} %read_ref.3, f32[6,16,64]{2,1,0:T(8,128)} %decay_ref.9, ...), custom_call_target="tpu_custom_call" | custom-call | flops 1000000000 | bytes 5000000 | tf_op jit(solution)/shard_map/probes/pallas_call | solution.py:516
  123.2 0.0 all-to-all-done.3.square_ref
  123.3 0.0 copy-start.3
  123.3 4.8 %all-to-all-start.5 = ((f32[8,1,8,128]{3,2,1,0:T(8,128)}), f32[8,1,8,128]{3,2,1,0:T(8,128)S(1)}, u32[]{:S(2)}, u32[]{:S(2)}) async-start(f32[8,1,8,128]{3,2,1,0:T(8,128)} %get-tuple-element.13), calls=%async_computation.5 | async-start | bytes 65536 | tf_op jit(solution)/shard_map/all_to_all | solution.py:387
  128.1 0.0 copy-done.3
  128.1 9.9 %norm.1 = bf16[4,1024,1024]{2,1,0:T(8,128)(2,1)} custom-call(f32[4,1024,1024]{2,1,0:T(8,128)} %get-tuple-element.8.mixed_ref, f32[8,4,8,128]{3,2,1,0:T(8,128)} %copy-done.3, f32[1,1024]{1,0:T(1,128)} %bitcast.9), custom_call_target="tpu_custom_call" | custom-call | flops 2000000000 | bytes 25000000 | tf_op jit(solution)/shard_map/norm/pallas_call | solution.py:504
  138.0 0.0 all-to-all-done.5.square_ref
  138.0 0.0 copy-start.4
  138.0 0.6 copy-done.4
  138.6 2.7 %probe_norm.1 = bf16[1,384,1024]{2,1,0:T(8,128)(2,1)} custom-call(f32[1,384,1024]{2,1,0:T(8,128)} %get-tuple-element.12.mixed_ref, f32[8,1,8,128]{3,2,1,0:T(8,128)} %copy-done.4, f32[1,1024]{1,0:T(1,128)} %bitcast.10), custom_call_target="tpu_custom_call" | custom-call | flops 100000000 | bytes 2000000 | tf_op jit(solution)/shard_map/probe_norm/pallas_call | solution.py:539
Async XLA Ops:
  2.6 17.6 %all-to-all-start.1 = ((bf16[16,80,128]{2,1,0:T(8,128)(2,1)}), bf16[16,80,128]{2,1,0:T(8,128)(2,1)S(1)}, u32[]{:S(2)}, u32[]{:S(2)}) async-start(bf16[16,80,128]{2,1,0:T(8,128)(2,1)} %route.1), calls=%async_computation.1 | async-start | bytes 655360 | tf_op jit(solution)/shard_map/all_to_all | solution.py:387
  20.2 21.3 %copy-start.2 = (bf16[16,80,128]{2,1,0:T(8,128)(2,1)}, bf16[16,80,128]{2,1,0:T(8,128)(2,1)S(1)}, u32[]{:S(2)}) copy-start(bf16[16,80,128]{2,1,0:T(8,128)(2,1)S(1)} %all-to-all-done.1.routed_ref) | copy-start | bytes 983044
  44.5 21.9 %all-to-all-start.2 = ((bf16[16,32,1024]{2,1,0:T(8,128)(2,1)}), bf16[16,32,1024]{2,1,0:T(8,128)(2,1)S(1)}, u32[]{:S(2)}, u32[]{:S(2)}) async-start(bf16[16,32,1024]{2,1,0:T(8,128)(2,1)} %scan.1), calls=%async_computation.2 | async-start | bytes 2097152 | tf_op jit(solution)/shard_map/all_to_all | solution.py:387
  66.3 1.0 copy-start
  72.8 35.5 %all-to-all-start.4 = ((bf16[16,64,1024]{2,1,0:T(8,128)(2,1)}), bf16[16,64,1024]{2,1,0:T(8,128)(2,1)S(1)}, u32[]{:S(2)}, u32[]{:S(2)}) async-start(bf16[16,64,1024]{2,1,0:T(8,128)(2,1)} %apply.1), calls=%async_computation.4 | async-start | bytes 4194304 | tf_op jit(solution)/shard_map/all_to_all | solution.py:387
  108.3 9.0 %copy-start.1 = (bf16[16,64,1024]{2,1,0:T(8,128)(2,1)}, bf16[16,64,1024]{2,1,0:T(8,128)(2,1)S(1)}, u32[]{:S(2)}) copy-start(bf16[16,64,1024]{2,1,0:T(8,128)(2,1)S(1)} %all-to-all-done.4.arrived_ref) | copy-start | bytes 6291460
  108.3 14.9 %all-to-all-start.3 = ((f32[8,4,8,128]{3,2,1,0:T(8,128)}), f32[8,4,8,128]{3,2,1,0:T(8,128)S(1)}, u32[]{:S(2)}, u32[]{:S(2)}) async-start(f32[8,4,8,128]{3,2,1,0:T(8,128)} %get-tuple-element.9), calls=%async_computation.3 | async-start | bytes 262144 | tf_op jit(solution)/shard_map/all_to_all | solution.py:387
  123.3 4.8 %copy-start.3 = (f32[8,4,8,128]{3,2,1,0:T(8,128)}, f32[8,4,8,128]{3,2,1,0:T(8,128)S(1)}, u32[]{:S(2)}) copy-start(f32[8,4,8,128]{3,2,1,0:T(8,128)S(1)} %all-to-all-done.3.square_ref) | copy-start | bytes 393220
  123.3 14.8 %all-to-all-start.5 = ((f32[8,1,8,128]{3,2,1,0:T(8,128)}), f32[8,1,8,128]{3,2,1,0:T(8,128)S(1)}, u32[]{:S(2)}, u32[]{:S(2)}) async-start(f32[8,1,8,128]{3,2,1,0:T(8,128)} %get-tuple-element.13), calls=%async_computation.5 | async-start | bytes 65536 | tf_op jit(solution)/shard_map/all_to_all | solution.py:387
  138.0 0.6 copy-start.4

commit v2 on v1

v2 whole, which is shorter than its diff:
```python
import functools

import jax
import jax.numpy as jnp
from jax import lax
from jax.experimental import pallas as pl
from jax.experimental.pallas import tpu as pltpu
from jax.sharding import PartitionSpec as P

F32 = jnp.float32
BF16 = jnp.bfloat16
DSTATE = 128
DIN = 8192
EPSILON = 1e-05
BLOCK = 128
EXTRA = 16


def dot(left, right, left_dim, right_dim, precision=None):
    return lax.dot_general(
        left,
        right,
        (((left_dim,), (right_dim,)), ((), ())),
        precision=precision,
        preferred_element_type=F32,
    )


def pieces(value, count):
    parts = []
    for _ in range(count):
        part = value.astype(BF16)
        parts.append(part)
        value = value - part.astype(F32)
    return parts


def spread(heads, width):
    shape = (heads, width)
    head = lax.broadcasted_iota(jnp.int32, shape, 0)
    channel = lax.broadcasted_iota(jnp.int32, shape, 1)
    per_head = width // heads
    return jnp.where(lax.div(channel, jnp.int32(per_head)) == head, 1.0, 0.0).astype(F32)


def spread_twice(one):
    half = one.astype(BF16)
    return jnp.concatenate([half, half], axis=0)


def widen(value, twice):
    return dot(jnp.concatenate(pieces(value, 2), axis=0), twice, 0, 0)


def widen_column(column, one):
    return jnp.sum(column * one, axis=0, keepdims=True)


def prefix(decay, length):
    heads = decay.shape[0]
    count = decay.shape[1] // length
    parts = pieces(decay, 3)
    rows = [part[:, k * length : (k + 1) * length] for k in range(count) for part in parts]
    shape = (length, length)
    upto = (
        lax.broadcasted_iota(jnp.int32, shape, 0) <= lax.broadcasted_iota(jnp.int32, shape, 1)
    )
    total = dot(jnp.concatenate(rows, axis=0), jnp.where(upto, 1.0, 0.0).astype(BF16), 1, 0)
    out = []
    for k in range(count):
        base = 3 * heads * k
        out.append(
            total[base : base + heads]
            + total[base + heads : base + 2 * heads]
            + total[base + 2 * heads : base + 3 * heads]
        )
    return out


def causal(queries, keys):
    shape = (queries, keys)
    return lax.broadcasted_iota(jnp.int32, shape, 0) >= lax.broadcasted_iota(jnp.int32, shape, 1)


def route_kernel(
    position_ref, premise_ref, me_ref, reads_ref, decay_ref, out_ref, table_ref, *, seq_dev
):
    slots = out_ref.shape[0]
    probe_dev, probe_len, _ = reads_ref.shape
    rows, heads, length = decay_ref.shape
    decay = decay_ref[...].reshape(rows * heads, length)
    ones = jnp.ones((EXTRA, length), BF16)
    fill = jnp.zeros((DSTATE - rows * heads, length), BF16)
    total = 0.0
    for part in pieces(decay, 3):
        total = total + dot(ones, jnp.concatenate([part, fill], axis=0), 1, 1)
    row = lax.broadcasted_iota(jnp.int32, (EXTRA, DSTATE), 0)
    block = jnp.zeros((EXTRA, DSTATE), F32)
    for index, part in enumerate(pieces(total, 3)):
        block = jnp.where(row == index, part.astype(F32), block)
    block = block.astype(BF16)
    nothing = jnp.zeros((probe_len, DSTATE), BF16)
    for slot in range(slots):
        out_ref[slot, 0:probe_len, :] = nothing
        out_ref[slot, probe_len : probe_len + EXTRA, :] = block
    for probe in range(probe_dev):
        owner = lax.div(position_ref[me_ref[0] * probe_dev + probe], jnp.int32(seq_dev))
        out_ref[owner, 0:probe_len, :] = reads_ref[probe]
    me = me_ref[0]
    for slot in range(slots):
        offset = jnp.int32(0)
        premise = jnp.int32(0)
        present = jnp.int32(0)
        for probe in range(probe_dev):
            position = position_ref[slot * probe_dev + probe]
            here = lax.div(position, jnp.int32(seq_dev)) == me
            offset = jnp.where(here, position - me * seq_dev, offset)
            premise = jnp.where(here, premise_ref[slot * probe_dev + probe], premise)
            present = jnp.where(here, jnp.int32(1), present)
        block = lax.div(offset, jnp.int32(BLOCK))
        table_ref[4 * slot] = present
        table_ref[4 * slot + 1] = premise
        table_ref[4 * slot + 2] = block
        table_ref[4 * slot + 3] = offset - block * BLOCK


def end_kernel(x_ref, in_ref, decay_ref, out_ref, scaled_ref):
    _, length, width = x_ref.shape
    heads = decay_ref.shape[1]
    twice = spread_twice(spread(heads, width))
    sums = prefix(decay_ref[0], BLOCK)
    after = jnp.zeros((heads, 1), F32)
    for k in reversed(range(length // BLOCK)):
        rows = slice(k * BLOCK, (k + 1) * BLOCK)
        last = sums[k][:, BLOCK - 1 : BLOCK]
        factor = widen(jnp.exp((last - sums[k]) + after), twice)
        scaled_ref[rows, :] = (x_ref[0, rows, :].astype(F32) * factor).astype(BF16)
        after = after + last
    out_ref[0] = dot(in_ref[0], scaled_ref[...], 0, 0).astype(BF16)


def chain_factors(sums, one):
    middle = BLOCK // 2 - 1
    factors = []
    tail = None
    for k in range(len(sums)):
        mid = sums[k][:, middle : middle + 1]
        step = mid if tail is None else tail + mid
        factors.append(widen_column(jnp.exp(step), one))
        tail = sums[k][:, BLOCK - 1 : BLOCK] - mid
    return factors


def build_kernel(x_ref, in_ref, decay_ref, out_ref, done_ref):
    _, length, width = x_ref.shape
    heads = decay_ref.shape[1]
    middle = BLOCK // 2 - 1
    one = spread(heads, width)
    twice = spread_twice(one)
    sums = prefix(decay_ref[0], BLOCK)
    factors = chain_factors(sums, one)
    count = length // BLOCK
    done_ref[...] = jnp.zeros_like(done_ref)
    for k in range(count):
        rows = slice(k * BLOCK, (k + 1) * BLOCK)
        near = sums[k] - sums[k][:, middle : middle + 1]
        factor = widen(jnp.exp(-near), twice)
        out_ref[0, k, 0:BLOCK, :] = (x_ref[0, rows, :].astype(F32) * factor).astype(BF16)
    out_ref[0, 0, BLOCK : BLOCK + DSTATE, :] = jnp.zeros((DSTATE, width), BF16)
    written = [
        dot(in_ref[0, k * BLOCK : (k + 1) * BLOCK, :], out_ref[0, k, 0:BLOCK, :], 0, 0)
        for k in range(count - 1)
    ]
    state = written[0]
    for k in range(1, count):
        state = state * factors[k]
        out_ref[0, k, BLOCK : BLOCK + DSTATE, :] = state.astype(BF16)
        if k < count - 1:
            state = state + written[k]


def branch_kernel(table_ref, right_ref, in_ref, decay_ref, routed_ref, out_ref, scale_ref):
    _, probe_len, width = out_ref.shape
    _, heads, length = decay_ref.shape
    slot = pl.program_id(0)
    present = table_ref[4 * slot] == 1

    @pl.when(present)
    def _():
        k = table_ref[4 * slot + 2]
        within = table_ref[4 * slot + 3]
        reads = routed_ref[0, 0:probe_len, :]
        keep = lax.broadcasted_iota(jnp.int32, (probe_len, BLOCK), 1) <= within
        gram = jnp.where(keep, dot(reads, in_ref[0], 1, 1), 0.0).astype(BF16)
        product = dot(jnp.concatenate([gram, reads], axis=1), right_ref[0, 0], 1, 0)
        one = spread(heads, width)
        lane = lax.broadcasted_iota(jnp.int32, (heads, length), 1)
        offset = k * BLOCK + within
        middle = k * BLOCK + BLOCK // 2 - 1
        decay = decay_ref[0]
        far = jnp.sum(jnp.where(lane <= offset, decay, 0.0), axis=1, keepdims=True)
        later = jnp.where((lane > middle) & (lane <= offset), decay, 0.0)
        earlier = jnp.where((lane > offset) & (lane <= middle), decay, 0.0)
        near = jnp.sum(later - earlier, axis=1, keepdims=True)
        out_ref[0] = product * widen_column(jnp.exp(near), one)
        scale_ref[0] = jnp.broadcast_to(widen_column(jnp.exp(far), one), (8, width))

    @pl.when(jnp.logical_not(present))
    def _():
        out_ref[...] = jnp.zeros_like(out_ref)
        scale_ref[...] = jnp.zeros_like(scale_ref)


def scan_kernel(me_ref, part_ref, routed_ref, after_ref, out_ref, *, probe_len, heads):
    count, height, width = part_ref.shape
    premise = lax.div(me_ref[0] * height, jnp.int32(DSTATE))
    shape = (DSTATE, width)
    lane = lax.broadcasted_iota(jnp.int32, shape, 0) - premise * heads
    channel = lax.broadcasted_iota(jnp.int32, shape, 1)
    pick = jnp.where(lax.div(channel, jnp.int32(width // heads)) == lane, 1.0, 0.0).astype(BF16)
    state = jnp.zeros((height, width), F32)
    for k in range(count):
        out_ref[k] = state.astype(BF16)
        total = dot(routed_ref[k, probe_len : probe_len + EXTRA, :], pick, 1, 0)
        total = jnp.sum(total[0:8], axis=0, keepdims=True)
        state = state * jnp.exp(total) + part_ref[k].astype(F32)


def apply_kernel(
    table_ref, incoming_ref, routed_ref, local_ref, scale_ref, after_ref, out_ref, done_ref
):
    done_ref[...] = jnp.zeros_like(done_ref)
    slots, probe_len, _ = out_ref.shape
    for slot in range(slots):
        premise = table_ref[4 * slot + 1]
        product = dot(routed_ref[slot, 0:probe_len, :], incoming_ref[premise], 1, 0)
        out_ref[slot] = (product * scale_ref[slot, 0:1, :] + local_ref[slot]).astype(BF16)


def squares(mixed):
    total = mixed[:, 0:128] * mixed[:, 0:128]
    for k in range(1, mixed.shape[1] // 128):
        part = mixed[:, 128 * k : 128 * (k + 1)]
        total = total + part * part
    ones = jnp.ones((8, 128), BF16)
    high, low = pieces(total, 2)
    return dot(ones, high, 1, 1) + dot(ones, low, 1, 1)


def main_kernel(
    in_ref, read_ref, decay_ref, incoming_ref, right_ref, after_ref, out_ref, square_ref
):
    _, length, width = out_ref.shape
    heads = decay_ref.shape[1]
    middle = BLOCK // 2 - 1
    count = length // BLOCK
    one = spread(heads, width)
    twice = spread_twice(one)
    mask = causal(BLOCK, BLOCK)
    line = lax.broadcasted_iota(jnp.int32, (8, BLOCK), 0)
    before = jnp.zeros((heads, 1), F32)
    sums = prefix(decay_ref[0], BLOCK)
    lefts, reaches = [], []
    for k in range(count):
        rows = slice(k * BLOCK, (k + 1) * BLOCK)
        reads = read_ref[0, rows, :]
        gram = jnp.where(mask, dot(reads, in_ref[0, rows, :], 1, 1), 0.0).astype(BF16)
        lefts.append(jnp.concatenate([gram, reads], axis=1))
        mid = sums[k][:, middle : middle + 1]
        reaches.append(widen_column(jnp.exp(before + mid), one))
        before = before + sums[k][:, BLOCK - 1 : BLOCK]
    total = jnp.zeros((8, BLOCK), F32)
    for k in range(count):
        rows = slice(k * BLOCK, (k + 1) * BLOCK)
        product = dot(lefts[k], right_ref[0, k], 1, 0)
        product = product + reaches[k] * dot(read_ref[0, rows, :], incoming_ref[0], 1, 0)
        near = sums[k] - sums[k][:, middle : middle + 1]
        mixed = product * widen(jnp.exp(near), twice)
        out_ref[0, rows, :] = mixed
        total = jnp.where(line == k, squares(mixed), total)
    square_ref[0] = total


def probe_kernel(x_ref, in_ref, read_ref, decay_ref, out_ref, factor_ref, done_ref):
    done_ref[...] = jnp.zeros_like(done_ref)
    probe_dev, length, width = x_ref.shape
    heads = decay_ref.shape[1]
    twice = spread_twice(spread(heads, width))
    mask = causal(length, length)
    for probe in range(probe_dev):
        sums = prefix(decay_ref[probe], length)[0]
        inputs = in_ref[probe]
        scaled = (x_ref[probe].astype(F32) * widen(jnp.exp(-sums), twice)).astype(BF16)
        gram = jnp.where(mask, dot(read_ref[probe], inputs, 1, 1), 0.0).astype(BF16)
        factor = widen(jnp.exp(sums), twice)
        out_ref[probe] = dot(gram, scaled, 1, 0) * factor
        factor_ref[probe] = factor


def join_kernel(
    position_ref,
    me_ref,
    inner_ref,
    factor_ref,
    arrived_ref,
    main_square_ref,
    out_ref,
    square_ref,
    *,
    seq_dev,
):
    probe_dev, length, width = inner_ref.shape
    line = lax.broadcasted_iota(jnp.int32, (8, 128), 0)
    total = jnp.zeros((8, 128), F32)
    pair = 128 // length
    for k in range(probe_dev // pair):
        parts = []
        for probe in range(k * pair, (k + 1) * pair):
            owner = lax.div(position_ref[me_ref[0] * probe_dev + probe], jnp.int32(seq_dev))
            parts.append(inner_ref[probe] + factor_ref[probe] * arrived_ref[owner].astype(F32))
        mixed = jnp.concatenate(parts, axis=0)
        out_ref[128 * k : 128 * (k + 1), :] = mixed
        total = jnp.where(line == k, squares(mixed), total)
    rows = main_square_ref.shape[0]
    for copy in range(square_ref.shape[0]):
        square_ref[copy, 0:rows] = main_square_ref[...]
        square_ref[copy, rows] = total


def norm_kernel(mixed_ref, square_ref, gain_ref, probe_ref, out_ref, probe_out_ref):
    _, length, width = mixed_ref.shape
    row = pl.program_id(0)
    gain = gain_ref[...]

    def rates(index):
        total = square_ref[0, index]
        for copy in range(1, square_ref.shape[0]):
            total = total + square_ref[copy, index]
        return lax.rsqrt(total / DIN + EPSILON)

    rate = rates(row)
    count = length // 128
    if count < 8:
        later = jnp.concatenate([rate[count:], rate[:count]], axis=0)
        rate = jnp.where(pl.program_id(1) == 0, rate, later)
    rate = rate.T
    for k in range(count):
        rows = slice(128 * k, 128 * (k + 1))
        out_ref[0, rows, :] = (mixed_ref[0, rows, :] * rate[:, k : k + 1] * gain).astype(BF16)

    @pl.when((row == 0) & (pl.program_id(1) == 0))
    def _():
        probe_rate = rates(square_ref.shape[1] - 1).T
        for k in range(probe_ref.shape[0] // 128):
            rows = slice(128 * k, 128 * (k + 1))
            probe_out_ref[rows, :] = (
                probe_ref[rows, :] * probe_rate[:, k : k + 1] * gain
            ).astype(BF16)


SMEM = pl.BlockSpec(memory_space=pltpu.SMEM)
VMEM = pl.BlockSpec(memory_space=pltpu.VMEM)


def along(shape, *dims):
    return pl.BlockSpec(
        shape, lambda *at: tuple(at[dims.index(d)] if d in dims else 0 for d in range(len(shape)))
    )


def call(kernel, name, in_specs, out_specs, out_shape, grid=None, scratch=(), limit=58, flops=0, moved=0):
    extra = {} if grid is None else {"grid": grid}
    return pl.pallas_call(
        kernel,
        name=name,
        in_specs=in_specs,
        out_specs=out_specs,
        out_shape=out_shape,
        scratch_shapes=list(scratch),
        compiler_params=pltpu.CompilerParams(vmem_limit_bytes=limit * 1024 * 1024),
        cost_estimate=pl.CostEstimate(flops=flops, bytes_accessed=moved, transcendentals=0),
        **extra,
    )


def shaped(shape, dtype):
    return jax.ShapeDtypeStruct(shape, dtype)


def exchange(value, axis):
    return lax.all_to_all(value, axis, split_axis=0, concat_axis=0, tiled=True)


def local(
    tokens,
    state_inputs,
    state_reads,
    log_decay,
    norm_gain,
    probe_tokens,
    probe_inputs,
    probe_reads,
    probe_decay,
    branch_premise,
    branch_position,
):
    seq = lax.axis_size("seq")
    ring = lax.axis_size("head")
    me = lax.axis_index("seq").astype(jnp.int32).reshape(1)
    row_count, seq_dev, width = tokens.shape
    heads = log_decay.shape[1]
    probe_dev, probe_len, _ = probe_tokens.shape
    height = row_count * DSTATE // seq
    routed_shape = (seq, probe_len + EXTRA, DSTATE)
    count = seq_dev // BLOCK
    depth = BLOCK + DSTATE

    routed, table = call(
        functools.partial(route_kernel, seq_dev=seq_dev),
        "route",
        [SMEM, SMEM, SMEM, along(probe_reads.shape), along(log_decay.shape)],
        [along(routed_shape), SMEM],
        [shaped(routed_shape, BF16), shaped((4 * seq,), jnp.int32)],
        (1,),
        moved=800_000,
    )(branch_position, branch_premise, me, probe_reads, log_decay)
    routed = exchange(routed, "seq")

    x_spec = along((1, seq_dev, width), 0)
    in_spec = along((1, seq_dev, DSTATE), 0)
    decay_spec = along((1, heads, seq_dev), 0)
    ends = call(
        end_kernel,
        "ends",
        [x_spec, in_spec, decay_spec],
        along((1, DSTATE, width), 0),
        shaped((row_count, DSTATE, width), BF16),
        (row_count,),
        [pltpu.VMEM((seq_dev, width), BF16)],
        flops=4_000_000_000,
        moved=20_000_000,
    )(tokens, state_inputs, log_decay)
    parts = exchange(ends.reshape(seq, height, width), "seq")

    token = shaped((8, 128), F32)
    token_spec = pl.BlockSpec((8, 128), lambda *at: (0, 0))
    right, built = call(
        build_kernel,
        "build",
        [x_spec, in_spec, decay_spec],
        [along((1, count, depth, width), 0), token_spec],
        [shaped((row_count, count, depth, width), BF16), token],
        (row_count,),
        flops=5_000_000_000,
        moved=40_000_000,
    )(tokens, state_inputs, log_decay)

    starts = call(
        functools.partial(scan_kernel, probe_len=probe_len, heads=heads),
        "scan",
        [SMEM, VMEM, VMEM, VMEM],
        VMEM,
        shaped((seq, height, width), BF16),
        limit=16,
        flops=1_000_000_000,
        moved=2_500_000,
    )(me, parts, routed, built)
    incoming = exchange(starts, "seq").reshape(row_count, DSTATE, width)

    local_part, scale = pl.pallas_call(
        branch_kernel,
        name="branch",
        grid_spec=pltpu.PrefetchScalarGridSpec(
            num_scalar_prefetch=1,
            grid=(seq,),
            in_specs=[
                pl.BlockSpec(
                    (1, 1, depth, width), lambda i, t: (t[4 * i + 1], t[4 * i + 2], 0, 0)
                ),
                pl.BlockSpec((1, BLOCK, DSTATE), lambda i, t: (t[4 * i + 1], t[4 * i + 2], 0)),
                pl.BlockSpec((1, heads, seq_dev), lambda i, t: (t[4 * i + 1], 0, 0)),
                pl.BlockSpec((1,) + routed_shape[1:], lambda i, t: (i, 0, 0)),
            ],
            out_specs=[
                pl.BlockSpec((1, probe_len, width), lambda i, t: (i, 0, 0)),
                pl.BlockSpec((1, 8, width), lambda i, t: (i, 0, 0)),
            ],
        ),
        out_shape=[shaped((seq, probe_len, width), F32), shaped((seq, 8, width), F32)],
        compiler_params=pltpu.CompilerParams(vmem_limit_bytes=48 * 1024 * 1024),
        cost_estimate=pl.CostEstimate(
            flops=1_000_000_000, bytes_accessed=20_000_000, transcendentals=0
        ),
    )(table, right, state_inputs, log_decay, routed)
    inner, factor, probed = call(
        probe_kernel,
        "probes",
        [VMEM] * 4,
        [VMEM] * 3,
        [shaped(probe_tokens.shape, F32)] * 2 + [token],
        limit=40,
        flops=1_000_000_000,
        moved=8_000_000,
    )(probe_tokens, probe_inputs, probe_reads, probe_decay)

    answers, applied = call(
        apply_kernel,
        "apply",
        [SMEM, VMEM, VMEM, VMEM, VMEM, VMEM],
        [VMEM, VMEM],
        [shaped((seq, probe_len, width), BF16), token],
        limit=40,
        flops=1_000_000_000,
        moved=8_000_000,
    )(table, incoming, routed, local_part, scale, probed)
    arrived = exchange(answers, "seq")

    mixed, square = call(
        main_kernel,
        "main",
        [
            in_spec,
            in_spec,
            decay_spec,
            along((1, DSTATE, width), 0),
            along((1, count, depth, width), 0),
            token_spec,
        ],
        [x_spec, along((1, 8, 128), 0)],
        [shaped(tokens.shape, F32), shaped((row_count, 8, 128), F32)],
        (row_count,),
        limit=40,
        flops=12_000_000_000,
        moved=60_000_000,
    )(state_inputs, state_reads, log_decay, incoming, right, applied)

    probe_rows = (probe_dev * probe_len, width)
    square_shape = (ring, row_count + 1, 8, 128)
    probe_mixed, square = call(
        functools.partial(join_kernel, seq_dev=seq_dev),
        "join",
        [SMEM, SMEM, VMEM, VMEM, VMEM, VMEM],
        [VMEM, VMEM],
        [shaped(probe_rows, F32), shaped(square_shape, F32)],
        limit=40,
        flops=1_000_000,
        moved=5_000_000,
    )(branch_position, me, inner, factor, arrived, square)
    square = exchange(square, "head")

    half_spec = along((1, seq_dev // 2, width), 0, 1)
    premise_out, probe_out = call(
        norm_kernel,
        "norm",
        [
            half_spec,
            along(square_shape),
            along((1, width)),
            along(probe_rows),
        ],
        [half_spec, along(probe_rows)],
        [shaped(tokens.shape, BF16), shaped(probe_rows, BF16)],
        (row_count, 2),
        limit=48,
        flops=1_000_000_000,
        moved=30_000_000,
    )(mixed, square, norm_gain.reshape(1, width), probe_mixed)
    return (premise_out, probe_out.reshape(probe_dev, probe_len, width))


def solution(mesh):
    return jax.shard_map(
        local,
        mesh=mesh,
        in_specs=(
            P(None, "seq", "head"),
            P(None, "seq", "head"),
            P(None, "seq", "head"),
            P(None, "head", "seq"),
            P("head"),
            P("seq", None, "head"),
            P("seq", None, "head"),
            P("seq", None, "head"),
            P("seq", "head", None),
            P(),
            P(),
        ),
        out_specs=(P(None, "seq", "head"), P("seq", None, "head")),
        check_vma=False,
    )
```

time: 143 us -> 137 us (0.958)
  Pallas kernels: 82 us -> 70 us
  local copies, waits for them, and re-layouts: 1.57 us -> 12.9 us
  waiting for transfers between devices: 0.01 us -> 7.85 us
  starting transfers between devices: 35.8 us -> 29.6 us
  blocking collectives: 21.3 us -> 15.6 us
    pallas_call x9 -> x10, Pallas kernels: 82 us -> 70 us  [the longest x1 18 us: local(): call(main_kernel, 'main', [in_spec, in_spec, decay_spec, along((1, DSTATE...]
    unnamed x10 -> x38, local copies, waits for them, and re-layouts: 1.57 us -> 12.9 us
    all_to_all x5 -> x4, waiting for transfers between devices: 0.01 us -> 7.85 us  [exchange(): return lax.all_to_all(value, axis, split_axis=0, concat_axis=0, tiled=True)]
    all_to_all x5 -> x4, starting transfers between devices: 35.8 us -> 29.6 us  [exchange(): return lax.all_to_all(value, axis, split_axis=0, concat_axis=0, tiled=True)]
    all_to_all x1, blocking collectives: 21.3 us -> 15.6 us  [exchange(): return lax.all_to_all(value, axis, split_axis=0, concat_axis=0, tiled=True)]
  transfers between devices with their start and end apart: 5 -> 4, of which waited for: 0 -> 2; matrix products, arithmetic and copies ran while one was open for 0% -> 0% of each run, Pallas kernels for 49% -> 38%
where the time goes in v2:
time: 137 us
  Pallas kernels  70 us (51%)
  starting transfers between devices  29.6 us (22%)
  blocking collectives  15.6 us (11%)
  local copies, waits for them, and re-layouts  12.9 us (9%)
  waiting for transfers between devices  7.85 us (6%)
    all_to_all x4, starting transfers between devices, exchange(): return lax.all_to_all(value, axis, split_axis=0, concat_axis=0, tiled=True)  29.6 us
    pallas_call x1, Pallas kernels, local(): call(main_kernel, 'main', [in_spec, in_spec, decay_spec, along((1, DSTATE...  18 us
    all_to_all x1, blocking collectives, exchange(): return lax.all_to_all(value, axis, split_axis=0, concat_axis=0, tiled=True)  15.6 us
    unnamed x38, local copies, waits for them, and re-layouts  12.9 us
    pallas_call x1, Pallas kernels, local(): call(norm_kernel, 'norm', [half_spec, along(square_shape), along((1, widt...  12.3 us
    pallas_call x1, Pallas kernels, local(): call(build_kernel, 'build', [x_spec, in_spec, decay_spec], [along((1, cou...  12 us
    pallas_call x1, Pallas kernels, local(): pl.pallas_call(branch_kernel, name='branch', grid_spec=pltpu.PrefetchScal...  10.2 us
    pallas_call x1, Pallas kernels, local(): call(end_kernel, 'ends', [x_spec, in_spec, decay_spec], along((1, DSTATE,...  8.98 us
  transfers between devices with their start and end apart: 4, of which 2 were waited for; matrix products, arithmetic and copies ran while one was open for 0% of the time, Pallas kernels for 38%

profile of v2, /device:TPU:1, one launch (start us, length us, event | category | flops | bytes accessed | tf_op | source)
XLA Modules:
  0.0 136.7 jit_solution(8428165739012256444)
XLA Ops:
  0.6 2.1 %route.1 = (bf16[16,80,128]{2,1,0:T(8,128)(2,1)}, s32[64]{0:T(128)}) custom-call(s32[96]{0:T(128)} %position_ref.3, s32[96]{0:T(128)} %premise_ref.1, s32[1]{0:T(128)} %bitcast.me_ref, bf16[6,64,128]{2,1,0:T(8,128)(2,1)} %read_ref.2, f32[4,16,1024]{2,1,0:T(8,128)} %decay_ref.11), custom_call_target="tpu_custom_call" | custom-call | bytes 800000 | tf_op jit(solution)/shard_map/route/pallas_call | solution.py:418
  2.7 8.6 %all-to-all-start.1 = ((bf16[16,80,128]{2,1,0:T(8,128)(2,1)}), bf16[16,80,128]{2,1,0:T(8,128)(2,1)S(1)}, u32[]{:S(2)}, u32[]{:S(2)}) async-start(bf16[16,80,128]{2,1,0:T(8,128)(2,1)} %get-tuple-element.19), calls=%async_computation.1 | async-start | bytes 655360 | tf_op jit(solution)/shard_map/all_to_all | solution.py:391
  11.4 9.0 %ends.1 = bf16[4,128,1024]{2,1,0:T(8,128)(2,1)} custom-call(bf16[4,1024,1024]{2,1,0:T(8,128)(2,1)} %x_ref.4, bf16[4,1024,128]{2,1,0:T(8,128)(2,1)} %in_ref.9, f32[4,16,1024]{2,1,0:T(8,128)} %decay_ref.11), custom_call_target="tpu_custom_call" | custom-call | flops 4000000000 | bytes 20000000 | tf_op jit(solution)/shard_map/ends/pallas_call | solution.py:432
  20.3 0.0 all-to-all-done.1.routed_ref
  20.3 6.7 %all-to-all-start = ((bf16[16,32,1024]{2,1,0:T(8,128)(2,1)}), bf16[16,32,1024]{2,1,0:T(8,128)(2,1)S(1)}, u32[]{:S(2)}, u32[]{:S(2)}) async-start(bf16[16,32,1024]{2,1,0:T(8,128)(2,1)} %bitcast.8), calls=%async_computation | async-start | bytes 2097152 | tf_op jit(solution)/shard_map/all_to_all | solution.py:391
  27.0 12.0 %build.1 = (bf16[4,8,256,1024]{3,2,1,0:T(8,128)(2,1)}, f32[8,128]{1,0:T(8,128)}) custom-call(bf16[4,1024,1024]{2,1,0:T(8,128)(2,1)} %x_ref.4, bf16[4,1024,128]{2,1,0:T(8,128)(2,1)} %in_ref.9, f32[4,16,1024]{2,1,0:T(8,128)} %decay_ref.11), custom_call_target="tpu_custom_call" | custom-call | flops 5000000000 | bytes 40000000 | tf_op jit(solution)/shard_map/build/pallas_call | solution.py:447
  39.0 3.2 %all-to-all-done.part_ref = bf16[16,32,1024]{2,1,0:T(8,128)(2,1)S(1)} async-done(((bf16[16,32,1024]{2,1,0:T(8,128)(2,1)}), bf16[16,32,1024]{2,1,0:T(8,128)(2,1)S(1)}, u32[]{:S(2)}, u32[]{:S(2)}) %all-to-all-start) | async-done | bytes 1048608 | tf_op jit(solution)/shard_map/all_to_all | solution.py:391
  42.2 0.7 copy-done.18
  42.9 1.7 %scan.1 = bf16[16,32,1024]{2,1,0:T(8,128)(2,1)} custom-call(s32[1]{0:T(128)} %bitcast.me_ref, bf16[16,32,1024]{2,1,0:T(8,128)(2,1)S(1)} %all-to-all-done.part_ref, bf16[16,80,128]{2,1,0:T(8,128)(2,1)S(1)} %all-to-all-done.1.routed_ref, f32[8,128]{1,0:T(8,128)S(1)} %copy-done.18), custom_call_target="tpu_custom_call" | custom-call | flops 1000000000 | bytes 2500000 | tf_op jit(solution)/shard_map/scan/pallas_call | solution.py:458
  44.6 4.0 %all-to-all-start.2 = ((bf16[16,32,1024]{2,1,0:T(8,128)(2,1)}), bf16[16,32,1024]{2,1,0:T(8,128)(2,1)S(1)}, u32[]{:S(2)}, u32[]{:S(2)}) async-start(bf16[16,32,1024]{2,1,0:T(8,128)(2,1)} %scan.1), calls=%async_computation.2 | async-start | bytes 2097152 | tf_op jit(solution)/shard_map/all_to_all | solution.py:391
  48.6 0.0 copy-start.15
  48.6 1.1 copy-done.15
  49.7 2.5 %probes.1 = (f32[6,64,1024]{2,1,0:T(8,128)S(1)}, f32[6,64,1024]{2,1,0:T(8,128)S(1)}, f32[8,128]{1,0:T(8,128)S(1)}) custom-call(bf16[6,64,1024]{2,1,0:T(8,128)(2,1)S(1)} %copy-done.15, bf16[6,64,128]{2,1,0:T(8,128)(2,1)S(1)} %copy-done.16, bf16[6,64,128]{2,1,0:T(8,128)(2,1)S(1)} %copy-done.10, f32[6,16,64]{2,1,0:T(8,128)S(1)} %copy-done.17), custom_call_target="tpu_custom_call" | custom-call | flops 1000000000 | bytes 8000000 | tf_op jit(solution)/shard_map/probes/pallas_call | solution.py:495
  52.3 1.1 copy-done.2
  53.4 1.1 copy-done.4
  54.6 10.2 %branch.1 = (f32[16,64,1024]{2,1,0:T(8,128)}, f32[16,8,1024]{2,1,0:T(8,128)S(1)}) custom-call(s32[64]{0:T(128)S(1)} %copy-done.13, bf16[4,8,256,1024]{3,2,1,0:T(8,128)(2,1)} %get-tuple-element.21.right_ref, bf16[4,1024,128]{2,1,0:T(8,128)(2,1)S(1)} %copy-done.8, f32[4,16,1024]{2,1,0:T(8,128)S(1)} %copy-done.6, bf16[16,80,128]{2,1,0:T(8,128)(2,1)S(1)} %all-to-all-done.1.routed_ref), custom_call_target="tpu_custom_call" | custom-call | flops 1000000000 | bytes 20000000 | tf_op jit(solution)/shard_map/branch/pallas_call | solution.py:470
  64.8 0.0 all-to-all-done.2
  64.8 2.2 %copy-done = f32[16,64,1024]{2,1,0:T(8,128)S(1)} copy-done((f32[16,64,1024]{2,1,0:T(8,128)S(1)}, f32[16,64,1024]{2,1,0:T(8,128)}, u32[]{:S(2)}) %copy-start) | copy-done | bytes 4194328
  67.0 1.3 apply.1
  68.2 0.0 copy-start.1
  68.3 1.3 copy-done.1
  69.6 10.4 %all-to-all-start.3 = ((bf16[16,64,1024]{2,1,0:T(8,128)(2,1)}), bf16[16,64,1024]{2,1,0:T(8,128)(2,1)S(1)}, u32[]{:S(2)}, u32[]{:S(2)}) async-start(bf16[16,64,1024]{2,1,0:T(8,128)(2,1)} %copy-done.1), calls=%async_computation.3 | async-start | bytes 4194304 | tf_op jit(solution)/shard_map/all_to_all | solution.py:391
  79.9 0.0 copy-start.9
  80.0 1.2 copy-done.9
  81.2 1.2 copy-done.14
  82.4 18.0 %main.1 = (f32[4,1024,1024]{2,1,0:T(8,128)}, f32[4,8,128]{2,1,0:T(8,128)S(1)}) custom-call(bf16[4,1024,128]{2,1,0:T(8,128)(2,1)S(1)} %copy-done.9, bf16[4,1024,128]{2,1,0:T(8,128)(2,1)S(1)} %copy-done.14, f32[4,16,1024]{2,1,0:T(8,128)S(1)} %copy-done.7, bf16[4,128,1024]{2,1,0:T(8,128)(2,1)S(1)} %bitcast.6, ...), custom_call_target="tpu_custom_call" | custom-call | flops 12000000000 | bytes 60000000 | tf_op jit(solution)/shard_map/main/pallas_call | solution.py:518
  100.4 4.7 %all-to-all-done.3.arrived_ref = bf16[16,64,1024]{2,1,0:T(8,128)(2,1)S(1)} async-done(((bf16[16,64,1024]{2,1,0:T(8,128)(2,1)}), bf16[16,64,1024]{2,1,0:T(8,128)(2,1)S(1)}, u32[]{:S(2)}, u32[]{:S(2)}) %all-to-all-start.3) | async-done | bytes 2097184 | tf_op jit(solution)/shard_map/all_to_all | solution.py:391
  105.1 1.4 %copy-done.3 = f32[6,64,1024]{2,1,0:T(8,128)S(1)} copy-done((f32[6,64,1024]{2,1,0:T(8,128)S(1)}, f32[6,64,1024]{2,1,0:T(8,128)}, u32[]{:S(2)}) %copy-start.3) | copy-done | bytes 1572888
  106.5 1.4 %copy-done.5 = f32[6,64,1024]{2,1,0:T(8,128)S(1)} copy-done((f32[6,64,1024]{2,1,0:T(8,128)S(1)}, f32[6,64,1024]{2,1,0:T(8,128)}, u32[]{:S(2)}) %copy-start.5) | copy-done | bytes 1572888
  107.9 0.9 join.1
  108.8 15.6 %all_to_all.25.square_ref = f32[8,5,8,128]{3,2,1,0:T(8,128)S(1)} all-to-all(f32[8,5,8,128]{3,2,1,0:T(8,128)S(1)} %get-tuple-element.32), channel_id=1, replica_groups=mesh['seq'=16,'head'=8] {'head'}, dimensions={0} | all-to-all | bytes 327680 | tf_op jit(solution)/shard_map/all_to_all | solution.py:391
  124.4 12.3 %norm.1 = (bf16[4,1024,1024]{2,1,0:T(8,128)(2,1)}, bf16[384,1024]{1,0:T(8,128)(2,1)}) custom-call(f32[4,1024,1024]{2,1,0:T(8,128)} %get-tuple-element.27.mixed_ref, f32[8,5,8,128]{3,2,1,0:T(8,128)S(1)} %all_to_all.25.square_ref, f32[1,1024]{1,0:T(1,128)S(1)} %bitcast.7, f32[384,1024]{1,0:T(8,128)S(1)} %get-tuple-element.33.probe_ref), custom_call_target="tpu_custom_call" | custom-call | flops 1000000000 | bytes 30000000 | tf_op jit(solution)/shard_map/norm/pallas_call | solution.py:552
  (25 shorter events, 0.0 us)
Async XLA Ops:
  2.7 17.6 %all-to-all-start.1 = ((bf16[16,80,128]{2,1,0:T(8,128)(2,1)}), bf16[16,80,128]{2,1,0:T(8,128)(2,1)S(1)}, u32[]{:S(2)}, u32[]{:S(2)}) async-start(bf16[16,80,128]{2,1,0:T(8,128)(2,1)} %get-tuple-element.19), calls=%async_computation.1 | async-start | bytes 655360 | tf_op jit(solution)/shard_map/all_to_all | solution.py:391
  20.3 21.9 %all-to-all-start = ((bf16[16,32,1024]{2,1,0:T(8,128)(2,1)}), bf16[16,32,1024]{2,1,0:T(8,128)(2,1)S(1)}, u32[]{:S(2)}, u32[]{:S(2)}) async-start(bf16[16,32,1024]{2,1,0:T(8,128)(2,1)} %bitcast.8), calls=%async_computation | async-start | bytes 2097152 | tf_op jit(solution)/shard_map/all_to_all | solution.py:391
  39.0 9.5 %copy-start.10 = (bf16[6,64,128]{2,1,0:T(8,128)(2,1)S(1)}, bf16[6,64,128]{2,1,0:T(8,128)(2,1)}, u32[]{:S(2)}) copy-start(bf16[6,64,128]{2,1,0:T(8,128)(2,1)} %read_ref.2) | copy-start | bytes 294916
  39.0 9.5 %copy-start.16 = (bf16[6,64,128]{2,1,0:T(8,128)(2,1)S(1)}, bf16[6,64,128]{2,1,0:T(8,128)(2,1)}, u32[]{:S(2)}) copy-start(bf16[6,64,128]{2,1,0:T(8,128)(2,1)} %in_ref.8) | copy-start | bytes 294916
  39.0 9.5 %copy-start.17 = (f32[6,16,64]{2,1,0:T(8,128)S(1)}, f32[6,16,64]{2,1,0:T(8,128)}, u32[]{:S(2)}) copy-start(f32[6,16,64]{2,1,0:T(8,128)} %decay_ref.10) | copy-start | bytes 73732
  42.2 0.7 copy-start.18
  42.9 11.6 %copy-start.6 = (f32[4,16,1024]{2,1,0:T(8,128)S(1)}, f32[4,16,1024]{2,1,0:T(8,128)}, u32[]{:S(2)}) copy-start(f32[4,16,1024]{2,1,0:T(8,128)} %decay_ref.11) | copy-start | bytes 786436
  42.9 11.6 %copy-start.8 = (bf16[4,1024,128]{2,1,0:T(8,128)(2,1)S(1)}, bf16[4,1024,128]{2,1,0:T(8,128)(2,1)}, u32[]{:S(2)}) copy-start(bf16[4,1024,128]{2,1,0:T(8,128)(2,1)} %in_ref.9) | copy-start | bytes 3145732
  42.9 11.6 %copy-start.13 = (s32[64]{0:T(128)S(1)}, s32[64]{0:T(128)}, u32[]{:S(2)}) copy-start(s32[64]{0:T(128)} %get-tuple-element.22.table_ref) | copy-start | bytes 772
  44.6 20.2 %all-to-all-start.2 = ((bf16[16,32,1024]{2,1,0:T(8,128)(2,1)}), bf16[16,32,1024]{2,1,0:T(8,128)(2,1)S(1)}, u32[]{:S(2)}, u32[]{:S(2)}) async-start(bf16[16,32,1024]{2,1,0:T(8,128)(2,1)} %scan.1), calls=%async_computation.2 | async-start | bytes 2097152 | tf_op jit(solution)/shard_map/all_to_all | solution.py:391
  48.6 1.1 copy-start.15
  52.3 1.2 copy-start.2
  53.4 1.1 copy-start.4
  64.8 2.2 %copy-start = (f32[16,64,1024]{2,1,0:T(8,128)S(1)}, f32[16,64,1024]{2,1,0:T(8,128)}, u32[]{:S(2)}) copy-start(f32[16,64,1024]{2,1,0:T(8,128)} %get-tuple-element.23.local_ref) | copy-start | bytes 12582916
  68.2 1.3 copy-start.1
  69.6 10.4 %copy-start.7 = (f32[4,16,1024]{2,1,0:T(8,128)S(1)}, f32[4,16,1024]{2,1,0:T(8,128)}, u32[]{:S(2)}) copy-start(f32[4,16,1024]{2,1,0:T(8,128)} %decay_ref.11) | copy-start | bytes 786436
  69.6 35.5 %all-to-all-start.3 = ((bf16[16,64,1024]{2,1,0:T(8,128)(2,1)}), bf16[16,64,1024]{2,1,0:T(8,128)(2,1)S(1)}, u32[]{:S(2)}, u32[]{:S(2)}) async-start(bf16[16,64,1024]{2,1,0:T(8,128)(2,1)} %copy-done.1), calls=%async_computation.3 | async-start | bytes 4194304 | tf_op jit(solution)/shard_map/all_to_all | solution.py:391
  79.9 1.2 copy-start.9
  81.2 1.2 copy-start.14
  82.4 22.7 %copy-start.12 = (s32[96]{0:T(128)S(1)}, s32[96]{0:T(128)}, u32[]{:S(2)}) copy-start(s32[96]{0:T(128)} %position_ref.3) | copy-start | bytes 1156
  100.4 24.0 %copy-start.11 = (f32[1024]{0:T(1024)S(1)}, f32[1024]{0:T(1024)}, u32[]{:S(2)}) copy-start(f32[1024]{0:T(1024)} %param.15) | copy-start | bytes 12292
  105.1 1.4 %copy-start.3 = (f32[6,64,1024]{2,1,0:T(8,128)S(1)}, f32[6,64,1024]{2,1,0:T(8,128)}, u32[]{:S(2)}) copy-start(f32[6,64,1024]{2,1,0:T(8,128)} %copy-done.2) | copy-start | bytes 4718596
  106.5 1.4 %copy-start.5 = (f32[6,64,1024]{2,1,0:T(8,128)S(1)}, f32[6,64,1024]{2,1,0:T(8,128)}, u32[]{:S(2)}) copy-start(f32[6,64,1024]{2,1,0:T(8,128)} %copy-done.4) | copy-start | bytes 4718596

commit v3 on v2

--- a/solution.py
+++ b/solution.py
@@ -179,39 +179,37 @@
             state = state + written[k]
 
 
-def branch_kernel(table_ref, right_ref, in_ref, decay_ref, routed_ref, out_ref, scale_ref):
+def branch_kernel(table_ref, *refs, step):
+    rights, inputs, decays = (refs[i * step : (i + 1) * step] for i in range(3))
+    routed_ref, out_ref, scale_ref = refs[3 * step :]
     _, probe_len, width = out_ref.shape
-    _, heads, length = decay_ref.shape
-    slot = pl.program_id(0)
-    present = table_ref[4 * slot] == 1
-
-    @pl.when(present)
-    def _():
-        k = table_ref[4 * slot + 2]
-        within = table_ref[4 * slot + 3]
-        reads = routed_ref[0, 0:probe_len, :]
-        keep = lax.broadcasted_iota(jnp.int32, (probe_len, BLOCK), 1) <= within
-        gram = jnp.where(keep, dot(reads, in_ref[0], 1, 1), 0.0).astype(BF16)
-        product = dot(jnp.concatenate([gram, reads], axis=1), right_ref[0, 0], 1, 0)
-        one = spread(heads, width)
-        lane = lax.broadcasted_iota(jnp.int32, (heads, length), 1)
-        offset = k * BLOCK + within
-        middle = k * BLOCK + BLOCK // 2 - 1
-        decay = decay_ref[0]
+    _, heads, length = decays[0].shape
+    one = spread(heads, width)
+    lane = lax.broadcasted_iota(jnp.int32, (heads, length), 1)
+    key = lax.broadcasted_iota(jnp.int32, (probe_len, BLOCK), 1)
+    lefts = []
+    for index in range(step):
+        slot = pl.program_id(0) * step + index
+        reads = routed_ref[index, 0:probe_len, :]
+        keep = key <= table_ref[4 * slot + 3]
+        gram = jnp.where(keep, dot(reads, inputs[index][0], 1, 1), 0.0).astype(BF16)
+        lefts.append(jnp.concatenate([gram, reads], axis=1))
+    for index in range(step):
+        slot = pl.program_id(0) * step + index
+        start = table_ref[4 * slot + 2] * BLOCK
+        offset = start + table_ref[4 * slot + 3]
+        middle = start + BLOCK // 2 - 1
+        decay = decays[index][0]
         far = jnp.sum(jnp.where(lane <= offset, decay, 0.0), axis=1, keepdims=True)
         later = jnp.where((lane > middle) & (lane <= offset), decay, 0.0)
         earlier = jnp.where((lane > offset) & (lane <= middle), decay, 0.0)
         near = jnp.sum(later - earlier, axis=1, keepdims=True)
-        out_ref[0] = product * widen_column(jnp.exp(near), one)
-        scale_ref[0] = jnp.broadcast_to(widen_column(jnp.exp(far), one), (8, width))
-
-    @pl.when(jnp.logical_not(present))
-    def _():
-        out_ref[...] = jnp.zeros_like(out_ref)
-        scale_ref[...] = jnp.zeros_like(scale_ref)
-
-
-def scan_kernel(me_ref, part_ref, routed_ref, after_ref, out_ref, *, probe_len, heads):
+        product = dot(lefts[index], rights[index][0, 0], 1, 0)
+        out_ref[index] = product * widen_column(jnp.exp(near), one)
+        scale_ref[index] = jnp.broadcast_to(widen_column(jnp.exp(far), one), (8, width))
+
+
+def scan_kernel(me_ref, part_ref, routed_ref, built_ref, probed_ref, out_ref, *, probe_len, heads):
     count, height, width = part_ref.shape
     premise = lax.div(me_ref[0] * height, jnp.int32(DSTATE))
     shape = (DSTATE, width)
@@ -226,15 +224,13 @@
         state = state * jnp.exp(total) + part_ref[k].astype(F32)
 
 
-def apply_kernel(
-    table_ref, incoming_ref, routed_ref, local_ref, scale_ref, after_ref, out_ref, done_ref
-):
+def apply_kernel(table_ref, incoming_ref, routed_ref, local_ref, scale_ref, out_ref, done_ref):
+    step, probe_len, _ = out_ref.shape
     done_ref[...] = jnp.zeros_like(done_ref)
-    slots, probe_len, _ = out_ref.shape
-    for slot in range(slots):
-        premise = table_ref[4 * slot + 1]
-        product = dot(routed_ref[slot, 0:probe_len, :], incoming_ref[premise], 1, 0)
-        out_ref[slot] = (product * scale_ref[slot, 0:1, :] + local_ref[slot]).astype(BF16)
+    for index in range(step):
+        premise = table_ref[4 * (pl.program_id(0) * step + index) + 1]
+        product = dot(routed_ref[index, 0:probe_len, :], incoming_ref[premise], 1, 0)
+        out_ref[index] = (product * scale_ref[index, 0:1, :] + local_ref[index]).astype(BF16)
 
 
 def squares(mixed):
@@ -248,7 +244,7 @@
 
 
 def main_kernel(
-    in_ref, read_ref, decay_ref, incoming_ref, right_ref, after_ref, out_ref, square_ref
+    in_ref, read_ref, decay_ref, incoming_ref, right_ref, gain_ref, after_ref, out_ref, square_ref
 ):
     _, length, width = out_ref.shape
     heads = decay_ref.shape[1]
@@ -276,7 +272,7 @@
         product = product + reaches[k] * dot(read_ref[0, rows, :], incoming_ref[0], 1, 0)
         near = sums[k] - sums[k][:, middle : middle + 1]
         mixed = product * widen(jnp.exp(near), twice)
-        out_ref[0, rows, :] = mixed
+        out_ref[0, rows, :] = mixed * gain_ref[...]
         total = jnp.where(line == k, squares(mixed), total)
     square_ref[0] = total
 
@@ -298,68 +294,43 @@
 
 
 def join_kernel(
-    position_ref,
-    me_ref,
-    inner_ref,
-    factor_ref,
-    arrived_ref,
-    main_square_ref,
-    out_ref,
-    square_ref,
-    *,
-    seq_dev,
+    position_ref, me_ref, inner_ref, factor_ref, gain_ref, arrived_ref, out_ref, square_ref, *, seq_dev
 ):
-    probe_dev, length, width = inner_ref.shape
+    pair, length, width = inner_ref.shape
+    row = pl.program_id(0)
+    probe_dev = pair * pl.num_programs(0)
+    parts = []
+    for index in range(pair):
+        probe = row * pair + index
+        owner = lax.div(position_ref[me_ref[0] * probe_dev + probe], jnp.int32(seq_dev))
+        parts.append(inner_ref[index] + factor_ref[index] * arrived_ref[owner].astype(F32))
+    mixed = jnp.concatenate(parts, axis=0)
+    out_ref[...] = mixed * gain_ref[...]
+    total = squares(mixed)
     line = lax.broadcasted_iota(jnp.int32, (8, 128), 0)
-    total = jnp.zeros((8, 128), F32)
-    pair = 128 // length
-    for k in range(probe_dev // pair):
-        parts = []
-        for probe in range(k * pair, (k + 1) * pair):
-            owner = lax.div(position_ref[me_ref[0] * probe_dev + probe], jnp.int32(seq_dev))
-            parts.append(inner_ref[probe] + factor_ref[probe] * arrived_ref[owner].astype(F32))
-        mixed = jnp.concatenate(parts, axis=0)
-        out_ref[128 * k : 128 * (k + 1), :] = mixed
-        total = jnp.where(line == k, squares(mixed), total)
-    rows = main_square_ref.shape[0]
+
+    @pl.when(row == 0)
+    def _():
+        square_ref[...] = jnp.zeros_like(square_ref)
+
     for copy in range(square_ref.shape[0]):
-        square_ref[copy, 0:rows] = main_square_ref[...]
-        square_ref[copy, rows] = total
-
-
-def norm_kernel(mixed_ref, square_ref, gain_ref, probe_ref, out_ref, probe_out_ref):
-    _, length, width = mixed_ref.shape
-    row = pl.program_id(0)
-    gain = gain_ref[...]
-
-    def rates(index):
-        total = square_ref[0, index]
-        for copy in range(1, square_ref.shape[0]):
-            total = total + square_ref[copy, index]
-        return lax.rsqrt(total / DIN + EPSILON)
-
-    rate = rates(row)
-    count = length // 128
-    if count < 8:
-        later = jnp.concatenate([rate[count:], rate[:count]], axis=0)
-        rate = jnp.where(pl.program_id(1) == 0, rate, later)
-    rate = rate.T
-    for k in range(count):
+        square_ref[copy] = jnp.where(line == row, total, square_ref[copy])
+
+
+def norm_kernel(mixed_ref, *refs):
+    out_ref = refs[-1]
+    total = 0.0
+    for ref in refs[:-1]:
+        total = total + jnp.sum(ref[...].reshape(-1, 8, 128), axis=0)
+    rate = lax.rsqrt(total / DIN + EPSILON).T
+    for k in range(mixed_ref.shape[1] // 128):
         rows = slice(128 * k, 128 * (k + 1))
-        out_ref[0, rows, :] = (mixed_ref[0, rows, :] * rate[:, k : k + 1] * gain).astype(BF16)
-
-    @pl.when((row == 0) & (pl.program_id(1) == 0))
-    def _():
-        probe_rate = rates(square_ref.shape[1] - 1).T
-        for k in range(probe_ref.shape[0] // 128):
-            rows = slice(128 * k, 128 * (k + 1))
-            probe_out_ref[rows, :] = (
-                probe_ref[rows, :] * probe_rate[:, k : k + 1] * gain
-            ).astype(BF16)
+        out_ref[0, rows, :] = (mixed_ref[0, rows, :] * rate[:, k : k + 1]).astype(BF16)
 
 
 SMEM = pl.BlockSpec(memory_space=pltpu.SMEM)
 VMEM = pl.BlockSpec(memory_space=pltpu.VMEM)
+ANY = pl.BlockSpec(memory_space=pl.ANY)
 
 
 def along(shape, *dims):
@@ -455,66 +426,90 @@
         moved=40_000_000,
     )(tokens, state_inputs, log_decay)
 
+    probe_rows = probe_dev * probe_len
+    inner, factor, probed = call(
+        probe_kernel,
+        "probes",
+        [along(part.shape) for part in (probe_tokens, probe_inputs, probe_reads, probe_decay)],
+        [along(probe_tokens.shape)] * 2 + [token_spec],
+        [shaped(probe_tokens.shape, F32)] * 2 + [token],
+        (1,),
+        flops=1_000_000_000,
+        moved=8_000_000,
+    )(probe_tokens, probe_inputs, probe_reads, probe_decay)
+
     starts = call(
         functools.partial(scan_kernel, probe_len=probe_len, heads=heads),
         "scan",
-        [SMEM, VMEM, VMEM, VMEM],
-        VMEM,
+        [SMEM, VMEM, along(routed_shape), ANY, ANY],
+        along((seq, height, width)),
         shaped((seq, height, width), BF16),
-        limit=16,
+        (1,),
+        limit=48,
         flops=1_000_000_000,
         moved=2_500_000,
-    )(me, parts, routed, built)
+    )(me, parts, routed, built, probed)
     incoming = exchange(starts, "seq").reshape(row_count, DSTATE, width)
 
+    step = 4
+
+    def picked(shape, index, blocked):
+        def at(i, t):
+            base = 4 * (step * i + index)
+            first = (t[base + 1], t[base + 2]) if blocked else (t[base + 1],)
+            return first + (0,) * (len(shape) - len(first))
+
+        return pl.BlockSpec(shape, at)
+
     local_part, scale = pl.pallas_call(
-        branch_kernel,
+        functools.partial(branch_kernel, step=step),
         name="branch",
         grid_spec=pltpu.PrefetchScalarGridSpec(
             num_scalar_prefetch=1,
-            grid=(seq,),
-            in_specs=[
-                pl.BlockSpec(
-                    (1, 1, depth, width), lambda i, t: (t[4 * i + 1], t[4 * i + 2], 0, 0)
-                ),
-                pl.BlockSpec((1, BLOCK, DSTATE), lambda i, t: (t[4 * i + 1], t[4 * i + 2], 0)),
-                pl.BlockSpec((1, heads, seq_dev), lambda i, t: (t[4 * i + 1], 0, 0)),
-                pl.BlockSpec((1,) + routed_shape[1:], lambda i, t: (i, 0, 0)),
-            ],
-            out_specs=[
-                pl.BlockSpec((1, probe_len, width), lambda i, t: (i, 0, 0)),
-                pl.BlockSpec((1, 8, width), lambda i, t: (i, 0, 0)),
-            ],
+            grid=(seq // step,),
+            in_specs=[picked((1, 1, depth, width), i, True) for i in range(step)]
+            + [picked((1, BLOCK, DSTATE), i, True) for i in range(step)]
+            + [picked((1, heads, seq_dev), i, False) for i in range(step)]
+            + [along((step,) + routed_shape[1:], 0)],
+            out_specs=[along((step, probe_len, width), 0), along((step, 8, width), 0)],
         ),
         out_shape=[shaped((seq, probe_len, width), F32), shaped((seq, 8, width), F32)],
-        compiler_params=pltpu.CompilerParams(vmem_limit_bytes=48 * 1024 * 1024),
+        compiler_params=pltpu.CompilerParams(vmem_limit_bytes=58 * 1024 * 1024),
         cost_estimate=pl.CostEstimate(
             flops=1_000_000_000, bytes_accessed=20_000_000, transcendentals=0
         ),
-    )(table, right, state_inputs, log_decay, routed)
-    inner, factor, probed = call(
-        probe_kernel,
-        "probes",
-        [VMEM] * 4,
-        [VMEM] * 3,
-        [shaped(probe_tokens.shape, F32)] * 2 + [token],
-        limit=40,
-        flops=1_000_000_000,
-        moved=8_000_000,
-    )(probe_tokens, probe_inputs, probe_reads, probe_decay)
+    )(
+        table,
+        *[right] * step,
+        *[state_inputs] * step,
+        *[log_decay] * step,
+        routed,
+    )
 
     answers, applied = call(
         apply_kernel,
         "apply",
-        [SMEM, VMEM, VMEM, VMEM, VMEM, VMEM],
-        [VMEM, VMEM],
+        [SMEM, VMEM]
+        + [
+            along(shape, 0)
+            for shape in (
+                (step,) + routed_shape[1:],
+                (step, probe_len, width),
+                (step, 8, width),
+            )
+        ],
+        [along((step, probe_len, width), 0), token_spec],
         [shaped((seq, probe_len, width), BF16), token],
-        limit=40,
+        (seq // step,),
+        limit=48,
         flops=1_000_000_000,
         moved=8_000_000,
-    )(table, incoming, routed, local_part, scale, probed)
+    )(table, incoming, routed, local_part, scale)
     arrived = exchange(answers, "seq")
 
+    gain = norm_gain.reshape(1, width)
+    square_spec = along((1, 8, 128), 0)
+    square_shape = (row_count, 8, 128)
     mixed, square = call(
         main_kernel,
         "main",
@@ -524,47 +519,63 @@
             decay_spec,
             along((1, DSTATE, width), 0),
             along((1, count, depth, width), 0),
-            token_spec,
+            along((1, width)),
+            ANY,
         ],
-        [x_spec, along((1, 8, 128), 0)],
-        [shaped(tokens.shape, F32), shaped((row_count, 8, 128), F32)],
+        [x_spec, square_spec],
+        [shaped(tokens.shape, F32), shaped(square_shape, F32)],
         (row_count,),
-        limit=40,
         flops=12_000_000_000,
         moved=60_000_000,
-    )(state_inputs, state_reads, log_decay, incoming, right, applied)
-
-    probe_rows = (probe_dev * probe_len, width)
-    square_shape = (ring, row_count + 1, 8, 128)
-    probe_mixed, square = call(
+    )(state_inputs, state_reads, log_decay, incoming, right, gain, applied)
+    shared = [square] + [
+        lax.ppermute(square, "head", [(i, (i + turn) % ring) for i in range(ring)])
+        for turn in range(1, ring)
+    ]
+
+    probe_mixed, probe_square = call(
         functools.partial(join_kernel, seq_dev=seq_dev),
         "join",
-        [SMEM, SMEM, VMEM, VMEM, VMEM, VMEM],
-        [VMEM, VMEM],
-        [shaped(probe_rows, F32), shaped(square_shape, F32)],
-        limit=40,
+        [
+            SMEM,
+            SMEM,
+            along((128 // probe_len, probe_len, width), 0),
+            along((128 // probe_len, probe_len, width), 0),
+            along((1, width)),
+            VMEM,
+        ],
+        [along((128, width), 0), along((ring, 8, 128))],
+        [shaped((probe_rows, width), F32), shaped((ring, 8, 128), F32)],
+        (probe_rows // 128,),
+        limit=48,
         flops=1_000_000,
         moved=5_000_000,
-    )(branch_position, me, inner, factor, arrived, square)
-    square = exchange(square, "head")
-
-    half_spec = along((1, seq_dev // 2, width), 0, 1)
-    premise_out, probe_out = call(
+    )(branch_position, me, inner, factor, gain, arrived)
+    probe_square = exchange(probe_square, "head")
+
+    premise_out = call(
         norm_kernel,
         "norm",
-        [
-            half_spec,
-            along(square_shape),
-            along((1, width)),
-            along(probe_rows),
-        ],
-        [half_spec, along(probe_rows)],
-        [shaped(tokens.shape, BF16), shaped(probe_rows, BF16)],
-        (row_count, 2),
-        limit=48,
+        [x_spec] + [square_spec] * ring,
+        x_spec,
+        shaped(tokens.shape, BF16),
+        (row_count,),
+        limit=50,
         flops=1_000_000_000,
         moved=30_000_000,
-    )(mixed, square, norm_gain.reshape(1, width), probe_mixed)
+    )(mixed, *shared)
+    probe_shape = (1, probe_rows, width)
+    probe_out = call(
+        norm_kernel,
+        "probe_norm",
+        [along(probe_shape), along((ring, 8, 128))],
+        along(probe_shape),
+        shaped(probe_shape, BF16),
+        (1,),
+        limit=54,
+        flops=1_000_000,
+        moved=2_000_000,
+    )(probe_mixed.reshape(probe_shape), probe_square)
     return (premise_out, probe_out.reshape(probe_dev, probe_len, width))
 
 

time: 137 us -> 132 us (0.964)
  blocking collectives: 15.6 us -> 0 us
  starting transfers between devices: 29.6 us -> 43 us
  local copies, waits for them, and re-layouts: 12.9 us -> 4.54 us
  Pallas kernels: 70 us -> 75.7 us
    all_to_all x1 -> x0, blocking collectives: 15.6 us -> none  [exchange(): return lax.all_to_all(value, axis, split_axis=0, concat_axis=0, tiled=True)]
    ppermute x0 -> x7, starting transfers between devices: none -> 11.8 us  [local(): lax.ppermute(square, 'head', [(i, (i + turn) % ring) for i in range(ring)])]
    unnamed x38 -> x30, local copies, waits for them, and re-layouts: 12.9 us -> 4.54 us
    pallas_call x4 -> x5, Pallas kernels: 26.3 us -> 29.3 us  [the longest x1 9.2 us: local(): call(norm_kernel, 'norm', [x_spec] + [square_spec] * ring, x_spec, shaped...]
    pallas_call x1, Pallas kernels: 0.95 us -> 3 us  [local(): call(functools.partial(join_kernel, seq_dev=seq_dev), 'join', [SMEM, SMEM...]
    all_to_all x4 -> x5, starting transfers between devices: 29.6 us -> 31.2 us  [exchange(): return lax.all_to_all(value, axis, split_axis=0, concat_axis=0, tiled=True)]
    all_to_all x4 -> x5, waiting for transfers between devices: 7.85 us -> 7.34 us  [exchange(): return lax.all_to_all(value, axis, split_axis=0, concat_axis=0, tiled=True)]
  transfers between devices with their start and end apart: 4 -> 12, of which waited for: 2 -> 1; matrix products, arithmetic and copies ran while one was open for 0% -> 0% of each run, Pallas kernels for 38% -> 49%
where the time goes in v3:
time: 132 us; the launch traced here: 131 us
  Pallas kernels  75.7 us (57%)
  starting transfers between devices  43 us (33%)
  waiting for transfers between devices  7.36 us (6%)
  local copies, waits for them, and re-layouts  4.54 us (3%)
    all_to_all x5, starting transfers between devices, exchange(): return lax.all_to_all(value, axis, split_axis=0, concat_axis=0, tiled=True)  31.2 us
    pallas_call x1, Pallas kernels, local(): call(main_kernel, 'main', [in_spec, in_spec, decay_spec, along((1, DSTATE...  18.7 us
    pallas_call x1, Pallas kernels, local(): call(build_kernel, 'build', [x_spec, in_spec, decay_spec], [along((1, cou...  12 us
    ppermute x7, starting transfers between devices, local(): lax.ppermute(square, 'head', [(i, (i + turn) % ring) for i in range(ring)])  11.8 us
    pallas_call x1, Pallas kernels, local(): call(norm_kernel, 'norm', [x_spec] + [square_spec] * ring, x_spec, shaped...  9.2 us
    pallas_call x1, Pallas kernels, local(): call(end_kernel, 'ends', [x_spec, in_spec, decay_spec], along((1, DSTATE,...  8.98 us
    pallas_call x1, Pallas kernels, local(): pl.pallas_call(functools.partial(branch_kernel, step=step), name='branch'...  7.5 us
    all_to_all x5, waiting for transfers between devices, exchange(): return lax.all_to_all(value, axis, split_axis=0, concat_axis=0, tiled=True)  7.34 us
  transfers between devices with their start and end apart: 12, of which 1 were waited for; matrix products, arithmetic and copies ran while one was open for 0% of the time, Pallas kernels for 49%

profile of v3, /device:TPU:1, one launch (start us, length us, event | category | flops | bytes accessed | tf_op | source)
XLA Modules:
  0.0 131.4 jit_solution(16350617262678118229)
XLA Ops:
  0.6 2.1 %route.1 = (bf16[16,80,128]{2,1,0:T(8,128)(2,1)}, s32[64]{0:T(128)}) custom-call(s32[96]{0:T(128)} %position_ref.3, s32[96]{0:T(128)} %premise_ref.1, s32[1]{0:T(128)} %bitcast.me_ref, bf16[6,64,128]{2,1,0:T(8,128)(2,1)} %read_ref.2, f32[4,16,1024]{2,1,0:T(8,128)} %decay_ref.9), custom_call_target="tpu_custom_call" | custom-call | bytes 800000 | tf_op jit(solution)/shard_map/route/pallas_call | solution.py:389
  2.7 8.6 %all-to-all-start.1 = ((bf16[16,80,128]{2,1,0:T(8,128)(2,1)}), bf16[16,80,128]{2,1,0:T(8,128)(2,1)S(1)}, u32[]{:S(2)}, u32[]{:S(2)}) async-start(bf16[16,80,128]{2,1,0:T(8,128)(2,1)} %get-tuple-element.17), calls=%async_computation.1 | async-start | bytes 655360 | tf_op jit(solution)/shard_map/all_to_all | solution.py:362
  11.4 9.0 %ends.1 = bf16[4,128,1024]{2,1,0:T(8,128)(2,1)} custom-call(bf16[4,1024,1024]{2,1,0:T(8,128)(2,1)} %x_ref.4, bf16[4,1024,128]{2,1,0:T(8,128)(2,1)} %in_ref.7, f32[4,16,1024]{2,1,0:T(8,128)} %decay_ref.9), custom_call_target="tpu_custom_call" | custom-call | flops 4000000000 | bytes 20000000 | tf_op jit(solution)/shard_map/ends/pallas_call | solution.py:403
  20.3 6.7 %all-to-all-start = ((bf16[16,32,1024]{2,1,0:T(8,128)(2,1)}), bf16[16,32,1024]{2,1,0:T(8,128)(2,1)S(1)}, u32[]{:S(2)}, u32[]{:S(2)}) async-start(bf16[16,32,1024]{2,1,0:T(8,128)(2,1)} %bitcast.11), calls=%async_computation | async-start | bytes 2097152 | tf_op jit(solution)/shard_map/all_to_all | solution.py:362
  27.0 5.2 %probes.1 = (f32[6,64,1024]{2,1,0:T(8,128)}, f32[6,64,1024]{2,1,0:T(8,128)}, f32[8,128]{1,0:T(8,128)}) custom-call(bf16[6,64,1024]{2,1,0:T(8,128)(2,1)} %x_ref.5, bf16[6,64,128]{2,1,0:T(8,128)(2,1)} %in_ref.6, bf16[6,64,128]{2,1,0:T(8,128)(2,1)} %read_ref.2, f32[6,16,64]{2,1,0:T(8,128)} %decay_ref.8), custom_call_target="tpu_custom_call" | custom-call | flops 1000000000 | bytes 8000000 | tf_op jit(solution)/shard_map/probes/pallas_call | solution.py:430
  32.3 12.0 %build.1 = (bf16[4,8,256,1024]{3,2,1,0:T(8,128)(2,1)}, f32[8,128]{1,0:T(8,128)}) custom-call(bf16[4,1024,1024]{2,1,0:T(8,128)(2,1)} %x_ref.4, bf16[4,1024,128]{2,1,0:T(8,128)(2,1)} %in_ref.7, f32[4,16,1024]{2,1,0:T(8,128)} %decay_ref.9), custom_call_target="tpu_custom_call" | custom-call | flops 5000000000 | bytes 40000000 | tf_op jit(solution)/shard_map/build/pallas_call | solution.py:418
  44.3 0.0 copy-start.13
  44.3 0.7 copy-done.13
  45.0 1.6 %scan.1 = bf16[16,32,1024]{2,1,0:T(8,128)(2,1)} custom-call(s32[1]{0:T(128)} %bitcast.me_ref, bf16[16,32,1024]{2,1,0:T(8,128)(2,1)S(1)} %all-to-all-done.part_ref, bf16[16,80,128]{2,1,0:T(8,128)(2,1)S(1)} %all-to-all-done.1.routed_ref.refs_12_, f32[8,128]{1,0:T(8,128)S(1)} %copy-done.13, f32[8,128]{1,0:T(8,128)S(1)} %copy-done.12), custom_call_target="tpu_custom_call" | custom-call | flops 1000000000 | bytes 2500000 | tf_op jit(solution)/shard_map/scan/pallas_call | solution.py:441
  46.6 6.7 %all-to-all-start.2 = ((bf16[16,32,1024]{2,1,0:T(8,128)(2,1)}), bf16[16,32,1024]{2,1,0:T(8,128)(2,1)S(1)}, u32[]{:S(2)}, u32[]{:S(2)}) async-start(bf16[16,32,1024]{2,1,0:T(8,128)(2,1)} %scan.1), calls=%async_computation.2 | async-start | bytes 2097152 | tf_op jit(solution)/shard_map/all_to_all | solution.py:362
  53.3 7.5 %branch.1 = (f32[16,64,1024]{2,1,0:T(8,128)}, f32[16,8,1024]{2,1,0:T(8,128)}) custom-call(s32[64]{0:T(128)} %get-tuple-element.21.table_ref, bf16[4,8,256,1024]{3,2,1,0:T(8,128)(2,1)} %get-tuple-element.20.refs_0_.refs_1_.refs_2_.refs_3_.right_ref, bf16[4,8,256,1024]{3,2,1,0:T(8,128)(2,1)} %get-tuple-element.20.refs_0_.refs_1_.refs_2_.refs_3_.right_ref, ...), custom_call_target="tpu_custom_call" | custom-call | flops 1000000000 | bytes 20000000 | tf_op jit(solution)/shard_map/branch/pallas_call | solution.py:464
  60.8 7.3 %all-to-all-done.2 = bf16[16,32,1024]{2,1,0:T(8,128)(2,1)S(1)} async-done(((bf16[16,32,1024]{2,1,0:T(8,128)(2,1)}), bf16[16,32,1024]{2,1,0:T(8,128)(2,1)S(1)}, u32[]{:S(2)}, u32[]{:S(2)}) %all-to-all-start.2) | async-done | bytes 1048608 | tf_op jit(solution)/shard_map/all_to_all | solution.py:362
  68.2 1.4 %copy-done.6 = f32[16,8,1024]{2,1,0:T(8,128)S(1)} copy-done((f32[16,8,1024]{2,1,0:T(8,128)S(1)}, f32[16,8,1024]{2,1,0:T(8,128)}, u32[]{:S(2)}) %copy-start.6) | copy-done | bytes 524312
  69.6 4.8 %apply.1 = (bf16[16,64,1024]{2,1,0:T(8,128)(2,1)}, f32[8,128]{1,0:T(8,128)S(1)}) custom-call(s32[64]{0:T(128)S(1)} %copy-done.9, bf16[4,128,1024]{2,1,0:T(8,128)(2,1)S(1)} %bitcast.6, bf16[16,80,128]{2,1,0:T(8,128)(2,1)S(1)} %copy-done.2, f32[16,64,1024]{2,1,0:T(8,128)} %get-tuple-element.22.local_ref, f32[16,8,1024]{2,1,0:T(8,128)S(1)} %copy-done.6), custom_call_target="tpu_custom_call" | custom-call | flops 1000000000 | bytes 8000000 | tf_op jit(solution)/shard_map/apply/pallas_call | solution.py:489
  74.3 0.6 copy-done.11
  74.9 4.6 %all-to-all-start.3 = ((bf16[16,64,1024]{2,1,0:T(8,128)(2,1)}), bf16[16,64,1024]{2,1,0:T(8,128)(2,1)}, u32[]{:S(2)}, u32[]{:S(2)}) async-start(bf16[16,64,1024]{2,1,0:T(8,128)(2,1)} %get-tuple-element.29), calls=%async_computation.3 | async-start | bytes 4194304 | tf_op jit(solution)/shard_map/all_to_all | solution.py:362
  79.6 0.0 copy-start.8
  79.6 0.0 copy-start.10
  79.6 18.7 %main.1 = (f32[4,1024,1024]{2,1,0:T(8,128)}, f32[4,8,128]{2,1,0:T(8,128)}) custom-call(bf16[4,1024,128]{2,1,0:T(8,128)(2,1)} %in_ref.7, bf16[4,1024,128]{2,1,0:T(8,128)(2,1)} %read_ref.3, f32[4,16,1024]{2,1,0:T(8,128)} %decay_ref.9, bf16[4,128,1024]{2,1,0:T(8,128)(2,1)} %bitcast.7, ...), custom_call_target="tpu_custom_call" | custom-call | flops 12000000000 | bytes 60000000 | tf_op jit(solution)/shard_map/main/pallas_call | solution.py:513
  98.3 4.1 %collective-permute-start = (f32[4,8,128]{2,1,0:T(8,128)}, f32[4,8,128]{2,1,0:T(8,128)S(1)}, u32[]{:S(2)}, u32[]{:S(2)}) collective-permute-start(f32[4,8,128]{2,1,0:T(8,128)} %get-tuple-element.26.refs_0_), channel_id=1, source_target_pairs={{0,1},{1,2},{2,3},{3,4},{4,5},{5,6},{6,7},{7,0},{8,9},{9,10},{10,1... | collective-permute-start | bytes 49160 | tf_op jit(solution)/shard_map/ppermute | solution.py:532
  102.5 1.2 collective-permute-start.1
  103.7 1.6 %collective-permute-start.2 = (f32[4,8,128]{2,1,0:T(8,128)}, f32[4,8,128]{2,1,0:T(8,128)S(1)}, u32[]{:S(2)}, u32[]{:S(2)}) collective-permute-start(f32[4,8,128]{2,1,0:T(8,128)} %get-tuple-element.26.refs_0_), channel_id=1, source_target_pairs={{0,3},{1,4},{2,5},{3,6},{4,7},{5,0},{6,1},{7,2},{8,11},{9,12},{10,... | collective-permute-start | bytes 49160 | tf_op jit(solution)/shard_map/ppermute | solution.py:532
  105.3 0.5 collective-permute-start.3
  105.8 1.9 %collective-permute-start.4 = (f32[4,8,128]{2,1,0:T(8,128)}, f32[4,8,128]{2,1,0:T(8,128)S(1)}, u32[]{:S(2)}, u32[]{:S(2)}) collective-permute-start(f32[4,8,128]{2,1,0:T(8,128)} %get-tuple-element.26.refs_0_), channel_id=1, source_target_pairs={{0,5},{1,6},{2,7},{3,0},{4,1},{5,2},{6,3},{7,4},{8,13},{9,14},{10,... | collective-permute-start | bytes 49160 | tf_op jit(solution)/shard_map/ppermute | solution.py:532
  107.7 0.7 collective-permute-start.5
  108.4 1.7 %collective-permute-start.6 = (f32[4,8,128]{2,1,0:T(8,128)}, f32[4,8,128]{2,1,0:T(8,128)S(1)}, u32[]{:S(2)}, u32[]{:S(2)}) collective-permute-start(f32[4,8,128]{2,1,0:T(8,128)} %get-tuple-element.26.refs_0_), channel_id=1, source_target_pairs={{0,7},{1,0},{2,1},{3,2},{4,3},{5,4},{6,5},{7,6},{8,15},{9,8},{10,9... | collective-permute-start | bytes 49160 | tf_op jit(solution)/shard_map/ppermute | solution.py:532
  110.1 3.0 %join.1 = (f32[384,1024]{1,0:T(8,128)S(1)}, f32[8,8,128]{2,1,0:T(8,128)}) custom-call(s32[96]{0:T(128)S(1)} %copy-done.10, s32[1]{0:T(128)} %bitcast.me_ref, f32[6,64,1024]{2,1,0:T(8,128)S(1)} %copy-done.4, f32[6,64,1024]{2,1,0:T(8,128)S(1)} %copy-done.5, f32[1,1024]{1,0:T(1,128)S(1)} %bitcast.10, bf16[16,64,1024]{2,1,0:T(8,128)(2,1)} %all-to-all-done.3.arrived_ref), custom_call_target="tpu_custom_call" | custom-call | flops 1000000 | bytes 5000000 | tf_op jit(solution)/shard_map/join/pallas_call | solution.py:536
  113.1 1.2 copy-done.3
  114.3 4.7 %all-to-all-start.4 = ((f32[8,8,128]{2,1,0:T(8,128)}), f32[8,8,128]{2,1,0:T(8,128)S(1)}, u32[]{:S(2)}, u32[]{:S(2)}) async-start(f32[8,8,128]{2,1,0:T(8,128)} %get-tuple-element.31), calls=%async_computation.4 | async-start | bytes 65536 | tf_op jit(solution)/shard_map/all_to_all | solution.py:362
  119.0 9.2 %norm.1 = bf16[4,1024,1024]{2,1,0:T(8,128)(2,1)} custom-call(f32[4,1024,1024]{2,1,0:T(8,128)} %get-tuple-element.25.mixed_ref, f32[4,8,128]{2,1,0:T(8,128)S(1)} %copy-done.7, f32[4,8,128]{2,1,0:T(8,128)S(1)} %collective-permute-done.refs_1_, f32[4,8,128]{2,1,0:T(8,128)S(1)} %collective-permute-done.1.refs_2_, ...), custom_call_target="tpu_custom_call" | custom-call | flops 1000000000 | bytes 30000000 | tf_op jit(solution)/shard_map/norm/pallas_call | solution.py:556
  128.2 0.6 copy-done.14
  128.8 2.5 %probe_norm.1 = bf16[1,384,1024]{2,1,0:T(8,128)(2,1)} custom-call(f32[1,384,1024]{2,1,0:T(8,128)} %bitcast.8, f32[8,8,128]{2,1,0:T(8,128)} %copy-done.14), custom_call_target="tpu_custom_call" | custom-call | flops 1000000 | bytes 2000000 | tf_op jit(solution)/shard_map/probe_norm/pallas_call | solution.py:568
  (33 shorter events, 0.1 us)
Async XLA Ops:
  2.7 17.6 %all-to-all-start.1 = ((bf16[16,80,128]{2,1,0:T(8,128)(2,1)}), bf16[16,80,128]{2,1,0:T(8,128)(2,1)S(1)}, u32[]{:S(2)}, u32[]{:S(2)}) async-start(bf16[16,80,128]{2,1,0:T(8,128)(2,1)} %get-tuple-element.17), calls=%async_computation.1 | async-start | bytes 655360 | tf_op jit(solution)/shard_map/all_to_all | solution.py:362
  20.3 23.9 %copy-start.1 = (bf16[16,80,128]{2,1,0:T(8,128)(2,1)}, bf16[16,80,128]{2,1,0:T(8,128)(2,1)S(1)}, u32[]{:S(2)}) copy-start(bf16[16,80,128]{2,1,0:T(8,128)(2,1)S(1)} %all-to-all-done.1.routed_ref.refs_12_) | copy-start | bytes 983044
  20.3 23.9 %all-to-all-start = ((bf16[16,32,1024]{2,1,0:T(8,128)(2,1)}), bf16[16,32,1024]{2,1,0:T(8,128)(2,1)S(1)}, u32[]{:S(2)}, u32[]{:S(2)}) async-start(bf16[16,32,1024]{2,1,0:T(8,128)(2,1)} %bitcast.11), calls=%async_computation | async-start | bytes 2097152 | tf_op jit(solution)/shard_map/all_to_all | solution.py:362
  32.3 12.0 %copy-start.12 = (f32[8,128]{1,0:T(8,128)S(1)}, f32[8,128]{1,0:T(8,128)}, u32[]{:S(2)}) copy-start(f32[8,128]{1,0:T(8,128)} %get-tuple-element.19.probed_ref) | copy-start | bytes 12292
  44.3 0.7 copy-start.13
  46.6 21.5 %all-to-all-start.2 = ((bf16[16,32,1024]{2,1,0:T(8,128)(2,1)}), bf16[16,32,1024]{2,1,0:T(8,128)(2,1)S(1)}, u32[]{:S(2)}, u32[]{:S(2)}) async-start(bf16[16,32,1024]{2,1,0:T(8,128)(2,1)} %scan.1), calls=%async_computation.2 | async-start | bytes 2097152 | tf_op jit(solution)/shard_map/all_to_all | solution.py:362
  53.3 14.9 %copy-start.2 = (bf16[16,80,128]{2,1,0:T(8,128)(2,1)S(1)}, bf16[16,80,128]{2,1,0:T(8,128)(2,1)}, u32[]{:S(2)}) copy-start(bf16[16,80,128]{2,1,0:T(8,128)(2,1)} %copy-done.1) | copy-start | bytes 983044
  53.3 14.9 %copy-start.9 = (s32[64]{0:T(128)S(1)}, s32[64]{0:T(128)}, u32[]{:S(2)}) copy-start(s32[64]{0:T(128)} %get-tuple-element.21.table_ref) | copy-start | bytes 772
  68.1 6.8 %copy-start = (bf16[16,32,1024]{2,1,0:T(8,128)(2,1)}, bf16[16,32,1024]{2,1,0:T(8,128)(2,1)S(1)}, u32[]{:S(2)}) copy-start(bf16[16,32,1024]{2,1,0:T(8,128)(2,1)S(1)} %all-to-all-done.2) | copy-start | bytes 3145732
  68.2 1.4 %copy-start.6 = (f32[16,8,1024]{2,1,0:T(8,128)S(1)}, f32[16,8,1024]{2,1,0:T(8,128)}, u32[]{:S(2)}) copy-start(f32[16,8,1024]{2,1,0:T(8,128)} %get-tuple-element.23.scale_ref) | copy-start | bytes 1572868
  74.3 0.6 copy-start.11
  74.9 35.1 %all-to-all-start.3 = ((bf16[16,64,1024]{2,1,0:T(8,128)(2,1)}), bf16[16,64,1024]{2,1,0:T(8,128)(2,1)}, u32[]{:S(2)}, u32[]{:S(2)}) async-start(bf16[16,64,1024]{2,1,0:T(8,128)(2,1)} %get-tuple-element.29), calls=%async_computation.3 | async-start | bytes 4194304 | tf_op jit(solution)/shard_map/all_to_all | solution.py:362
  79.6 30.5 %copy-start.4 = (f32[6,64,1024]{2,1,0:T(8,128)S(1)}, f32[6,64,1024]{2,1,0:T(8,128)}, u32[]{:S(2)}) copy-start(f32[6,64,1024]{2,1,0:T(8,128)} %get-tuple-element.27.inner_ref) | copy-start | bytes 4718596
  79.6 30.5 %copy-start.5 = (f32[6,64,1024]{2,1,0:T(8,128)S(1)}, f32[6,64,1024]{2,1,0:T(8,128)}, u32[]{:S(2)}) copy-start(f32[6,64,1024]{2,1,0:T(8,128)} %get-tuple-element.28.factor_ref) | copy-start | bytes 4718596
  79.6 30.5 %copy-start.8 = (f32[1024]{0:T(1024)S(1)}, f32[1024]{0:T(1024)}, u32[]{:S(2)}) copy-start(f32[1024]{0:T(1024)} %param.15) | copy-start | bytes 12292
  79.6 30.5 %copy-start.10 = (s32[96]{0:T(128)S(1)}, s32[96]{0:T(128)}, u32[]{:S(2)}) copy-start(s32[96]{0:T(128)} %position_ref.3) | copy-start | bytes 1156
  98.3 20.7 %copy-start.7 = (f32[4,8,128]{2,1,0:T(8,128)S(1)}, f32[4,8,128]{2,1,0:T(8,128)}, u32[]{:S(2)}) copy-start(f32[4,8,128]{2,1,0:T(8,128)} %get-tuple-element.26.refs_0_) | copy-start | bytes 49156
  98.3 9.4 %collective-permute-start = (f32[4,8,128]{2,1,0:T(8,128)}, f32[4,8,128]{2,1,0:T(8,128)S(1)}, u32[]{:S(2)}, u32[]{:S(2)}) collective-permute-start(f32[4,8,128]{2,1,0:T(8,128)} %get-tuple-element.26.refs_0_), channel_id=1, source_target_pairs={{0,1},{1,2},{2,3},{3,4},{4,5},{5,6},{6,7},{7,0},{8,9},{9,10},{10,1... | collective-permute-start | bytes 49160 | tf_op jit(solution)/shard_map/ppermute | solution.py:532
  102.5 6.0 %collective-permute-start.1 = (f32[4,8,128]{2,1,0:T(8,128)}, f32[4,8,128]{2,1,0:T(8,128)S(1)}, u32[]{:S(2)}, u32[]{:S(2)}) collective-permute-start(f32[4,8,128]{2,1,0:T(8,128)} %get-tuple-element.26.refs_0_), channel_id=1, source_target_pairs={{0,2},{1,3},{2,4},{3,5},{4,6},{5,7},{6,0},{7,1},{8,10},{9,11},{10,... | collective-permute-start | bytes 49160 | tf_op jit(solution)/shard_map/ppermute | solution.py:532
  103.7 15.3 %collective-permute-start.2 = (f32[4,8,128]{2,1,0:T(8,128)}, f32[4,8,128]{2,1,0:T(8,128)S(1)}, u32[]{:S(2)}, u32[]{:S(2)}) collective-permute-start(f32[4,8,128]{2,1,0:T(8,128)} %get-tuple-element.26.refs_0_), channel_id=1, source_target_pairs={{0,3},{1,4},{2,5},{3,6},{4,7},{5,0},{6,1},{7,2},{8,11},{9,12},{10,... | collective-permute-start | bytes 49160 | tf_op jit(solution)/shard_map/ppermute | solution.py:532
  105.3 13.7 %collective-permute-start.3 = (f32[4,8,128]{2,1,0:T(8,128)}, f32[4,8,128]{2,1,0:T(8,128)S(1)}, u32[]{:S(2)}, u32[]{:S(2)}) collective-permute-start(f32[4,8,128]{2,1,0:T(8,128)} %get-tuple-element.26.refs_0_), channel_id=1, source_target_pairs={{0,4},{1,5},{2,6},{3,7},{4,0},{5,1},{6,2},{7,3},{8,12},{9,13},{10,... | collective-permute-start | bytes 49160 | tf_op jit(solution)/shard_map/ppermute | solution.py:532
  105.8 13.2 %collective-permute-start.4 = (f32[4,8,128]{2,1,0:T(8,128)}, f32[4,8,128]{2,1,0:T(8,128)S(1)}, u32[]{:S(2)}, u32[]{:S(2)}) collective-permute-start(f32[4,8,128]{2,1,0:T(8,128)} %get-tuple-element.26.refs_0_), channel_id=1, source_target_pairs={{0,5},{1,6},{2,7},{3,0},{4,1},{5,2},{6,3},{7,4},{8,13},{9,14},{10,... | collective-permute-start | bytes 49160 | tf_op jit(solution)/shard_map/ppermute | solution.py:532
  107.7 11.3 %collective-permute-start.5 = (f32[4,8,128]{2,1,0:T(8,128)}, f32[4,8,128]{2,1,0:T(8,128)S(1)}, u32[]{:S(2)}, u32[]{:S(2)}) collective-permute-start(f32[4,8,128]{2,1,0:T(8,128)} %get-tuple-element.26.refs_0_), channel_id=1, source_target_pairs={{0,6},{1,7},{2,0},{3,1},{4,2},{5,3},{6,4},{7,5},{8,14},{9,15},{10,... | collective-permute-start | bytes 49160 | tf_op jit(solution)/shard_map/ppermute | solution.py:532
  108.4 10.6 %collective-permute-start.6 = (f32[4,8,128]{2,1,0:T(8,128)}, f32[4,8,128]{2,1,0:T(8,128)S(1)}, u32[]{:S(2)}, u32[]{:S(2)}) collective-permute-start(f32[4,8,128]{2,1,0:T(8,128)} %get-tuple-element.26.refs_0_), channel_id=1, source_target_pairs={{0,7},{1,0},{2,1},{3,2},{4,3},{5,4},{6,5},{7,6},{8,15},{9,8},{10,9... | collective-permute-start | bytes 49160 | tf_op jit(solution)/shard_map/ppermute | solution.py:532
  113.1 1.2 copy-start.3
  114.3 13.9 %all-to-all-start.4 = ((f32[8,8,128]{2,1,0:T(8,128)}), f32[8,8,128]{2,1,0:T(8,128)S(1)}, u32[]{:S(2)}, u32[]{:S(2)}) async-start(f32[8,8,128]{2,1,0:T(8,128)} %get-tuple-element.31), calls=%async_computation.4 | async-start | bytes 65536 | tf_op jit(solution)/shard_map/all_to_all | solution.py:362
  128.2 0.6 copy-start.14

commit v4 on v3

--- a/solution.py
+++ b/solution.py
@@ -209,7 +209,7 @@
         scale_ref[index] = jnp.broadcast_to(widen_column(jnp.exp(far), one), (8, width))
 
 
-def scan_kernel(me_ref, part_ref, routed_ref, built_ref, probed_ref, out_ref, *, probe_len, heads):
+def scan_kernel(me_ref, part_ref, routed_ref, built_ref, out_ref, *, probe_len, heads):
     count, height, width = part_ref.shape
     premise = lax.div(me_ref[0] * height, jnp.int32(DSTATE))
     shape = (DSTATE, width)
@@ -224,13 +224,15 @@
         state = state * jnp.exp(total) + part_ref[k].astype(F32)
 
 
-def apply_kernel(table_ref, incoming_ref, routed_ref, local_ref, scale_ref, out_ref, done_ref):
-    step, probe_len, _ = out_ref.shape
+def apply_kernel(
+    table_ref, incoming_ref, routed_ref, local_ref, scale_ref, after_ref, out_ref, done_ref
+):
+    slots, probe_len, _ = out_ref.shape
     done_ref[...] = jnp.zeros_like(done_ref)
-    for index in range(step):
-        premise = table_ref[4 * (pl.program_id(0) * step + index) + 1]
-        product = dot(routed_ref[index, 0:probe_len, :], incoming_ref[premise], 1, 0)
-        out_ref[index] = (product * scale_ref[index, 0:1, :] + local_ref[index]).astype(BF16)
+    for slot in range(slots):
+        premise = table_ref[4 * slot + 1]
+        product = dot(routed_ref[slot, 0:probe_len, :], incoming_ref[premise], 1, 0)
+        out_ref[slot] = (product * scale_ref[slot, 0:1, :] + local_ref[slot]).astype(BF16)
 
 
 def squares(mixed):
@@ -272,7 +274,7 @@
         product = product + reaches[k] * dot(read_ref[0, rows, :], incoming_ref[0], 1, 0)
         near = sums[k] - sums[k][:, middle : middle + 1]
         mixed = product * widen(jnp.exp(near), twice)
-        out_ref[0, rows, :] = mixed * gain_ref[...]
+        out_ref[0, rows, :] = (mixed * gain_ref[...]).astype(BF16)
         total = jnp.where(line == k, squares(mixed), total)
     square_ref[0] = total
 
@@ -296,25 +298,21 @@
 def join_kernel(
     position_ref, me_ref, inner_ref, factor_ref, gain_ref, arrived_ref, out_ref, square_ref, *, seq_dev
 ):
-    pair, length, width = inner_ref.shape
-    row = pl.program_id(0)
-    probe_dev = pair * pl.num_programs(0)
-    parts = []
-    for index in range(pair):
-        probe = row * pair + index
-        owner = lax.div(position_ref[me_ref[0] * probe_dev + probe], jnp.int32(seq_dev))
-        parts.append(inner_ref[index] + factor_ref[index] * arrived_ref[owner].astype(F32))
-    mixed = jnp.concatenate(parts, axis=0)
-    out_ref[...] = mixed * gain_ref[...]
-    total = squares(mixed)
+    probe_dev, length, width = inner_ref.shape
+    pair = 128 // length
+    gain = gain_ref[...]
     line = lax.broadcasted_iota(jnp.int32, (8, 128), 0)
-
-    @pl.when(row == 0)
-    def _():
-        square_ref[...] = jnp.zeros_like(square_ref)
-
+    total = jnp.zeros((8, 128), F32)
+    for row in range(probe_dev // pair):
+        parts = []
+        for probe in range(row * pair, (row + 1) * pair):
+            owner = lax.div(position_ref[me_ref[0] * probe_dev + probe], jnp.int32(seq_dev))
+            parts.append(inner_ref[probe] + factor_ref[probe] * arrived_ref[owner].astype(F32))
+        mixed = jnp.concatenate(parts, axis=0)
+        out_ref[0, 128 * row : 128 * (row + 1), :] = mixed * gain
+        total = jnp.where(line == row, squares(mixed), total)
     for copy in range(square_ref.shape[0]):
-        square_ref[copy] = jnp.where(line == row, total, square_ref[copy])
+        square_ref[copy] = total
 
 
 def norm_kernel(mixed_ref, *refs):
@@ -325,7 +323,7 @@
     rate = lax.rsqrt(total / DIN + EPSILON).T
     for k in range(mixed_ref.shape[1] // 128):
         rows = slice(128 * k, 128 * (k + 1))
-        out_ref[0, rows, :] = (mixed_ref[0, rows, :] * rate[:, k : k + 1]).astype(BF16)
+        out_ref[0, rows, :] = (mixed_ref[0, rows, :].astype(F32) * rate[:, k : k + 1]).astype(BF16)
 
 
 SMEM = pl.BlockSpec(memory_space=pltpu.SMEM)
@@ -427,13 +425,17 @@
     )(tokens, state_inputs, log_decay)
 
     probe_rows = probe_dev * probe_len
+    pair = 128 // probe_len
     inner, factor, probed = call(
         probe_kernel,
         "probes",
-        [along(part.shape) for part in (probe_tokens, probe_inputs, probe_reads, probe_decay)],
-        [along(probe_tokens.shape)] * 2 + [token_spec],
+        [
+            along((pair,) + part.shape[1:], 0)
+            for part in (probe_tokens, probe_inputs, probe_reads, probe_decay)
+        ],
+        [along((pair, probe_len, width), 0)] * 2 + [token_spec],
         [shaped(probe_tokens.shape, F32)] * 2 + [token],
-        (1,),
+        (probe_dev // pair,),
         flops=1_000_000_000,
         moved=8_000_000,
     )(probe_tokens, probe_inputs, probe_reads, probe_decay)
@@ -441,14 +443,14 @@
     starts = call(
         functools.partial(scan_kernel, probe_len=probe_len, heads=heads),
         "scan",
-        [SMEM, VMEM, along(routed_shape), ANY, ANY],
+        [SMEM, VMEM, along(routed_shape), ANY],
         along((seq, height, width)),
         shaped((seq, height, width), BF16),
         (1,),
         limit=48,
         flops=1_000_000_000,
         moved=2_500_000,
-    )(me, parts, routed, built, probed)
+    )(me, parts, routed, built)
     incoming = exchange(starts, "seq").reshape(row_count, DSTATE, width)
 
     step = 4
@@ -489,22 +491,14 @@
     answers, applied = call(
         apply_kernel,
         "apply",
-        [SMEM, VMEM]
-        + [
-            along(shape, 0)
-            for shape in (
-                (step,) + routed_shape[1:],
-                (step, probe_len, width),
-                (step, 8, width),
-            )
-        ],
-        [along((step, probe_len, width), 0), token_spec],
+        [SMEM, VMEM, VMEM, VMEM, VMEM, ANY],
+        [along((seq, probe_len, width)), token_spec],
         [shaped((seq, probe_len, width), BF16), token],
-        (seq // step,),
-        limit=48,
+        (1,),
+        limit=40,
         flops=1_000_000_000,
         moved=8_000_000,
-    )(table, incoming, routed, local_part, scale)
+    )(table, incoming, routed, local_part, scale, probed)
     arrived = exchange(answers, "seq")
 
     gain = norm_gain.reshape(1, width)
@@ -523,8 +517,9 @@
             ANY,
         ],
         [x_spec, square_spec],
-        [shaped(tokens.shape, F32), shaped(square_shape, F32)],
+        [shaped(tokens.shape, BF16), shaped(square_shape, F32)],
         (row_count,),
+        limit=58,
         flops=12_000_000_000,
         moved=60_000_000,
     )(state_inputs, state_reads, log_decay, incoming, right, gain, applied)
@@ -533,21 +528,14 @@
         for turn in range(1, ring)
     ]
 
+    probe_shape = (1, probe_rows, width)
     probe_mixed, probe_square = call(
         functools.partial(join_kernel, seq_dev=seq_dev),
         "join",
-        [
-            SMEM,
-            SMEM,
-            along((128 // probe_len, probe_len, width), 0),
-            along((128 // probe_len, probe_len, width), 0),
-            along((1, width)),
-            VMEM,
-        ],
-        [along((128, width), 0), along((ring, 8, 128))],
-        [shaped((probe_rows, width), F32), shaped((ring, 8, 128), F32)],
-        (probe_rows // 128,),
-        limit=48,
+        [SMEM, SMEM, VMEM, VMEM, VMEM, VMEM],
+        [VMEM, VMEM],
+        [shaped(probe_shape, F32), shaped((ring, 8, 128), F32)],
+        limit=40,
         flops=1_000_000,
         moved=5_000_000,
     )(branch_position, me, inner, factor, gain, arrived)
@@ -560,22 +548,20 @@
         x_spec,
         shaped(tokens.shape, BF16),
         (row_count,),
-        limit=50,
+        limit=54,
         flops=1_000_000_000,
         moved=30_000_000,
     )(mixed, *shared)
-    probe_shape = (1, probe_rows, width)
     probe_out = call(
         norm_kernel,
         "probe_norm",
-        [along(probe_shape), along((ring, 8, 128))],
-        along(probe_shape),
+        [VMEM, VMEM],
+        VMEM,
         shaped(probe_shape, BF16),
-        (1,),
-        limit=54,
+        limit=40,
         flops=1_000_000,
         moved=2_000_000,
-    )(probe_mixed.reshape(probe_shape), probe_square)
+    )(probe_mixed, probe_square)
     return (premise_out, probe_out.reshape(probe_dev, probe_len, width))
 
 

time: 132 us -> 127 us (0.962)
  Pallas kernels: 75.7 us -> 69.1 us
  local copies, waits for them, and re-layouts: 4.54 us -> 10.8 us
  waiting for transfers between devices: 7.36 us -> 3.87 us
    unnamed x30 -> x46, local copies, waits for them, and re-layouts: 4.54 us -> 10.8 us
    pallas_call x3, Pallas kernels: 12.6 us -> 7.33 us  [the longest x1 4.9 us: local(): call(probe_kernel, 'probes', [along((pair,) + part.shape[1:], 0) for part...]
    all_to_all x5, waiting for transfers between devices: 7.34 us -> 3.85 us  [exchange(): return lax.all_to_all(value, axis, split_axis=0, concat_axis=0, tiled=True)]
    pallas_call x1, Pallas kernels: 3 us -> 1.65 us  [local(): call(functools.partial(join_kernel, seq_dev=seq_dev), 'join', [SMEM, SMEM...]
  transfers between devices with their start and end apart: 12 -> 12, of which waited for: 1 -> 2; matrix products, arithmetic and copies ran while one was open for 0% -> 0% of each run, Pallas kernels for 49% -> 50%
where the time goes in v4:
time: 127 us
  Pallas kernels  69.1 us (54%)
  starting transfers between devices  42.1 us (33%)
  local copies, waits for them, and re-layouts  10.8 us (9%)
  waiting for transfers between devices  3.87 us (3%)
    all_to_all x5, starting transfers between devices, exchange(): return lax.all_to_all(value, axis, split_axis=0, concat_axis=0, tiled=True)  30.1 us
    pallas_call x1, Pallas kernels, local(): call(main_kernel, 'main', [in_spec, in_spec, decay_spec, along((1, DSTATE...  18.6 us
    pallas_call x1, Pallas kernels, local(): call(build_kernel, 'build', [x_spec, in_spec, decay_spec], [along((1, cou...  12 us
    ppermute x7, starting transfers between devices, local(): lax.ppermute(square, 'head', [(i, (i + turn) % ring) for i in range(ring)])  12 us
    unnamed x46, local copies, waits for them, and re-layouts  10.8 us
    pallas_call x1, Pallas kernels, local(): call(end_kernel, 'ends', [x_spec, in_spec, decay_spec], along((1, DSTATE,...  8.98 us
    pallas_call x1, Pallas kernels, local(): pl.pallas_call(functools.partial(branch_kernel, step=step), name='branch'...  8.76 us
    pallas_call x1, Pallas kernels, local(): call(norm_kernel, 'norm', [x_spec] + [square_spec] * ring, x_spec, shaped...  7.91 us
  transfers between devices with their start and end apart: 12, of which 2 were waited for; matrix products, arithmetic and copies ran while one was open for 0% of the time, Pallas kernels for 50%

profile of v4, /device:TPU:1, one launch (start us, length us, event | category | flops | bytes accessed | tf_op | source)
XLA Modules:
  0.0 126.7 jit_solution(7331131182072473688)
XLA Ops:
  0.6 2.1 %route.1 = (bf16[16,80,128]{2,1,0:T(8,128)(2,1)}, s32[64]{0:T(128)}) custom-call(s32[96]{0:T(128)} %position_ref.3, s32[96]{0:T(128)} %premise_ref.1, s32[1]{0:T(128)} %bitcast.me_ref, bf16[6,64,128]{2,1,0:T(8,128)(2,1)} %read_ref.2, f32[4,16,1024]{2,1,0:T(8,128)} %decay_ref.9), custom_call_target="tpu_custom_call" | custom-call | bytes 800000 | tf_op jit(solution)/shard_map/route/pallas_call | solution.py:387
  2.7 8.6 %all-to-all-start.1 = ((bf16[16,80,128]{2,1,0:T(8,128)(2,1)}), bf16[16,80,128]{2,1,0:T(8,128)(2,1)S(1)}, u32[]{:S(2)}, u32[]{:S(2)}) async-start(bf16[16,80,128]{2,1,0:T(8,128)(2,1)} %get-tuple-element.17), calls=%async_computation.1 | async-start | bytes 655360 | tf_op jit(solution)/shard_map/all_to_all | solution.py:360
  11.4 9.0 %ends.1 = bf16[4,128,1024]{2,1,0:T(8,128)(2,1)} custom-call(bf16[4,1024,1024]{2,1,0:T(8,128)(2,1)} %x_ref.4, bf16[4,1024,128]{2,1,0:T(8,128)(2,1)} %in_ref.7, f32[4,16,1024]{2,1,0:T(8,128)} %decay_ref.9), custom_call_target="tpu_custom_call" | custom-call | flops 4000000000 | bytes 20000000 | tf_op jit(solution)/shard_map/ends/pallas_call | solution.py:401
  20.3 6.7 %all-to-all-start = ((bf16[16,32,1024]{2,1,0:T(8,128)(2,1)}), bf16[16,32,1024]{2,1,0:T(8,128)(2,1)S(1)}, u32[]{:S(2)}, u32[]{:S(2)}) async-start(bf16[16,32,1024]{2,1,0:T(8,128)(2,1)} %bitcast.9), calls=%async_computation | async-start | bytes 2097152 | tf_op jit(solution)/shard_map/all_to_all | solution.py:360
  27.0 12.0 %build.1 = (bf16[4,8,256,1024]{3,2,1,0:T(8,128)(2,1)}, f32[8,128]{1,0:T(8,128)}) custom-call(bf16[4,1024,1024]{2,1,0:T(8,128)(2,1)} %x_ref.4, bf16[4,1024,128]{2,1,0:T(8,128)(2,1)} %in_ref.7, f32[4,16,1024]{2,1,0:T(8,128)} %decay_ref.9), custom_call_target="tpu_custom_call" | custom-call | flops 5000000000 | bytes 40000000 | tf_op jit(solution)/shard_map/build/pallas_call | solution.py:416
  39.0 3.2 %all-to-all-done.part_ref = bf16[16,32,1024]{2,1,0:T(8,128)(2,1)S(1)} async-done(((bf16[16,32,1024]{2,1,0:T(8,128)(2,1)}), bf16[16,32,1024]{2,1,0:T(8,128)(2,1)S(1)}, u32[]{:S(2)}, u32[]{:S(2)}) %all-to-all-start) | async-done | bytes 1048608 | tf_op jit(solution)/shard_map/all_to_all | solution.py:360
  42.2 0.7 copy-done.15
  42.9 1.7 %scan.1 = bf16[16,32,1024]{2,1,0:T(8,128)(2,1)} custom-call(s32[1]{0:T(128)} %bitcast.me_ref, bf16[16,32,1024]{2,1,0:T(8,128)(2,1)S(1)} %all-to-all-done.part_ref, bf16[16,80,128]{2,1,0:T(8,128)(2,1)S(1)} %all-to-all-done.1.routed_ref.refs_12_, f32[8,128]{1,0:T(8,128)S(1)} %copy-done.15), custom_call_target="tpu_custom_call" | custom-call | flops 1000000000 | bytes 2500000 | tf_op jit(solution)/shard_map/scan/pallas_call | solution.py:443
  44.6 4.0 %all-to-all-start.2 = ((bf16[16,32,1024]{2,1,0:T(8,128)(2,1)}), bf16[16,32,1024]{2,1,0:T(8,128)(2,1)S(1)}, u32[]{:S(2)}, u32[]{:S(2)}) async-start(bf16[16,32,1024]{2,1,0:T(8,128)(2,1)} %scan.1), calls=%async_computation.2 | async-start | bytes 2097152 | tf_op jit(solution)/shard_map/all_to_all | solution.py:360
  48.6 4.9 %probes.1 = (f32[6,64,1024]{2,1,0:T(8,128)}, f32[6,64,1024]{2,1,0:T(8,128)}, f32[8,128]{1,0:T(8,128)}) custom-call(bf16[6,64,1024]{2,1,0:T(8,128)(2,1)} %x_ref.5, bf16[6,64,128]{2,1,0:T(8,128)(2,1)} %in_ref.6, bf16[6,64,128]{2,1,0:T(8,128)(2,1)} %read_ref.2, f32[6,16,64]{2,1,0:T(8,128)} %decay_ref.8), custom_call_target="tpu_custom_call" | custom-call | flops 1000000000 | bytes 8000000 | tf_op jit(solution)/shard_map/probes/pallas_call | solution.py:429
  53.5 8.8 %branch.1 = (f32[16,64,1024]{2,1,0:T(8,128)}, f32[16,8,1024]{2,1,0:T(8,128)}) custom-call(s32[64]{0:T(128)} %get-tuple-element.20.table_ref, bf16[4,8,256,1024]{3,2,1,0:T(8,128)(2,1)} %get-tuple-element.19.refs_0_.refs_1_.refs_2_.refs_3_.right_ref, bf16[4,8,256,1024]{3,2,1,0:T(8,128)(2,1)} %get-tuple-element.19.refs_0_.refs_1_.refs_2_.refs_3_.right_ref, ...), custom_call_target="tpu_custom_call" | custom-call | flops 1000000000 | bytes 20000000 | tf_op jit(solution)/shard_map/branch/pallas_call | solution.py:466
  62.3 0.7 all-to-all-done.2
  63.0 2.6 %copy-done = f32[16,64,1024]{2,1,0:T(8,128)S(1)} copy-done((f32[16,64,1024]{2,1,0:T(8,128)S(1)}, f32[16,64,1024]{2,1,0:T(8,128)}, u32[]{:S(2)}) %copy-start) | copy-done | bytes 4194328
  65.5 1.0 copy-done.9
  66.6 1.3 %apply.1 = (bf16[16,64,1024]{2,1,0:T(8,128)(2,1)S(1)}, f32[8,128]{1,0:T(8,128)S(1)}) custom-call(s32[64]{0:T(128)S(1)} %copy-done.12, bf16[4,128,1024]{2,1,0:T(8,128)(2,1)S(1)} %bitcast.5, bf16[16,80,128]{2,1,0:T(8,128)(2,1)S(1)} %copy-done.3, f32[16,64,1024]{2,1,0:T(8,128)S(1)} %copy-done, f32[16,8,1024]{2,1,0:T(8,128)S(1)} %copy-done.9, ...), custom_call_target="tpu_custom_call" | custom-call | flops 1000000000 | bytes 8000000 | tf_op jit(solution)/shard_map/apply/pallas_call | solution.py:491
  67.9 1.3 %copy-done.4 = bf16[16,64,1024]{2,1,0:T(8,128)(2,1)} copy-done((bf16[16,64,1024]{2,1,0:T(8,128)(2,1)}, bf16[16,64,1024]{2,1,0:T(8,128)(2,1)S(1)}, u32[]{:S(2)}) %copy-start.4) | copy-done | bytes 2097176
  69.2 0.6 copy-done.14
  69.8 6.2 %all-to-all-start.3 = ((bf16[16,64,1024]{2,1,0:T(8,128)(2,1)}), bf16[16,64,1024]{2,1,0:T(8,128)(2,1)S(1)}, u32[]{:S(2)}, u32[]{:S(2)}) async-start(bf16[16,64,1024]{2,1,0:T(8,128)(2,1)} %copy-done.4), calls=%async_computation.3 | async-start | bytes 4194304 | tf_op jit(solution)/shard_map/all_to_all | solution.py:360
  76.0 18.6 %main.1 = (bf16[4,1024,1024]{2,1,0:T(8,128)(2,1)}, f32[4,8,128]{2,1,0:T(8,128)}) custom-call(bf16[4,1024,128]{2,1,0:T(8,128)(2,1)} %in_ref.7, bf16[4,1024,128]{2,1,0:T(8,128)(2,1)} %read_ref.3, f32[4,16,1024]{2,1,0:T(8,128)} %decay_ref.9, bf16[4,128,1024]{2,1,0:T(8,128)(2,1)} %bitcast.6, ...), custom_call_target="tpu_custom_call" | custom-call | flops 12000000000 | bytes 60000000 | tf_op jit(solution)/shard_map/main/pallas_call | solution.py:507
  94.6 4.4 %collective-permute-start = (f32[4,8,128]{2,1,0:T(8,128)}, f32[4,8,128]{2,1,0:T(8,128)S(1)}, u32[]{:S(2)}, u32[]{:S(2)}) collective-permute-start(f32[4,8,128]{2,1,0:T(8,128)} %get-tuple-element.26.refs_0_), channel_id=1, source_target_pairs={{0,1},{1,2},{2,3},{3,4},{4,5},{5,6},{6,7},{7,0},{8,9},{9,10},{10,1... | collective-permute-start | bytes 49160 | tf_op jit(solution)/shard_map/ppermute | solution.py:527
  99.0 1.2 collective-permute-start.1
  100.2 1.6 %collective-permute-start.2 = (f32[4,8,128]{2,1,0:T(8,128)}, f32[4,8,128]{2,1,0:T(8,128)S(1)}, u32[]{:S(2)}, u32[]{:S(2)}) collective-permute-start(f32[4,8,128]{2,1,0:T(8,128)} %get-tuple-element.26.refs_0_), channel_id=1, source_target_pairs={{0,3},{1,4},{2,5},{3,6},{4,7},{5,0},{6,1},{7,2},{8,11},{9,12},{10,... | collective-permute-start | bytes 49160 | tf_op jit(solution)/shard_map/ppermute | solution.py:527
  102.3 2.0 %collective-permute-start.4 = (f32[4,8,128]{2,1,0:T(8,128)}, f32[4,8,128]{2,1,0:T(8,128)S(1)}, u32[]{:S(2)}, u32[]{:S(2)}) collective-permute-start(f32[4,8,128]{2,1,0:T(8,128)} %get-tuple-element.26.refs_0_), channel_id=1, source_target_pairs={{0,5},{1,6},{2,7},{3,0},{4,1},{5,2},{6,3},{7,4},{8,13},{9,14},{10,... | collective-permute-start | bytes 49160 | tf_op jit(solution)/shard_map/ppermute | solution.py:527
  104.3 0.7 collective-permute-start.5
  105.0 1.7 %collective-permute-start.6 = (f32[4,8,128]{2,1,0:T(8,128)}, f32[4,8,128]{2,1,0:T(8,128)S(1)}, u32[]{:S(2)}, u32[]{:S(2)}) collective-permute-start(f32[4,8,128]{2,1,0:T(8,128)} %get-tuple-element.26.refs_0_), channel_id=1, source_target_pairs={{0,7},{1,0},{2,1},{3,2},{4,3},{5,4},{6,5},{7,6},{8,15},{9,8},{10,9... | collective-permute-start | bytes 49160 | tf_op jit(solution)/shard_map/ppermute | solution.py:527
  106.6 1.4 %copy-done.7 = f32[6,64,1024]{2,1,0:T(8,128)S(1)} copy-done((f32[6,64,1024]{2,1,0:T(8,128)S(1)}, f32[6,64,1024]{2,1,0:T(8,128)}, u32[]{:S(2)}) %copy-start.7) | copy-done | bytes 1572888
  108.0 1.4 %copy-done.8 = f32[6,64,1024]{2,1,0:T(8,128)S(1)} copy-done((f32[6,64,1024]{2,1,0:T(8,128)S(1)}, f32[6,64,1024]{2,1,0:T(8,128)}, u32[]{:S(2)}) %copy-start.8) | copy-done | bytes 1572888
  109.5 1.6 %join.1 = (f32[1,384,1024]{2,1,0:T(8,128)S(1)}, f32[8,8,128]{2,1,0:T(8,128)}) custom-call(s32[96]{0:T(128)S(1)} %copy-done.13, s32[1]{0:T(128)} %bitcast.me_ref, f32[6,64,1024]{2,1,0:T(8,128)S(1)} %copy-done.7, f32[6,64,1024]{2,1,0:T(8,128)S(1)} %copy-done.8, f32[1,1024]{1,0:T(1,128)S(1)} %bitcast.8, bf16[16,64,1024]{2,1,0:T(8,128)(2,1)S(1)} %all-to-all-done.3.arrived_ref), custom_call_target="tpu_custom_call" | custom-call | flops 1000000 | bytes 5000000 | tf_op jit(solution)/shard_map/join/pallas_call | solution.py:532
  111.1 1.2 copy-done.5
  112.3 4.6 %all-to-all-start.4 = ((f32[8,8,128]{2,1,0:T(8,128)}), f32[8,8,128]{2,1,0:T(8,128)S(1)}, u32[]{:S(2)}, u32[]{:S(2)}) async-start(f32[8,8,128]{2,1,0:T(8,128)} %get-tuple-element.31), calls=%async_computation.4 | async-start | bytes 65536 | tf_op jit(solution)/shard_map/all_to_all | solution.py:360
  117.6 7.9 %norm.1 = bf16[4,1024,1024]{2,1,0:T(8,128)(2,1)} custom-call(bf16[4,1024,1024]{2,1,0:T(8,128)(2,1)} %get-tuple-element.25.mixed_ref, f32[4,8,128]{2,1,0:T(8,128)} %get-tuple-element.26.refs_0_, f32[4,8,128]{2,1,0:T(8,128)} %copy-done.16, f32[4,8,128]{2,1,0:T(8,128)} %copy-done.17, f32[4,8,128]{2,1,0:T(8,128)} %copy-done.18, f32[4,8,128]{2,1,0:T(8,128)} %copy-done.19, ...), custom_call_target="tpu_custom_call" | custom-call | flops 1000000000 | bytes 30000000 | tf_op jit(solution)/shard_map/norm/pallas_call | solution.py:544
  125.5 1.1 probe_norm.1
  (49 shorter events, 1.2 us)
Async XLA Ops:
  2.7 17.6 %all-to-all-start.1 = ((bf16[16,80,128]{2,1,0:T(8,128)(2,1)}), bf16[16,80,128]{2,1,0:T(8,128)(2,1)S(1)}, u32[]{:S(2)}, u32[]{:S(2)}) async-start(bf16[16,80,128]{2,1,0:T(8,128)(2,1)} %get-tuple-element.17), calls=%async_computation.1 | async-start | bytes 655360 | tf_op jit(solution)/shard_map/all_to_all | solution.py:360
  20.3 21.9 %copy-start.2 = (bf16[16,80,128]{2,1,0:T(8,128)(2,1)}, bf16[16,80,128]{2,1,0:T(8,128)(2,1)S(1)}, u32[]{:S(2)}) copy-start(bf16[16,80,128]{2,1,0:T(8,128)(2,1)S(1)} %all-to-all-done.1.routed_ref.refs_12_) | copy-start | bytes 983044
  20.3 21.9 %all-to-all-start = ((bf16[16,32,1024]{2,1,0:T(8,128)(2,1)}), bf16[16,32,1024]{2,1,0:T(8,128)(2,1)S(1)}, u32[]{:S(2)}, u32[]{:S(2)}) async-start(bf16[16,32,1024]{2,1,0:T(8,128)(2,1)} %bitcast.9), calls=%async_computation | async-start | bytes 2097152 | tf_op jit(solution)/shard_map/all_to_all | solution.py:360
  42.2 0.7 copy-start.15
  44.6 18.3 %all-to-all-start.2 = ((bf16[16,32,1024]{2,1,0:T(8,128)(2,1)}), bf16[16,32,1024]{2,1,0:T(8,128)(2,1)S(1)}, u32[]{:S(2)}, u32[]{:S(2)}) async-start(bf16[16,32,1024]{2,1,0:T(8,128)(2,1)} %scan.1), calls=%async_computation.2 | async-start | bytes 2097152 | tf_op jit(solution)/shard_map/all_to_all | solution.py:360
  53.5 9.4 %copy-start.3 = (bf16[16,80,128]{2,1,0:T(8,128)(2,1)S(1)}, bf16[16,80,128]{2,1,0:T(8,128)(2,1)}, u32[]{:S(2)}) copy-start(bf16[16,80,128]{2,1,0:T(8,128)(2,1)} %copy-done.2) | copy-start | bytes 983044
  53.5 9.4 %copy-start.11 = (f32[8,128]{1,0:T(8,128)S(1)}, f32[8,128]{1,0:T(8,128)}, u32[]{:S(2)}) copy-start(f32[8,128]{1,0:T(8,128)} %get-tuple-element.23.after_ref) | copy-start | bytes 12292
  53.5 9.4 %copy-start.12 = (s32[64]{0:T(128)S(1)}, s32[64]{0:T(128)}, u32[]{:S(2)}) copy-start(s32[64]{0:T(128)} %get-tuple-element.20.table_ref) | copy-start | bytes 772
  62.9 6.8 %copy-start.1 = (bf16[16,32,1024]{2,1,0:T(8,128)(2,1)}, bf16[16,32,1024]{2,1,0:T(8,128)(2,1)S(1)}, u32[]{:S(2)}) copy-start(bf16[16,32,1024]{2,1,0:T(8,128)(2,1)S(1)} %all-to-all-done.2) | copy-start | bytes 3145732
  63.0 2.6 %copy-start = (f32[16,64,1024]{2,1,0:T(8,128)S(1)}, f32[16,64,1024]{2,1,0:T(8,128)}, u32[]{:S(2)}) copy-start(f32[16,64,1024]{2,1,0:T(8,128)} %get-tuple-element.21.local_ref) | copy-start | bytes 12582916
  65.5 1.0 copy-start.9
  67.9 1.3 %copy-start.4 = (bf16[16,64,1024]{2,1,0:T(8,128)(2,1)}, bf16[16,64,1024]{2,1,0:T(8,128)(2,1)S(1)}, u32[]{:S(2)}) copy-start(bf16[16,64,1024]{2,1,0:T(8,128)(2,1)S(1)} %get-tuple-element.29) | copy-start | bytes 6291460
  69.8 36.8 %all-to-all-start.3 = ((bf16[16,64,1024]{2,1,0:T(8,128)(2,1)}), bf16[16,64,1024]{2,1,0:T(8,128)(2,1)S(1)}, u32[]{:S(2)}, u32[]{:S(2)}) async-start(bf16[16,64,1024]{2,1,0:T(8,128)(2,1)} %copy-done.4), calls=%async_computation.3 | async-start | bytes 4194304 | tf_op jit(solution)/shard_map/all_to_all | solution.py:360
  76.0 30.7 %copy-start.10 = (f32[1024]{0:T(1024)S(1)}, f32[1024]{0:T(1024)}, u32[]{:S(2)}) copy-start(f32[1024]{0:T(1024)} %param.15) | copy-start | bytes 12292
  76.0 30.7 %copy-start.13 = (s32[96]{0:T(128)S(1)}, s32[96]{0:T(128)}, u32[]{:S(2)}) copy-start(s32[96]{0:T(128)} %position_ref.3) | copy-start | bytes 1156
  94.6 9.7 %collective-permute-start = (f32[4,8,128]{2,1,0:T(8,128)}, f32[4,8,128]{2,1,0:T(8,128)S(1)}, u32[]{:S(2)}, u32[]{:S(2)}) collective-permute-start(f32[4,8,128]{2,1,0:T(8,128)} %get-tuple-element.26.refs_0_), channel_id=1, source_target_pairs={{0,1},{1,2},{2,3},{3,4},{4,5},{5,6},{6,7},{7,0},{8,9},{9,10},{10,1... | collective-permute-start | bytes 49160 | tf_op jit(solution)/shard_map/ppermute | solution.py:527
  99.0 6.0 %collective-permute-start.1 = (f32[4,8,128]{2,1,0:T(8,128)}, f32[4,8,128]{2,1,0:T(8,128)S(1)}, u32[]{:S(2)}, u32[]{:S(2)}) collective-permute-start(f32[4,8,128]{2,1,0:T(8,128)} %get-tuple-element.26.refs_0_), channel_id=1, source_target_pairs={{0,2},{1,3},{2,4},{3,5},{4,6},{5,7},{6,0},{7,1},{8,10},{9,11},{10,... | collective-permute-start | bytes 49160 | tf_op jit(solution)/shard_map/ppermute | solution.py:527
  100.2 16.7 %collective-permute-start.2 = (f32[4,8,128]{2,1,0:T(8,128)}, f32[4,8,128]{2,1,0:T(8,128)S(1)}, u32[]{:S(2)}, u32[]{:S(2)}) collective-permute-start(f32[4,8,128]{2,1,0:T(8,128)} %get-tuple-element.26.refs_0_), channel_id=1, source_target_pairs={{0,3},{1,4},{2,5},{3,6},{4,7},{5,0},{6,1},{7,2},{8,11},{9,12},{10,... | collective-permute-start | bytes 49160 | tf_op jit(solution)/shard_map/ppermute | solution.py:527
  101.8 15.1 %collective-permute-start.3 = (f32[4,8,128]{2,1,0:T(8,128)}, f32[4,8,128]{2,1,0:T(8,128)S(1)}, u32[]{:S(2)}, u32[]{:S(2)}) collective-permute-start(f32[4,8,128]{2,1,0:T(8,128)} %get-tuple-element.26.refs_0_), channel_id=1, source_target_pairs={{0,4},{1,5},{2,6},{3,7},{4,0},{5,1},{6,2},{7,3},{8,12},{9,13},{10,... | collective-permute-start | bytes 49160 | tf_op jit(solution)/shard_map/ppermute | solution.py:527
  102.3 14.6 %collective-permute-start.4 = (f32[4,8,128]{2,1,0:T(8,128)}, f32[4,8,128]{2,1,0:T(8,128)S(1)}, u32[]{:S(2)}, u32[]{:S(2)}) collective-permute-start(f32[4,8,128]{2,1,0:T(8,128)} %get-tuple-element.26.refs_0_), channel_id=1, source_target_pairs={{0,5},{1,6},{2,7},{3,0},{4,1},{5,2},{6,3},{7,4},{8,13},{9,14},{10,... | collective-permute-start | bytes 49160 | tf_op jit(solution)/shard_map/ppermute | solution.py:527
  104.3 12.7 %copy-start.16 = (f32[4,8,128]{2,1,0:T(8,128)}, f32[4,8,128]{2,1,0:T(8,128)S(1)}, u32[]{:S(2)}) copy-start(f32[4,8,128]{2,1,0:T(8,128)S(1)} %collective-permute-done.refs_1_) | copy-start | bytes 49156
  104.3 12.7 %collective-permute-start.5 = (f32[4,8,128]{2,1,0:T(8,128)}, f32[4,8,128]{2,1,0:T(8,128)S(1)}, u32[]{:S(2)}, u32[]{:S(2)}) collective-permute-start(f32[4,8,128]{2,1,0:T(8,128)} %get-tuple-element.26.refs_0_), channel_id=1, source_target_pairs={{0,6},{1,7},{2,0},{3,1},{4,2},{5,3},{6,4},{7,5},{8,14},{9,15},{10,... | collective-permute-start | bytes 49160 | tf_op jit(solution)/shard_map/ppermute | solution.py:527
  105.0 12.1 %copy-start.17 = (f32[4,8,128]{2,1,0:T(8,128)}, f32[4,8,128]{2,1,0:T(8,128)S(1)}, u32[]{:S(2)}) copy-start(f32[4,8,128]{2,1,0:T(8,128)S(1)} %collective-permute-done.1.refs_2_) | copy-start | bytes 49156
  105.0 12.0 %collective-permute-start.6 = (f32[4,8,128]{2,1,0:T(8,128)}, f32[4,8,128]{2,1,0:T(8,128)S(1)}, u32[]{:S(2)}, u32[]{:S(2)}) collective-permute-start(f32[4,8,128]{2,1,0:T(8,128)} %get-tuple-element.26.refs_0_), channel_id=1, source_target_pairs={{0,7},{1,0},{2,1},{3,2},{4,3},{5,4},{6,5},{7,6},{8,15},{9,8},{10,9... | collective-permute-start | bytes 49160 | tf_op jit(solution)/shard_map/ppermute | solution.py:527
  106.6 1.4 %copy-start.7 = (f32[6,64,1024]{2,1,0:T(8,128)S(1)}, f32[6,64,1024]{2,1,0:T(8,128)}, u32[]{:S(2)}) copy-start(f32[6,64,1024]{2,1,0:T(8,128)} %get-tuple-element.27.inner_ref) | copy-start | bytes 4718596
  108.0 1.4 %copy-start.8 = (f32[6,64,1024]{2,1,0:T(8,128)S(1)}, f32[6,64,1024]{2,1,0:T(8,128)}, u32[]{:S(2)}) copy-start(f32[6,64,1024]{2,1,0:T(8,128)} %get-tuple-element.28.factor_ref) | copy-start | bytes 4718596
  111.1 1.2 copy-start.5
  112.3 13.2 %all-to-all-start.4 = ((f32[8,8,128]{2,1,0:T(8,128)}), f32[8,8,128]{2,1,0:T(8,128)S(1)}, u32[]{:S(2)}, u32[]{:S(2)}) async-start(f32[8,8,128]{2,1,0:T(8,128)} %get-tuple-element.31), calls=%async_computation.4 | async-start | bytes 65536 | tf_op jit(solution)/shard_map/all_to_all | solution.py:360
  116.9 0.6 copy-start.18
  117.0 0.6 copy-start.19
  117.0 0.6 copy-start.20
  117.6 7.9 %copy-start.6 = (f32[1,384,1024]{2,1,0:T(8,128)S(1)}, f32[1,384,1024]{2,1,0:T(8,128)}, u32[]{:S(2)}) copy-start(f32[1,384,1024]{2,1,0:T(8,128)} %copy-done.5) | copy-start | bytes 4718596
  (3 other events, 1.8 us)

commit v5 on v3

--- a/solution.py
+++ b/solution.py
@@ -13,7 +13,6 @@
 DIN = 8192
 EPSILON = 1e-05
 BLOCK = 128
-EXTRA = 16
 
 
 def dot(left, right, left_dim, right_dim, precision=None):
@@ -82,53 +81,43 @@
     return lax.broadcasted_iota(jnp.int32, shape, 0) >= lax.broadcasted_iota(jnp.int32, shape, 1)
 
 
-def route_kernel(
-    position_ref, premise_ref, me_ref, reads_ref, decay_ref, out_ref, table_ref, *, seq_dev
+def end_kernel(
+    position_ref, me_ref, x_ref, in_ref, decay_ref, reads_ref, out_ref, scaled_ref, *, seq_dev, height
 ):
-    slots = out_ref.shape[0]
+    _, length, width = x_ref.shape
+    heads = decay_ref.shape[1]
     probe_dev, probe_len, _ = reads_ref.shape
-    rows, heads, length = decay_ref.shape
-    decay = decay_ref[...].reshape(rows * heads, length)
-    ones = jnp.ones((EXTRA, length), BF16)
-    fill = jnp.zeros((DSTATE - rows * heads, length), BF16)
+    row = pl.program_id(0)
+    slices = DSTATE // height
+    folds = probe_len // height
+    decay = decay_ref[0]
+    ones = jnp.ones((height, length), BF16)
+    fill = jnp.zeros((DSTATE - heads, length), BF16)
     total = 0.0
     for part in pieces(decay, 3):
         total = total + dot(ones, jnp.concatenate([part, fill], axis=0), 1, 1)
-    row = lax.broadcasted_iota(jnp.int32, (EXTRA, DSTATE), 0)
-    block = jnp.zeros((EXTRA, DSTATE), F32)
+    line = lax.broadcasted_iota(jnp.int32, (height, DSTATE), 0)
+    block = jnp.zeros((height, DSTATE), F32)
     for index, part in enumerate(pieces(total, 3)):
-        block = jnp.where(row == index, part.astype(F32), block)
+        block = jnp.where(line == index, part.astype(F32), block)
     block = block.astype(BF16)
-    nothing = jnp.zeros((probe_len, DSTATE), BF16)
-    for slot in range(slots):
-        out_ref[slot, 0:probe_len, :] = nothing
-        out_ref[slot, probe_len : probe_len + EXTRA, :] = block
-    for probe in range(probe_dev):
-        owner = lax.div(position_ref[me_ref[0] * probe_dev + probe], jnp.int32(seq_dev))
-        out_ref[owner, 0:probe_len, :] = reads_ref[probe]
-    me = me_ref[0]
-    for slot in range(slots):
-        offset = jnp.int32(0)
-        premise = jnp.int32(0)
-        present = jnp.int32(0)
+    owners = [
+        lax.div(position_ref[me_ref[0] * probe_dev + probe], jnp.int32(seq_dev))
+        for probe in range(probe_dev)
+    ]
+    for part in range(slices):
+        rows = slice(part * height, (part + 1) * height)
+        chosen = jnp.zeros((probe_len, DSTATE), F32)
         for probe in range(probe_dev):
-            position = position_ref[slot * probe_dev + probe]
-            here = lax.div(position, jnp.int32(seq_dev)) == me
-            offset = jnp.where(here, position - me * seq_dev, offset)
-            premise = jnp.where(here, premise_ref[slot * probe_dev + probe], premise)
-            present = jnp.where(here, jnp.int32(1), present)
-        block = lax.div(offset, jnp.int32(BLOCK))
-        table_ref[4 * slot] = present
-        table_ref[4 * slot + 1] = premise
-        table_ref[4 * slot + 2] = block
-        table_ref[4 * slot + 3] = offset - block * BLOCK
-
-
-def end_kernel(x_ref, in_ref, decay_ref, out_ref, scaled_ref):
-    _, length, width = x_ref.shape
-    heads = decay_ref.shape[1]
+            here = owners[probe] == row * slices + part
+            chosen = jnp.where(here, reads_ref[probe].astype(F32), chosen)
+        for fold in range(folds):
+            lanes = slice(width + fold * DSTATE, width + (fold + 1) * DSTATE)
+            out_ref[0, rows, lanes] = chosen[fold * height : (fold + 1) * height].astype(BF16)
+        out_ref[0, rows, width + folds * DSTATE :] = block
+
     twice = spread_twice(spread(heads, width))
-    sums = prefix(decay_ref[0], BLOCK)
+    sums = prefix(decay, BLOCK)
     after = jnp.zeros((heads, 1), F32)
     for k in reversed(range(length // BLOCK)):
         rows = slice(k * BLOCK, (k + 1) * BLOCK)
@@ -136,7 +125,7 @@
         factor = widen(jnp.exp((last - sums[k]) + after), twice)
         scaled_ref[rows, :] = (x_ref[0, rows, :].astype(F32) * factor).astype(BF16)
         after = after + last
-    out_ref[0] = dot(in_ref[0], scaled_ref[...], 0, 0).astype(BF16)
+    out_ref[0, :, 0:width] = dot(in_ref[0], scaled_ref[...], 0, 0).astype(BF16)
 
 
 def chain_factors(sums, one):
@@ -151,7 +140,9 @@
     return factors
 
 
-def build_kernel(x_ref, in_ref, decay_ref, out_ref, done_ref):
+def build_kernel(
+    position_ref, premise_ref, me_ref, x_ref, in_ref, decay_ref, out_ref, table_ref, *, seq_dev, probe_dev
+):
     _, length, width = x_ref.shape
     heads = decay_ref.shape[1]
     middle = BLOCK // 2 - 1
@@ -160,7 +151,24 @@
     sums = prefix(decay_ref[0], BLOCK)
     factors = chain_factors(sums, one)
     count = length // BLOCK
-    done_ref[...] = jnp.zeros_like(done_ref)
+
+    @pl.when(pl.program_id(0) == 0)
+    def _():
+        me = me_ref[0]
+        for slot in range(table_ref.shape[0] // 4):
+            offset = jnp.int32(0)
+            premise = jnp.int32(0)
+            for probe in range(probe_dev):
+                position = position_ref[slot * probe_dev + probe]
+                here = lax.div(position, jnp.int32(seq_dev)) == me
+                offset = jnp.where(here, position - me * seq_dev, offset)
+                premise = jnp.where(here, premise_ref[slot * probe_dev + probe], premise)
+            block = lax.div(offset, jnp.int32(BLOCK))
+            table_ref[4 * slot] = jnp.int32(0)
+            table_ref[4 * slot + 1] = premise
+            table_ref[4 * slot + 2] = block
+            table_ref[4 * slot + 3] = offset - block * BLOCK
+
     for k in range(count):
         rows = slice(k * BLOCK, (k + 1) * BLOCK)
         near = sums[k] - sums[k][:, middle : middle + 1]
@@ -181,8 +189,9 @@
 
 def branch_kernel(table_ref, *refs, step):
     rights, inputs, decays = (refs[i * step : (i + 1) * step] for i in range(3))
-    routed_ref, out_ref, scale_ref = refs[3 * step :]
-    _, probe_len, width = out_ref.shape
+    reads_refs, out_ref = refs[3 * step : -1], refs[-1]
+    _, depth, width = out_ref.shape
+    probe_len = depth - 8
     _, heads, length = decays[0].shape
     one = spread(heads, width)
     lane = lax.broadcasted_iota(jnp.int32, (heads, length), 1)
@@ -190,7 +199,7 @@
     lefts = []
     for index in range(step):
         slot = pl.program_id(0) * step + index
-        reads = routed_ref[index, 0:probe_len, :]
+        reads = jnp.concatenate([ref[index] for ref in reads_refs], axis=0)
         keep = key <= table_ref[4 * slot + 3]
         gram = jnp.where(keep, dot(reads, inputs[index][0], 1, 1), 0.0).astype(BF16)
         lefts.append(jnp.concatenate([gram, reads], axis=1))
@@ -205,46 +214,45 @@
         earlier = jnp.where((lane > offset) & (lane <= middle), decay, 0.0)
         near = jnp.sum(later - earlier, axis=1, keepdims=True)
         product = dot(lefts[index], rights[index][0, 0], 1, 0)
-        out_ref[index] = product * widen_column(jnp.exp(near), one)
-        scale_ref[index] = jnp.broadcast_to(widen_column(jnp.exp(far), one), (8, width))
-
-
-def scan_kernel(me_ref, part_ref, routed_ref, built_ref, probed_ref, out_ref, *, probe_len, heads):
-    count, height, width = part_ref.shape
-    premise = lax.div(me_ref[0] * height, jnp.int32(DSTATE))
+        out_ref[index, 0:probe_len, :] = product * widen_column(jnp.exp(near), one)
+        scale = widen_column(jnp.exp(far), one)
+        out_ref[index, probe_len:, :] = jnp.broadcast_to(scale, (8, width))
+
+
+def scan_kernel(part_ref, built_ref, probed_ref, out_ref, *, heads):
+    count, height, width = out_ref.shape
     shape = (DSTATE, width)
-    lane = lax.broadcasted_iota(jnp.int32, shape, 0) - premise * heads
+    lane = lax.broadcasted_iota(jnp.int32, shape, 0)
     channel = lax.broadcasted_iota(jnp.int32, shape, 1)
     pick = jnp.where(lax.div(channel, jnp.int32(width // heads)) == lane, 1.0, 0.0).astype(BF16)
     state = jnp.zeros((height, width), F32)
+    last = part_ref.shape[2] - DSTATE
     for k in range(count):
         out_ref[k] = state.astype(BF16)
-        total = dot(routed_ref[k, probe_len : probe_len + EXTRA, :], pick, 1, 0)
+        total = dot(part_ref[k, 0:16, last:], pick, 1, 0)
         total = jnp.sum(total[0:8], axis=0, keepdims=True)
-        state = state * jnp.exp(total) + part_ref[k].astype(F32)
-
-
-def apply_kernel(table_ref, incoming_ref, routed_ref, local_ref, scale_ref, out_ref, done_ref):
+        state = state * jnp.exp(total) + part_ref[k, :, 0:width].astype(F32)
+
+
+def apply_kernel(table_ref, incoming_ref, *refs):
+    reads_refs, local_ref, out_ref = refs[:-2], refs[-2], refs[-1]
     step, probe_len, _ = out_ref.shape
-    done_ref[...] = jnp.zeros_like(done_ref)
     for index in range(step):
         premise = table_ref[4 * (pl.program_id(0) * step + index) + 1]
-        product = dot(routed_ref[index, 0:probe_len, :], incoming_ref[premise], 1, 0)
-        out_ref[index] = (product * scale_ref[index, 0:1, :] + local_ref[index]).astype(BF16)
+        reads = jnp.concatenate([ref[index] for ref in reads_refs], axis=0)
+        product = dot(reads, incoming_ref[premise], 1, 0)
+        scale = local_ref[index, probe_len : probe_len + 1, :]
+        answer = product * scale + local_ref[index, 0:probe_len, :]
+        out_ref[index] = answer.astype(BF16)
 
 
 def squares(mixed):
-    total = mixed[:, 0:128] * mixed[:, 0:128]
-    for k in range(1, mixed.shape[1] // 128):
-        part = mixed[:, 128 * k : 128 * (k + 1)]
-        total = total + part * part
-    ones = jnp.ones((8, 128), BF16)
-    high, low = pieces(total, 2)
-    return dot(ones, high, 1, 1) + dot(ones, low, 1, 1)
+    half = mixed.astype(BF16)
+    return dot(jnp.ones((8, mixed.shape[1]), BF16), half * half, 1, 1)
 
 
 def main_kernel(
-    in_ref, read_ref, decay_ref, incoming_ref, right_ref, gain_ref, after_ref, out_ref, square_ref
+    in_ref, read_ref, decay_ref, incoming_ref, right_ref, gain_ref, out_ref, square_ref
 ):
     _, length, width = out_ref.shape
     heads = decay_ref.shape[1]
@@ -272,7 +280,7 @@
         product = product + reaches[k] * dot(read_ref[0, rows, :], incoming_ref[0], 1, 0)
         near = sums[k] - sums[k][:, middle : middle + 1]
         mixed = product * widen(jnp.exp(near), twice)
-        out_ref[0, rows, :] = mixed * gain_ref[...]
+        out_ref[0, rows, :] = (mixed * gain_ref[...]).astype(BF16)
         total = jnp.where(line == k, squares(mixed), total)
     square_ref[0] = total
 
@@ -305,7 +313,7 @@
         owner = lax.div(position_ref[me_ref[0] * probe_dev + probe], jnp.int32(seq_dev))
         parts.append(inner_ref[index] + factor_ref[index] * arrived_ref[owner].astype(F32))
     mixed = jnp.concatenate(parts, axis=0)
-    out_ref[...] = mixed * gain_ref[...]
+    out_ref[0] = mixed * gain_ref[...]
     total = squares(mixed)
     line = lax.broadcasted_iota(jnp.int32, (8, 128), 0)
 
@@ -321,11 +329,13 @@
     out_ref = refs[-1]
     total = 0.0
     for ref in refs[:-1]:
-        total = total + jnp.sum(ref[...].reshape(-1, 8, 128), axis=0)
-    rate = lax.rsqrt(total / DIN + EPSILON).T
-    for k in range(mixed_ref.shape[1] // 128):
-        rows = slice(128 * k, 128 * (k + 1))
-        out_ref[0, rows, :] = (mixed_ref[0, rows, :] * rate[:, k : k + 1]).astype(BF16)
+        total = total + jnp.sum(ref[...].reshape((-1,) + (mixed_ref.shape[0], 8, 128)), axis=0)
+    for index in range(mixed_ref.shape[0]):
+        rate = lax.rsqrt(total[index] / DIN + EPSILON).T
+        for k in range(mixed_ref.shape[1] // 128):
+            rows = slice(128 * k, 128 * (k + 1))
+            scaled = mixed_ref[index, rows, :].astype(F32) * rate[:, k : k + 1]
+            out_ref[index, rows, :] = scaled.astype(BF16)
 
 
 SMEM = pl.BlockSpec(memory_space=pltpu.SMEM)
@@ -382,73 +392,67 @@
     heads = log_decay.shape[1]
     probe_dev, probe_len, _ = probe_tokens.shape
     height = row_count * DSTATE // seq
-    routed_shape = (seq, probe_len + EXTRA, DSTATE)
     count = seq_dev // BLOCK
     depth = BLOCK + DSTATE
-
-    routed, table = call(
-        functools.partial(route_kernel, seq_dev=seq_dev),
-        "route",
-        [SMEM, SMEM, SMEM, along(probe_reads.shape), along(log_decay.shape)],
-        [along(routed_shape), SMEM],
-        [shaped(routed_shape, BF16), shaped((4 * seq,), jnp.int32)],
-        (1,),
-        moved=800_000,
-    )(branch_position, branch_premise, me, probe_reads, log_decay)
-    routed = exchange(routed, "seq")
 
     x_spec = along((1, seq_dev, width), 0)
     in_spec = along((1, seq_dev, DSTATE), 0)
     decay_spec = along((1, heads, seq_dev), 0)
+    folds = probe_len // height
+    wide = width + (folds + 1) * DSTATE
     ends = call(
-        end_kernel,
+        functools.partial(end_kernel, seq_dev=seq_dev, height=height),
         "ends",
-        [x_spec, in_spec, decay_spec],
-        along((1, DSTATE, width), 0),
-        shaped((row_count, DSTATE, width), BF16),
+        [SMEM, SMEM, x_spec, in_spec, decay_spec, along(probe_reads.shape)],
+        along((1, DSTATE, wide), 0),
+        shaped((row_count, DSTATE, wide), BF16),
         (row_count,),
         [pltpu.VMEM((seq_dev, width), BF16)],
         flops=4_000_000_000,
         moved=20_000_000,
-    )(tokens, state_inputs, log_decay)
-    parts = exchange(ends.reshape(seq, height, width), "seq")
+    )(branch_position, me, tokens, state_inputs, log_decay, probe_reads)
+    parts = exchange(ends.reshape(seq, height, wide), "seq")
 
     token = shaped((8, 128), F32)
     token_spec = pl.BlockSpec((8, 128), lambda *at: (0, 0))
-    right, built = call(
-        build_kernel,
+    right, table = call(
+        functools.partial(build_kernel, seq_dev=seq_dev, probe_dev=probe_dev),
         "build",
-        [x_spec, in_spec, decay_spec],
-        [along((1, count, depth, width), 0), token_spec],
-        [shaped((row_count, count, depth, width), BF16), token],
+        [SMEM, SMEM, SMEM, x_spec, in_spec, decay_spec],
+        [along((1, count, depth, width), 0), SMEM],
+        [shaped((row_count, count, depth, width), BF16), shaped((4 * seq,), jnp.int32)],
         (row_count,),
         flops=5_000_000_000,
         moved=40_000_000,
-    )(tokens, state_inputs, log_decay)
+    )(branch_position, branch_premise, me, tokens, state_inputs, log_decay)
 
     probe_rows = probe_dev * probe_len
+    pair = 128 // probe_len
     inner, factor, probed = call(
         probe_kernel,
         "probes",
-        [along(part.shape) for part in (probe_tokens, probe_inputs, probe_reads, probe_decay)],
-        [along(probe_tokens.shape)] * 2 + [token_spec],
+        [
+            along((pair,) + part.shape[1:], 0)
+            for part in (probe_tokens, probe_inputs, probe_reads, probe_decay)
+        ],
+        [along((pair, probe_len, width), 0)] * 2 + [token_spec],
         [shaped(probe_tokens.shape, F32)] * 2 + [token],
-        (1,),
+        (probe_dev // pair,),
         flops=1_000_000_000,
         moved=8_000_000,
     )(probe_tokens, probe_inputs, probe_reads, probe_decay)
 
     starts = call(
-        functools.partial(scan_kernel, probe_len=probe_len, heads=heads),
+        functools.partial(scan_kernel, heads=heads),
         "scan",
-        [SMEM, VMEM, along(routed_shape), ANY, ANY],
+        [VMEM, ANY, ANY],
         along((seq, height, width)),
         shaped((seq, height, width), BF16),
         (1,),
         limit=48,
         flops=1_000_000_000,
         moved=2_500_000,
-    )(me, parts, routed, built, probed)
+    )(parts, right, probed)
     incoming = exchange(starts, "seq").reshape(row_count, DSTATE, width)
 
     step = 4
@@ -461,7 +465,14 @@
 
         return pl.BlockSpec(shape, at)
 
-    local_part, scale = pl.pallas_call(
+    def reads_specs(group):
+        first = width // DSTATE
+        return [
+            pl.BlockSpec((group, height, DSTATE), lambda i, *_, lane=first + fold: (i, 0, lane))
+            for fold in range(folds)
+        ]
+
+    local_part = pl.pallas_call(
         functools.partial(branch_kernel, step=step),
         name="branch",
         grid_spec=pltpu.PrefetchScalarGridSpec(
@@ -470,10 +481,10 @@
             in_specs=[picked((1, 1, depth, width), i, True) for i in range(step)]
             + [picked((1, BLOCK, DSTATE), i, True) for i in range(step)]
             + [picked((1, heads, seq_dev), i, False) for i in range(step)]
-            + [along((step,) + routed_shape[1:], 0)],
-            out_specs=[along((step, probe_len, width), 0), along((step, 8, width), 0)],
+            + reads_specs(step),
+            out_specs=along((step, probe_len + 8, width), 0),
         ),
-        out_shape=[shaped((seq, probe_len, width), F32), shaped((seq, 8, width), F32)],
+        out_shape=shaped((seq, probe_len + 8, width), F32),
         compiler_params=pltpu.CompilerParams(vmem_limit_bytes=58 * 1024 * 1024),
         cost_estimate=pl.CostEstimate(
             flops=1_000_000_000, bytes_accessed=20_000_000, transcendentals=0
@@ -483,28 +494,21 @@
         *[right] * step,
         *[state_inputs] * step,
         *[log_decay] * step,
-        routed,
+        *[parts] * folds,
     )
 
-    answers, applied = call(
+    group = seq // 2
+    answers = call(
         apply_kernel,
         "apply",
-        [SMEM, VMEM]
-        + [
-            along(shape, 0)
-            for shape in (
-                (step,) + routed_shape[1:],
-                (step, probe_len, width),
-                (step, 8, width),
-            )
-        ],
-        [along((step, probe_len, width), 0), token_spec],
-        [shaped((seq, probe_len, width), BF16), token],
-        (seq // step,),
+        [SMEM, VMEM] + reads_specs(group) + [along((group, probe_len + 8, width), 0)],
+        along((group, probe_len, width), 0),
+        shaped((seq, probe_len, width), BF16),
+        (seq // group,),
         limit=48,
         flops=1_000_000_000,
         moved=8_000_000,
-    )(table, incoming, routed, local_part, scale)
+    )(table, incoming, *[parts] * folds, local_part)
     arrived = exchange(answers, "seq")
 
     gain = norm_gain.reshape(1, width)
@@ -520,34 +524,35 @@
             along((1, DSTATE, width), 0),
             along((1, count, depth, width), 0),
             along((1, width)),
-            ANY,
         ],
         [x_spec, square_spec],
-        [shaped(tokens.shape, F32), shaped(square_shape, F32)],
+        [shaped(tokens.shape, BF16), shaped(square_shape, F32)],
         (row_count,),
+        limit=58,
         flops=12_000_000_000,
         moved=60_000_000,
-    )(state_inputs, state_reads, log_decay, incoming, right, gain, applied)
+    )(state_inputs, state_reads, log_decay, incoming, right, gain)
     shared = [square] + [
         lax.ppermute(square, "head", [(i, (i + turn) % ring) for i in range(ring)])
         for turn in range(1, ring)
     ]
 
+    probe_shape = (1, probe_rows, width)
     probe_mixed, probe_square = call(
         functools.partial(join_kernel, seq_dev=seq_dev),
         "join",
         [
             SMEM,
             SMEM,
-            along((128 // probe_len, probe_len, width), 0),
-            along((128 // probe_len, probe_len, width), 0),
+            along((pair, probe_len, width), 0),
+            along((pair, probe_len, width), 0),
             along((1, width)),
             VMEM,
         ],
-        [along((128, width), 0), along((ring, 8, 128))],
-        [shaped((probe_rows, width), F32), shaped((ring, 8, 128), F32)],
-        (probe_rows // 128,),
-        limit=48,
+        [pl.BlockSpec((1, 128, width), lambda i: (0, i, 0)), along((ring, 8, 128))],
+        [shaped(probe_shape, F32), shaped((ring, 8, 128), F32)],
+        (probe_dev // pair,),
+        limit=52,
         flops=1_000_000,
         moved=5_000_000,
     )(branch_position, me, inner, factor, gain, arrived)
@@ -556,26 +561,24 @@
     premise_out = call(
         norm_kernel,
         "norm",
-        [x_spec] + [square_spec] * ring,
-        x_spec,
+        [along((2, seq_dev, width), 0)] + [along((2, 8, 128), 0)] * ring,
+        along((2, seq_dev, width), 0),
         shaped(tokens.shape, BF16),
-        (row_count,),
-        limit=50,
+        (row_count // 2,),
+        limit=54,
         flops=1_000_000_000,
         moved=30_000_000,
     )(mixed, *shared)
-    probe_shape = (1, probe_rows, width)
     probe_out = call(
         norm_kernel,
         "probe_norm",
-        [along(probe_shape), along((ring, 8, 128))],
-        along(probe_shape),
+        [VMEM, VMEM],
+        VMEM,
         shaped(probe_shape, BF16),
-        (1,),
-        limit=54,
+        limit=40,
         flops=1_000_000,
         moved=2_000_000,
-    )(probe_mixed.reshape(probe_shape), probe_square)
+    )(probe_mixed, probe_square)
     return (premise_out, probe_out.reshape(probe_dev, probe_len, width))
 
 

time: 132 us -> 116 us (0.88)
  starting transfers between devices: 43 us -> 36.1 us
  Pallas kernels: 75.7 us -> 69.3 us
  local copies, waits for them, and re-layouts: 4.54 us -> 0.63 us
  waiting for transfers between devices: 7.36 us -> 8.96 us
    all_to_all x5 -> x4, starting transfers between devices: 31.2 us -> 24.5 us  [exchange(): return lax.all_to_all(value, axis, split_axis=0, concat_axis=0, tiled=True)]
    pallas_call x8 -> x7, Pallas kernels: 46.5 us -> 40.2 us  [the longest x1 12.8 us: local(): call(functools.partial(build_kernel, seq_dev=seq_dev, probe_dev=probe_dev...]
    unnamed x30 -> x28, local copies, waits for them, and re-layouts: 4.54 us -> 0.63 us
    all_to_all x5 -> x4, waiting for transfers between devices: 7.34 us -> 8.95 us  [exchange(): return lax.all_to_all(value, axis, split_axis=0, concat_axis=0, tiled=True)]
  transfers between devices with their start and end apart: 12 -> 11, of which waited for: 1 -> 2; matrix products, arithmetic and copies ran while one was open for 0% -> 0% of each run, Pallas kernels for 49% -> 46%
where the time goes in v5:
time: 116 us
  Pallas kernels  69.3 us (60%)
  starting transfers between devices  36.1 us (31%)
  waiting for transfers between devices  8.96 us (8%)
    all_to_all x4, starting transfers between devices, exchange(): return lax.all_to_all(value, axis, split_axis=0, concat_axis=0, tiled=True)  24.5 us
    pallas_call x1, Pallas kernels, local(): call(main_kernel, 'main', [in_spec, in_spec, decay_spec, along((1, DSTATE...  17.6 us
    pallas_call x1, Pallas kernels, local(): call(functools.partial(build_kernel, seq_dev=seq_dev, probe_dev=probe_dev...  12.8 us
    ppermute x7, starting transfers between devices, local(): lax.ppermute(square, 'head', [(i, (i + turn) % ring) for i in range(ring)])  11.6 us
    pallas_call x1, Pallas kernels, local(): call(functools.partial(end_kernel, seq_dev=seq_dev, height=height), 'ends...  9.16 us
    all_to_all x4, waiting for transfers between devices, exchange(): return lax.all_to_all(value, axis, split_axis=0, concat_axis=0, tiled=True)  8.95 us
    pallas_call x1, Pallas kernels, local(): pl.pallas_call(functools.partial(branch_kernel, step=step), name='branch'...  7.28 us
    pallas_call x1, Pallas kernels, local(): call(norm_kernel, 'norm', [along((2, seq_dev, width), 0)] + [along((2, 8,...  6.49 us
  transfers between devices with their start and end apart: 11, of which 2 were waited for; matrix products, arithmetic and copies ran while one was open for 0% of the time, Pallas kernels for 46%

profile of v5, /device:TPU:1, one launch (start us, length us, event | category | flops | bytes accessed | tf_op | source)
XLA Modules:
  0.0 115.8 jit_solution(17398295820934699544)
XLA Ops:
  0.6 9.2 %ends.1 = bf16[4,128,1408]{2,1,0:T(8,128)(2,1)} custom-call(s32[96]{0:T(128)} %position_ref.5, s32[1]{0:T(128)} %bitcast.me_ref, bf16[4,1024,1024]{2,1,0:T(8,128)(2,1)} %x_ref.4, bf16[4,1024,128]{2,1,0:T(8,128)(2,1)} %refs_7_.1, f32[4,16,1024]{2,1,0:T(8,128)} %refs_11_.1, bf16[6,64,128]{2,1,0:T(8,128)(2,1)} %read_ref.2), custom_call_target="tpu_custom_call" | custom-call | flops 4000000000 | bytes 20000000 | tf_op jit(solution)/shard_map/ends/pallas_call | solution.py:403
  9.8 8.6 %all-to-all-start = ((bf16[16,32,1408]{2,1,0:T(8,128)(2,1)}), bf16[16,32,1408]{2,1,0:T(8,128)(2,1)S(1)}, u32[]{:S(2)}, u32[]{:S(2)}) async-start(bf16[16,32,1408]{2,1,0:T(8,128)(2,1)} %bitcast.9), calls=%async_computation | async-start | bytes 2883584 | tf_op jit(solution)/shard_map/all_to_all | solution.py:372
  18.4 4.9 %probes.1 = (f32[6,64,1024]{2,1,0:T(8,128)}, f32[6,64,1024]{2,1,0:T(8,128)}, f32[8,128]{1,0:T(8,128)}) custom-call(bf16[6,64,1024]{2,1,0:T(8,128)(2,1)} %x_ref.5, bf16[6,64,128]{2,1,0:T(8,128)(2,1)} %in_ref.6, bf16[6,64,128]{2,1,0:T(8,128)(2,1)} %read_ref.2, f32[6,16,64]{2,1,0:T(8,128)} %decay_ref.6), custom_call_target="tpu_custom_call" | custom-call | flops 1000000000 | bytes 8000000 | tf_op jit(solution)/shard_map/probes/pallas_call | solution.py:431
  23.3 12.8 %build.1 = (bf16[4,8,256,1024]{3,2,1,0:T(8,128)(2,1)}, s32[64]{0:T(128)}) custom-call(s32[96]{0:T(128)} %position_ref.5, s32[96]{0:T(128)} %premise_ref.1, s32[1]{0:T(128)} %bitcast.me_ref, bf16[4,1024,1024]{2,1,0:T(8,128)(2,1)} %x_ref.4, bf16[4,1024,128]{2,1,0:T(8,128)(2,1)} %refs_7_.1, f32[4,16,1024]{2,1,0:T(8,128)} %refs_11_.1), custom_call_target="tpu_custom_call" | custom-call | flops 5000000000 | bytes 40000000 | tf_op jit(solution)/shard_map/build/pallas_call | solution.py:418
  36.1 1.6 %all-to-all-done.part_ref.refs_12_.refs_13_.refs_0_.refs_1_ = bf16[16,32,1408]{2,1,0:T(8,128)(2,1)S(1)} async-done(((bf16[16,32,1408]{2,1,0:T(8,128)(2,1)}), bf16[16,32,1408]{2,1,0:T(8,128)(2,1)S(1)}, u32[]{:S(2)}, u32[]{:S(2)}) %all-to-all-start) | async-done | bytes 1441824 | tf_op jit(solution)/shard_map/all_to_all | solution.py:372
  37.7 1.5 %scan.1 = bf16[16,32,1024]{2,1,0:T(8,128)(2,1)} custom-call(bf16[16,32,1408]{2,1,0:T(8,128)(2,1)S(1)} %all-to-all-done.part_ref.refs_12_.refs_13_.refs_0_.refs_1_, bf16[4,8,256,1024]{3,2,1,0:T(8,128)(2,1)} %get-tuple-element.11.built_ref.right_ref.refs_0_.refs_1_.refs_2_.refs_3_, f32[8,128]{1,0:T(8,128)S(1)} %copy-done.4), custom_call_target="tpu_custom_call" | custom-call | flops 1000000000 | bytes 2500000 | tf_op jit(solution)/shard_map/scan/pallas_call | solution.py:445
  39.2 5.1 %all-to-all-start.1 = ((bf16[16,32,1024]{2,1,0:T(8,128)(2,1)}), bf16[16,32,1024]{2,1,0:T(8,128)(2,1)S(1)}, u32[]{:S(2)}, u32[]{:S(2)}) async-start(bf16[16,32,1024]{2,1,0:T(8,128)(2,1)} %scan.1), calls=%async_computation.1 | async-start | bytes 2097152 | tf_op jit(solution)/shard_map/all_to_all | solution.py:372
  44.3 7.3 %branch.1.refs_2_ = f32[16,72,1024]{2,1,0:T(8,128)} custom-call(s32[64]{0:T(128)} %get-tuple-element.17.table_ref, bf16[4,8,256,1024]{3,2,1,0:T(8,128)(2,1)} %get-tuple-element.11.built_ref.right_ref.refs_0_.refs_1_.refs_2_.refs_3_, bf16[4,8,256,1024]{3,2,1,0:T(8,128)(2,1)} %get-tuple-element.11.built_ref.right_ref.refs_0_.refs_1_.refs_2_.refs_3_, ...), custom_call_target="tpu_custom_call" | custom-call | flops 1000000000 | bytes 20000000 | tf_op jit(solution)/shard_map/branch/pallas_call | solution.py:475
  51.6 7.3 %all-to-all-done.1 = bf16[16,32,1024]{2,1,0:T(8,128)(2,1)S(1)} async-done(((bf16[16,32,1024]{2,1,0:T(8,128)(2,1)}), bf16[16,32,1024]{2,1,0:T(8,128)(2,1)S(1)}, u32[]{:S(2)}, u32[]{:S(2)}) %all-to-all-start.1) | async-done | bytes 1048608 | tf_op jit(solution)/shard_map/all_to_all | solution.py:372
  58.9 4.2 %apply.1 = bf16[16,64,1024]{2,1,0:T(8,128)(2,1)} custom-call(s32[64]{0:T(128)S(1)} %copy-done.5, bf16[4,128,1024]{2,1,0:T(8,128)(2,1)S(1)} %bitcast.5, bf16[16,32,1408]{2,1,0:T(8,128)(2,1)S(1)} %copy-done.1, bf16[16,32,1408]{2,1,0:T(8,128)(2,1)S(1)} %copy-done.1, f32[16,72,1024]{2,1,0:T(8,128)} %branch.1.refs_2_), custom_call_target="tpu_custom_call" | custom-call | flops 1000000000 | bytes 8000000 | tf_op jit(solution)/shard_map/apply/pallas_call | solution.py:501
  63.2 5.0 %all-to-all-start.2 = ((bf16[16,64,1024]{2,1,0:T(8,128)(2,1)}), bf16[16,64,1024]{2,1,0:T(8,128)(2,1)}, u32[]{:S(2)}, u32[]{:S(2)}) async-start(bf16[16,64,1024]{2,1,0:T(8,128)(2,1)} %apply.1), calls=%async_computation.2 | async-start | bytes 4194304 | tf_op jit(solution)/shard_map/all_to_all | solution.py:372
  68.1 0.0 copy-start.3
  68.1 0.0 copy-start.6
  68.2 17.6 %main.1 = (bf16[4,1024,1024]{2,1,0:T(8,128)(2,1)}, f32[4,8,128]{2,1,0:T(8,128)}) custom-call(bf16[4,1024,128]{2,1,0:T(8,128)(2,1)} %refs_7_.1, bf16[4,1024,128]{2,1,0:T(8,128)(2,1)} %read_ref.3, f32[4,16,1024]{2,1,0:T(8,128)} %refs_11_.1, bf16[4,128,1024]{2,1,0:T(8,128)(2,1)} %bitcast.6, ...), custom_call_target="tpu_custom_call" | custom-call | flops 12000000000 | bytes 60000000 | tf_op jit(solution)/shard_map/main/pallas_call | solution.py:517
  85.8 4.0 %collective-permute-start = (f32[4,8,128]{2,1,0:T(8,128)}, f32[4,8,128]{2,1,0:T(8,128)S(1)}, u32[]{:S(2)}, u32[]{:S(2)}) collective-permute-start(f32[4,8,128]{2,1,0:T(8,128)} %get-tuple-element.14.refs_0_), channel_id=1, source_target_pairs={{0,1},{1,2},{2,3},{3,4},{4,5},{5,6},{6,7},{7,0},{8,9},{9,10},{10,1... | collective-permute-start | bytes 49160 | tf_op jit(solution)/shard_map/ppermute | solution.py:536
  89.8 1.2 %collective-permute-start.1 = (f32[4,8,128]{2,1,0:T(8,128)}, f32[4,8,128]{2,1,0:T(8,128)S(1)}, u32[]{:S(2)}, u32[]{:S(2)}) collective-permute-start(f32[4,8,128]{2,1,0:T(8,128)} %get-tuple-element.14.refs_0_), channel_id=1, source_target_pairs={{0,2},{1,3},{2,4},{3,5},{4,6},{5,7},{6,0},{7,1},{8,10},{9,11},{10,... | collective-permute-start | bytes 49160 | tf_op jit(solution)/shard_map/ppermute | solution.py:536
  91.0 1.6 %collective-permute-start.2 = (f32[4,8,128]{2,1,0:T(8,128)}, f32[4,8,128]{2,1,0:T(8,128)S(1)}, u32[]{:S(2)}, u32[]{:S(2)}) collective-permute-start(f32[4,8,128]{2,1,0:T(8,128)} %get-tuple-element.14.refs_0_), channel_id=1, source_target_pairs={{0,3},{1,4},{2,5},{3,6},{4,7},{5,0},{6,1},{7,2},{8,11},{9,12},{10,... | collective-permute-start | bytes 49160 | tf_op jit(solution)/shard_map/ppermute | solution.py:536
  92.6 0.5 collective-permute-start.3
  93.1 2.0 %collective-permute-start.4 = (f32[4,8,128]{2,1,0:T(8,128)}, f32[4,8,128]{2,1,0:T(8,128)S(1)}, u32[]{:S(2)}, u32[]{:S(2)}) collective-permute-start(f32[4,8,128]{2,1,0:T(8,128)} %get-tuple-element.14.refs_0_), channel_id=1, source_target_pairs={{0,5},{1,6},{2,7},{3,0},{4,1},{5,2},{6,3},{7,4},{8,13},{9,14},{10,... | collective-permute-start | bytes 49160 | tf_op jit(solution)/shard_map/ppermute | solution.py:536
  95.1 0.0 collective-permute-done.refs_1_
  95.1 0.7 collective-permute-start.5
  95.7 1.7 %collective-permute-start.6 = (f32[4,8,128]{2,1,0:T(8,128)}, f32[4,8,128]{2,1,0:T(8,128)S(1)}, u32[]{:S(2)}, u32[]{:S(2)}) collective-permute-start(f32[4,8,128]{2,1,0:T(8,128)} %get-tuple-element.14.refs_0_), channel_id=1, source_target_pairs={{0,7},{1,0},{2,1},{3,2},{4,3},{5,4},{6,5},{7,6},{8,15},{9,8},{10,9... | collective-permute-start | bytes 49160 | tf_op jit(solution)/shard_map/ppermute | solution.py:536
  97.4 0.0 all-to-all-done.2.arrived_ref
  97.4 4.2 %join.1 = (f32[1,384,1024]{2,1,0:T(8,128)S(1)}, f32[8,8,128]{2,1,0:T(8,128)}) custom-call(s32[96]{0:T(128)S(1)} %copy-done.6, s32[1]{0:T(128)} %bitcast.me_ref, f32[6,64,1024]{2,1,0:T(8,128)} %get-tuple-element.15.inner_ref, f32[6,64,1024]{2,1,0:T(8,128)} %get-tuple-element.16.factor_ref, f32[1,1024]{1,0:T(1,128)S(1)} %bitcast.8, ...), custom_call_target="tpu_custom_call" | custom-call | flops 1000000 | bytes 5000000 | tf_op jit(solution)/shard_map/join/pallas_call | solution.py:541
  101.6 5.9 %all-to-all-start.3 = ((f32[8,8,128]{2,1,0:T(8,128)}), f32[8,8,128]{2,1,0:T(8,128)S(1)}, u32[]{:S(2)}, u32[]{:S(2)}) async-start(f32[8,8,128]{2,1,0:T(8,128)} %get-tuple-element.19), calls=%async_computation.3 | async-start | bytes 65536 | tf_op jit(solution)/shard_map/all_to_all | solution.py:372
  107.6 0.5 copy-done.9
  108.1 0.0 copy-done.10
  108.1 0.0 copy-done.11
  108.1 0.0 copy-done.12
  108.1 0.0 copy-done.13
  108.2 6.5 %norm.1 = bf16[4,1024,1024]{2,1,0:T(8,128)(2,1)} custom-call(bf16[4,1024,1024]{2,1,0:T(8,128)(2,1)} %get-tuple-element.13.mixed_ref, f32[4,8,128]{2,1,0:T(8,128)} %get-tuple-element.14.refs_0_, f32[4,8,128]{2,1,0:T(8,128)} %copy-done.7, f32[4,8,128]{2,1,0:T(8,128)} %copy-done.8, f32[4,8,128]{2,1,0:T(8,128)} %copy-done.9, f32[4,8,128]{2,1,0:T(8,128)} %copy-done.10, ...), custom_call_target="tpu_custom_call" | custom-call | flops 1000000000 | bytes 30000000 | tf_op jit(solution)/shard_map/norm/pallas_call | solution.py:561
  114.7 1.1 probe_norm.1
  (28 shorter events, 0.1 us)
Async XLA Ops:
  9.8 27.9 %all-to-all-start = ((bf16[16,32,1408]{2,1,0:T(8,128)(2,1)}), bf16[16,32,1408]{2,1,0:T(8,128)(2,1)S(1)}, u32[]{:S(2)}, u32[]{:S(2)}) async-start(bf16[16,32,1408]{2,1,0:T(8,128)(2,1)} %bitcast.9), calls=%async_computation | async-start | bytes 2883584 | tf_op jit(solution)/shard_map/all_to_all | solution.py:372
  23.3 14.4 %copy-start.4 = (f32[8,128]{1,0:T(8,128)S(1)}, f32[8,128]{1,0:T(8,128)}, u32[]{:S(2)}) copy-start(f32[8,128]{1,0:T(8,128)} %get-tuple-element.12.probed_ref) | copy-start | bytes 12292
  37.7 1.5 %copy-start = (bf16[16,32,1408]{2,1,0:T(8,128)(2,1)}, bf16[16,32,1408]{2,1,0:T(8,128)(2,1)S(1)}, u32[]{:S(2)}) copy-start(bf16[16,32,1408]{2,1,0:T(8,128)(2,1)S(1)} %all-to-all-done.part_ref.refs_12_.refs_13_.refs_0_.refs_1_) | copy-start | bytes 4325380
  39.2 19.7 %all-to-all-start.1 = ((bf16[16,32,1024]{2,1,0:T(8,128)(2,1)}), bf16[16,32,1024]{2,1,0:T(8,128)(2,1)S(1)}, u32[]{:S(2)}, u32[]{:S(2)}) async-start(bf16[16,32,1024]{2,1,0:T(8,128)(2,1)} %scan.1), calls=%async_computation.1 | async-start | bytes 2097152 | tf_op jit(solution)/shard_map/all_to_all | solution.py:372
  44.3 14.6 %copy-start.1 = (bf16[16,32,1408]{2,1,0:T(8,128)(2,1)S(1)}, bf16[16,32,1408]{2,1,0:T(8,128)(2,1)}, u32[]{:S(2)}) copy-start(bf16[16,32,1408]{2,1,0:T(8,128)(2,1)} %copy-done) | copy-start | bytes 4325380
  44.3 14.6 %copy-start.5 = (s32[64]{0:T(128)S(1)}, s32[64]{0:T(128)}, u32[]{:S(2)}) copy-start(s32[64]{0:T(128)} %get-tuple-element.17.table_ref) | copy-start | bytes 772
  58.9 4.2 %copy-start.2 = (bf16[16,32,1024]{2,1,0:T(8,128)(2,1)}, bf16[16,32,1024]{2,1,0:T(8,128)(2,1)S(1)}, u32[]{:S(2)}) copy-start(bf16[16,32,1024]{2,1,0:T(8,128)(2,1)S(1)} %all-to-all-done.1) | copy-start | bytes 3145732
  63.2 34.2 %all-to-all-start.2 = ((bf16[16,64,1024]{2,1,0:T(8,128)(2,1)}), bf16[16,64,1024]{2,1,0:T(8,128)(2,1)}, u32[]{:S(2)}, u32[]{:S(2)}) async-start(bf16[16,64,1024]{2,1,0:T(8,128)(2,1)} %apply.1), calls=%async_computation.2 | async-start | bytes 4194304 | tf_op jit(solution)/shard_map/all_to_all | solution.py:372
  68.1 29.3 %copy-start.3 = (f32[1024]{0:T(1024)S(1)}, f32[1024]{0:T(1024)}, u32[]{:S(2)}) copy-start(f32[1024]{0:T(1024)} %param.15) | copy-start | bytes 12292
  68.1 29.3 %copy-start.6 = (s32[96]{0:T(128)S(1)}, s32[96]{0:T(128)}, u32[]{:S(2)}) copy-start(s32[96]{0:T(128)} %position_ref.5) | copy-start | bytes 1156
  85.8 9.3 %collective-permute-start = (f32[4,8,128]{2,1,0:T(8,128)}, f32[4,8,128]{2,1,0:T(8,128)S(1)}, u32[]{:S(2)}, u32[]{:S(2)}) collective-permute-start(f32[4,8,128]{2,1,0:T(8,128)} %get-tuple-element.14.refs_0_), channel_id=1, source_target_pairs={{0,1},{1,2},{2,3},{3,4},{4,5},{5,6},{6,7},{7,0},{8,9},{9,10},{10,1... | collective-permute-start | bytes 49160 | tf_op jit(solution)/shard_map/ppermute | solution.py:536
  89.8 5.9 %collective-permute-start.1 = (f32[4,8,128]{2,1,0:T(8,128)}, f32[4,8,128]{2,1,0:T(8,128)S(1)}, u32[]{:S(2)}, u32[]{:S(2)}) collective-permute-start(f32[4,8,128]{2,1,0:T(8,128)} %get-tuple-element.14.refs_0_), channel_id=1, source_target_pairs={{0,2},{1,3},{2,4},{3,5},{4,6},{5,7},{6,0},{7,1},{8,10},{9,11},{10,... | collective-permute-start | bytes 49160 | tf_op jit(solution)/shard_map/ppermute | solution.py:536
  91.0 16.5 %collective-permute-start.2 = (f32[4,8,128]{2,1,0:T(8,128)}, f32[4,8,128]{2,1,0:T(8,128)S(1)}, u32[]{:S(2)}, u32[]{:S(2)}) collective-permute-start(f32[4,8,128]{2,1,0:T(8,128)} %get-tuple-element.14.refs_0_), channel_id=1, source_target_pairs={{0,3},{1,4},{2,5},{3,6},{4,7},{5,0},{6,1},{7,2},{8,11},{9,12},{10,... | collective-permute-start | bytes 49160 | tf_op jit(solution)/shard_map/ppermute | solution.py:536
  92.6 14.9 %collective-permute-start.3 = (f32[4,8,128]{2,1,0:T(8,128)}, f32[4,8,128]{2,1,0:T(8,128)S(1)}, u32[]{:S(2)}, u32[]{:S(2)}) collective-permute-start(f32[4,8,128]{2,1,0:T(8,128)} %get-tuple-element.14.refs_0_), channel_id=1, source_target_pairs={{0,4},{1,5},{2,6},{3,7},{4,0},{5,1},{6,2},{7,3},{8,12},{9,13},{10,... | collective-permute-start | bytes 49160 | tf_op jit(solution)/shard_map/ppermute | solution.py:536
  93.1 14.4 %collective-permute-start.4 = (f32[4,8,128]{2,1,0:T(8,128)}, f32[4,8,128]{2,1,0:T(8,128)S(1)}, u32[]{:S(2)}, u32[]{:S(2)}) collective-permute-start(f32[4,8,128]{2,1,0:T(8,128)} %get-tuple-element.14.refs_0_), channel_id=1, source_target_pairs={{0,5},{1,6},{2,7},{3,0},{4,1},{5,2},{6,3},{7,4},{8,13},{9,14},{10,... | collective-permute-start | bytes 49160 | tf_op jit(solution)/shard_map/ppermute | solution.py:536
  95.1 6.6 %copy-start.7 = (f32[4,8,128]{2,1,0:T(8,128)}, f32[4,8,128]{2,1,0:T(8,128)S(1)}, u32[]{:S(2)}) copy-start(f32[4,8,128]{2,1,0:T(8,128)S(1)} %collective-permute-done.refs_1_) | copy-start | bytes 49156
  95.1 12.5 %collective-permute-start.5 = (f32[4,8,128]{2,1,0:T(8,128)}, f32[4,8,128]{2,1,0:T(8,128)S(1)}, u32[]{:S(2)}, u32[]{:S(2)}) collective-permute-start(f32[4,8,128]{2,1,0:T(8,128)} %get-tuple-element.14.refs_0_), channel_id=1, source_target_pairs={{0,6},{1,7},{2,0},{3,1},{4,2},{5,3},{6,4},{7,5},{8,14},{9,15},{10,... | collective-permute-start | bytes 49160 | tf_op jit(solution)/shard_map/ppermute | solution.py:536
  95.7 5.9 %copy-start.8 = (f32[4,8,128]{2,1,0:T(8,128)}, f32[4,8,128]{2,1,0:T(8,128)S(1)}, u32[]{:S(2)}) copy-start(f32[4,8,128]{2,1,0:T(8,128)S(1)} %collective-permute-done.1.refs_2_) | copy-start | bytes 49156
  95.7 11.8 %collective-permute-start.6 = (f32[4,8,128]{2,1,0:T(8,128)}, f32[4,8,128]{2,1,0:T(8,128)S(1)}, u32[]{:S(2)}, u32[]{:S(2)}) collective-permute-start(f32[4,8,128]{2,1,0:T(8,128)} %get-tuple-element.14.refs_0_), channel_id=1, source_target_pairs={{0,7},{1,0},{2,1},{3,2},{4,3},{5,4},{6,5},{7,6},{8,15},{9,8},{10,9... | collective-permute-start | bytes 49160 | tf_op jit(solution)/shard_map/ppermute | solution.py:536
  101.6 13.0 %all-to-all-start.3 = ((f32[8,8,128]{2,1,0:T(8,128)}), f32[8,8,128]{2,1,0:T(8,128)S(1)}, u32[]{:S(2)}, u32[]{:S(2)}) async-start(f32[8,8,128]{2,1,0:T(8,128)} %get-tuple-element.19), calls=%async_computation.3 | async-start | bytes 65536 | tf_op jit(solution)/shard_map/all_to_all | solution.py:372
  107.5 0.6 copy-start.9
  107.5 0.6 copy-start.10
  107.5 0.6 copy-start.11
  107.5 0.6 copy-start.12
  107.6 0.6 copy-start.13
